TPU v7x, 32 devices: a whole 2x2x4 slice. The times are simulated.
32 devices in a mesh: dp: 8 (over z, y), mp: 4 (over x, core).
Axes of the slice: x: 2, y: 2, z: 4, core: 2. Of those that a mesh axis runs over, the one named last changes fastest.
Arguments:
- tokens: bfloat16 [8192, 1152], P('dp'), may hold values from -6 to 6
- timesteps: int32 [32], P('dp'), may hold values from 0 to 999
- relative_index: int32 [256, 256], replicated, may hold values from 0 to 960, as said below
- time_table: bfloat16 [1000, 1152], replicated, may hold values from -6 to 6
- query_weight: bfloat16 [1152, 1152], replicated, may hold values from -0.1875 to 0.1875
- key_weight: bfloat16 [1152, 1152], replicated, may hold values from -0.1875 to 0.1875
- value_weight: bfloat16 [1152, 1152], replicated, may hold values from -0.1875 to 0.1875
- time_query_weight: bfloat16 [1152, 1152], replicated, may hold values from -0.1875 to 0.1875
- time_value_weight: bfloat16 [1152, 1152], replicated, may hold values from -0.09375 to 0.09375
- out_weight: bfloat16 [1152, 1152], replicated, may hold values from -0.5 to 0.5
- out_bias: float32 [1152], replicated, may hold values from -3 to 3
- first_gain: float32 [1152], replicated, may hold values from 0.5 to 1.5
- first_shift: float32 [1152], replicated, may hold values from -3 to 3
- second_gain: float32 [1152], replicated, may hold values from 0.5 to 1.5
- second_shift: float32 [1152], replicated, may hold values from -3 to 3
- up_weight: bfloat16 [1152, 4608], P(None, 'mp'), may hold values from -0.1875 to 0.1875
- up_bias: float32 [4608], P('mp'), may hold values from -3 to 3
- down_weight: bfloat16 [4608, 1152], P('mp'), may hold values from -0.09375 to 0.09375
- down_bias: float32 [1152], replicated, may hold values from -3 to 3
- bias_table: float32 [961, 16], replicated, may hold values from -4 to 4
- cotangent: bfloat16 [8192, 1152], P(('dp', 'mp')), may hold values from -6 to 6
Outputs:
- block_out: bfloat16 [8192, 1152], P(('dp', 'mp'))
- tokens_grad: float32 [8192, 1152], P(('dp', 'mp'))
- time_table_grad: float32 [1000, 1152], P(None, 'mp')
- query_weight_grad: float32 [1152, 1152], P(None, 'mp')
- key_weight_grad: float32 [1152, 1152], P(None, 'mp')
- value_weight_grad: float32 [1152, 1152], P(None, 'mp')
- time_query_grad: float32 [1152, 1152], P(None, 'mp')
- time_value_grad: float32 [1152, 1152], P(None, 'mp')
- out_weight_grad: float32 [1152, 1152], P('mp')
- out_bias_grad: float32 [1152], P('mp')
- first_gain_grad: float32 [1152], P('mp')
- first_shift_grad: float32 [1152], P('mp')
- second_gain_grad: float32 [1152], P('mp')
- second_shift_grad: float32 [1152], P('mp')
- up_weight_grad: float32 [1152, 4608], P(None, 'mp')
- up_bias_grad: float32 [4608], P('mp')
- down_weight_grad: float32 [4608, 1152], P('mp')
- down_bias_grad: float32 [1152], P('mp')
- bias_table_grad: float32 [961, 16], P(None, 'mp')
Inputs may be any that keep to these rules, and one draw needn't show every extreme that they name: `relative_index`: the tokens of an image sit on distinct cells of a 16 x 16 grid; entry (i, j) is (row_i - row_j + 15) * 31 + column_i - column_j + 15.
All inputs are finite; a program needn't handle non-finite values.
Results may differ from a plain program's by a relative error of at most 0.013.
Values may be sent and summed in bfloat16 or wider, within the bound.
No kernel may reach another device: no remote copies, remote signals or barrier semaphores. Data moves between devices by JAX's collectives and lax.ppermute only.
A program may use at most 256 MiB of HBM per device.

v0:
```python
import math
from functools import partial

import jax
import jax.numpy as jnp
from jax import lax
from jax.experimental import pallas as pl
from jax.experimental.pallas import tpu as pltpu
from jax.sharding import PartitionSpec as P

EPSILON = 1e-06
HIGHEST = lax.Precision.HIGHEST
F32 = jnp.float32
BF16 = jnp.bfloat16
LANES = 128


def mm(left, right):
    return lax.dot_general(left, right, (((1,), (0,)), ((), ())), preferred_element_type=F32)


def mm_nt(left, right):
    return lax.dot_general(left, right, (((1,), (1,)), ((), ())), preferred_element_type=F32)


def mm_tn(left, right):
    return lax.dot_general(left, right, (((0,), (0,)), ((), ())), preferred_element_type=F32)


def round_up(value, step):
    return -(-value // step) * step


def head_window(slot, head_width):
    first = slot * head_width // LANES * LANES
    last = round_up((slot + 1) * head_width, LANES)
    return first, last - first, slot * head_width - first


def head_mask(lanes, offset, head_width):
    lane = lax.broadcasted_iota(jnp.int32, (1, lanes), 1)
    return jnp.where((lane >= offset) & (lane < offset + head_width), 1.0, 0.0).astype(BF16)


def unit_rows(values):
    centred = values - jnp.mean(values, axis=-1, keepdims=True)
    inverse = lax.rsqrt(jnp.mean(centred * centred, axis=-1, keepdims=True) + EPSILON)
    return centred * inverse, inverse


def norm_back(grad_out, unit, inverse, gain_row):
    grad_unit = grad_out * gain_row
    first_mean = jnp.mean(grad_unit, axis=-1, keepdims=True)
    second_mean = jnp.mean(grad_unit * unit, axis=-1, keepdims=True)
    return inverse * (grad_unit - first_mean - unit * second_mean)


def add_tiles(tiles, product, first):
    for part in range(product.shape[1] // LANES):
        place = first // LANES + part
        piece = product[:, part * LANES : (part + 1) * LANES]
        tiles[place] = piece if tiles[place] is None else tiles[place] + piece


def squeeze_part(part, side, stride):
    each = LANES // side
    first = part * each * stride // LANES * LANES
    last = round_up((part * each + each - 1) * stride + side, LANES)
    wide = lax.broadcasted_iota(jnp.int32, (last - first, LANES), 0) + first
    close = lax.broadcasted_iota(jnp.int32, (last - first, LANES), 1)
    same = wide == (part * each + close // side) * stride + close % side
    return first, last - first, jnp.where(same, 1.0, 0.0).astype(BF16)


def place_matrix(relative_row, side):
    stride = 2 * side - 1
    entry = relative_row.astype(F32)
    row_part = jnp.floor((entry + 0.5) * (1.0 / stride))
    column_part = entry - row_part * stride
    row_part = jnp.max(row_part, axis=1, keepdims=True) - row_part
    column_part = jnp.max(column_part, axis=1, keepdims=True) - column_part
    cells = (row_part * side + column_part).astype(jnp.int32)
    length = side * side
    cell = lax.broadcasted_iota(jnp.int32, (length, length), 0)
    return jnp.where(cell == cells, 1.0, 0.0).astype(BF16)


def split_two(values):
    high = values.astype(BF16)
    return high, (values - high.astype(F32)).astype(BF16)


def attend_kernel(
    dims,
    ranks,
    steps_ref,
    relative_ref,
    table_ref,
    params,
    tokens_hbm,
    times_hbm,
    query_hbm,
    key_hbm,
    value_hbm,
    time_query_hbm,
    time_value_hbm,
    out_hbm,
    query_ref,
    key_ref,
    value_ref,
    probs_ref,
    mixed_0,
    mixed_1,
    mixed_2,
    mixed_3,
    middle_ref,
    normed_ref,
    embed_ref,
    weights,
    own_tokens,
    times,
    table,
    wide_high,
    wide_low,
    windows,
    flat,
    mixed_ref,
    sems,
):
    groups, slots, head_width, side, scale = dims
    group_width = slots * head_width
    rank = ranks[0]
    length = side * side
    step = steps_ref[rank]
    own_copy = pltpu.make_async_copy(
        tokens_hbm.at[pl.ds(pl.multiple_of(rank * length, length), length)], own_tokens, sems.at[6]
    )
    own_copy.start()
    sources = (query_hbm, key_hbm, value_hbm, time_query_hbm, time_value_hbm, out_hbm)
    copies = {}
    for item in (0, 1, 3, 2, 4, 5):
        copies[item] = pltpu.make_async_copy(sources[item], weights.at[item], sems.at[item])
        copies[item].start()
    times_copy = pltpu.make_async_copy(times_hbm.at[step // 8], times, sems.at[7])
    times_copy.start()
    stride = 2 * side - 1
    heads = groups * slots
    row_lanes = table.shape[1]
    table[...] = jnp.zeros_like(table)
    table[:, : stride * stride] = table_ref[...]
    for head in range(heads):
        row = jnp.broadcast_to(table[head : head + 1, :], (side, row_lanes))
        shifted = pltpu.roll(row, row_lanes - (side - 1), 1, stride=1, stride_axis=0)
        high, low = split_two(shifted)
        wide_high[head * side : (head + 1) * side, :] = high
        wide_low[head * side : (head + 1) * side, :] = low
    span_lanes = windows.shape[2]
    for part in range(span_lanes // LANES):
        first, lanes, squeeze = squeeze_part(part, side, stride)
        span = slice(first, first + lanes)
        narrow = mm(wide_high[:, span], squeeze) + mm(wide_low[:, span], squeeze)
        windows[:, :, part * LANES : (part + 1) * LANES] = narrow.reshape(heads, side, LANES)
    place = place_matrix(relative_ref[0:1, :], side)
    own_copy.wait()
    own = mm(place, own_tokens[...])
    unit, _ = unit_rows(own)
    normed = (unit * params[0:1, :] + params[1:2, :]).astype(BF16)

    def into_groups(rows, target):
        fill = jnp.zeros((rows.shape[0], target.shape[2] - group_width), rows.dtype)
        for group in range(groups):
            piece = rows[:, group * group_width : (group + 1) * group_width]
            target[group] = jnp.concatenate([piece, fill], axis=1)

    copies[0].wait()
    query = mm(normed, weights[0])
    copies[1].wait()
    into_groups(mm(normed, weights[1]).astype(BF16), key_ref)
    key_ref.send()
    times_copy.wait()
    line = lax.broadcasted_iota(jnp.int32, times.shape, 0)
    chosen = jnp.where(line == step % 8, times[...].astype(F32), 0.0)
    embed = jnp.broadcast_to(jnp.sum(chosen, axis=0, keepdims=True), times.shape)
    embed_ref[...] = embed
    embed = embed.astype(BF16)
    copies[3].wait()
    into_groups((query + mm(embed, weights[3])[0:1]).astype(BF16), query_ref)
    query_ref.send()
    copies[2].wait()
    value = mm(normed, weights[2])
    copies[4].wait()
    into_groups((value + mm(embed, weights[4])[0:1]).astype(BF16), value_ref)
    value_ref.send()

    def one_group(group, carry):
        tiles = [None] * (query_ref.shape[2] // LANES)
        for slot in range(slots):
            head = group * slots + slot
            first, lanes, offset = head_window(slot, head_width)
            mask = head_mask(lanes, offset, head_width)
            window = windows[head]
            blocks = [None] * side
            steps = LANES // side
            for turn in range(steps):
                turned = window
                if turn:
                    turned = pltpu.roll(window, span_lanes - turn * side, 1)
                for jump in range(-(-side // steps)):
                    block = side - 1 - (jump * steps + turn)
                    if block >= 0:
                        blocks[block] = turned[:, jump * LANES : jump * LANES + length]
            bias = jnp.concatenate(blocks, axis=0)
            keys = key_ref[group, :, first : first + lanes]
            queries = query_ref[group, :, first : first + lanes] * mask
            scores = mm_nt(keys, queries) * scale + bias
            weights_now = jnp.exp(scores - jnp.max(scores, axis=0, keepdims=True))
            totals = jnp.sum(weights_now, axis=0, keepdims=True)
            probs = (weights_now * (1.0 / totals)).astype(BF16)
            probs_ref[head] = probs
            values = value_ref[group, :, first : first + lanes] * mask
            add_tiles(tiles, mm_tn(probs, values), first)
        mixed_ref[group] = jnp.concatenate(tiles, axis=1).astype(BF16)
        return carry

    lax.fori_loop(0, groups, one_group, 0)
    probs_ref.send()
    for group in range(groups):
        flat[:, group * group_width : (group + 1) * group_width] = mixed_ref[group][:, :group_width]
    for away, target in enumerate((mixed_0, mixed_1, mixed_2, mixed_3)):
        target[...] = mixed_ref[rank ^ away]
        target.send()
    copies[5].wait()
    middle = own + mm(flat[...], weights[5]) + params[4:5, :]
    middle_ref[...] = middle
    middle_ref.send()
    unit, _ = unit_rows(middle)
    normed_ref[...] = (unit * params[2:3, :] + params[3:4, :]).astype(BF16)


def normed_kernel(side, ranks, relative_ref, tokens_ref, params, dep, other, normed_ref):
    unit, _ = unit_rows(mm(place_matrix(relative_ref[0:1, :], side), tokens_ref[...]))
    normed_ref[...] = (unit * params[0:1, :] + params[1:2, :]).astype(BF16)


def gelu_pair(hidden):
    root = math.sqrt(2.0 / math.pi)
    square = hidden * hidden
    bend = jnp.tanh(hidden * (root + (root * 0.044715) * square))
    half = 0.5 + 0.5 * bend
    slope = half + (0.5 * hidden) * (1.0 - bend * bend) * (root + (3.0 * root * 0.044715) * square)
    return hidden * half, slope


def feed_rows(side, relative_ref, normed, cotangent, up_ref, up_bias, down_ref, active, hidden, moved):
    place = place_matrix(relative_ref[0:1, :], side)
    rows = place.shape[0]
    for chunk in range(len(normed)):
        span = slice(chunk * rows, (chunk + 1) * rows)
        turned = mm(place, cotangent[chunk][...]).astype(BF16)
        moved[span, :] = turned
        gelu_out, slope = gelu_pair(mm(normed[chunk][...], up_ref[...]) + up_bias[...])
        active[span, :] = gelu_out.astype(BF16)
        hidden[span, :] = (mm_nt(turned, down_ref[...]) * slope).astype(BF16)


def feed_near_kernel(
    side,
    relative_ref,
    normed_own,
    normed_near,
    cot_own,
    cot_near,
    up_ref,
    up_bias,
    down_ref,
    active,
    hidden,
    moved,
    grad_own,
    grad_near,
):
    feed_rows(
        side,
        relative_ref,
        (normed_own, normed_near),
        (cot_own, cot_near),
        up_ref,
        up_bias,
        down_ref,
        active,
        hidden,
        moved,
    )
    active.send()
    moved.send()
    hidden.send()
    rows = grad_own.shape[0]
    grad_near[...] = mm_nt(hidden[rows:, :], up_ref[...]).astype(BF16)
    grad_near.send()
    grad_own[...] = mm_nt(hidden[:rows, :], up_ref[...]).astype(BF16)


def halves(values, bit):
    half = values.shape[0] // 2
    low, high = values[:half], values[half:]
    return jnp.where(bit == 0, low, high), jnp.where(bit == 0, high, low)


def feed_far_kernel(
    side,
    relative_ref,
    normed_far,
    normed_last,
    cot_far,
    cot_last,
    up_ref,
    up_bias,
    down_ref,
    near_hidden,
    active,
    hidden,
    moved,
    grad_far,
    grad_last,
    bias_ref,
):
    feed_rows(
        side,
        relative_ref,
        (normed_far, normed_last),
        (cot_far, cot_last),
        up_ref,
        up_bias,
        down_ref,
        active,
        hidden,
        moved,
    )
    rows = grad_far.shape[0]
    grad_last[...] = mm_nt(hidden[rows:, :], up_ref[...]).astype(BF16)
    grad_far[...] = mm_nt(hidden[:rows, :], up_ref[...]).astype(BF16)
    total = jnp.sum(hidden[...].astype(F32), axis=0, keepdims=True)
    total = total + jnp.sum(near_hidden[...].astype(F32), axis=0, keepdims=True)
    bias_ref[...] = jnp.broadcast_to(total, bias_ref.shape)


def down_grad_kernel(level, ranks, near_active, near_moved, active, moved, keep_ref, send_ref):
    grad = mm_tn(near_active[...], near_moved[...]) + mm_tn(active[...], moved[...])
    keep, send = halves(grad.astype(BF16), (ranks[1] >> level) & 1)
    send_ref[...] = send
    keep_ref[...] = keep


def up_grad_kernel(
    level, ranks, own, near, far, last, near_hidden, hidden, keep_ref, send_ref, normed
):
    rows = own.shape[0]
    for chunk, ref in enumerate((own, near, far, last)):
        normed[chunk * rows : (chunk + 1) * rows, :] = ref[...]
    grad = mm_tn(normed[: 2 * rows, :], near_hidden[...]) + mm_tn(normed[2 * rows :, :], hidden[...])
    keep, send = halves(grad.astype(BF16), (ranks[1] >> level) & 1)
    send_ref[...] = send
    send_ref.send()
    keep_ref[...] = keep


def out_kernel(near_active, active, down_ref, keep_ref, send_ref):
    rows = keep_ref.shape[1]
    keep_ref[0] = mm(near_active[:rows, :], down_ref[...]).astype(BF16)
    send_ref[0] = mm(near_active[rows:, :], down_ref[...]).astype(BF16)
    keep_ref[1] = mm(active[:rows, :], down_ref[...]).astype(BF16)
    send_ref[1] = mm(active[rows:, :], down_ref[...]).astype(BF16)


def add_kernel(left, right, out_ref):
    out_ref[...] = (left[...].astype(F32) + right[...].astype(F32)).astype(out_ref.dtype)


def middle_kernel(
    own_ref,
    near_ref,
    far_ref,
    middle_ref,
    moved_ref,
    params,
    branch_ref,
    grad_ref,
    sums_ref,
):
    rows = own_ref.shape[0]
    grad_normed = own_ref[...].astype(F32) + near_ref[...].astype(F32) + far_ref[...].astype(F32)
    unit, inverse = unit_rows(middle_ref[...])
    cotangent = moved_ref[:rows, :].astype(F32)
    grad_middle = cotangent + norm_back(grad_normed, unit, inverse, params[2:3, :])
    branch_ref[...] = grad_middle.astype(BF16)
    branch_ref.send()
    grad_ref[...] = grad_middle
    grad_ref.send()
    sums_ref[...] = jnp.zeros(sums_ref.shape, F32)
    sums_ref[0:1, :] = jnp.sum(grad_normed * unit, axis=0, keepdims=True)
    sums_ref[1:2, :] = jnp.sum(grad_normed, axis=0, keepdims=True)
    sums_ref[2:3, :] = jnp.sum(grad_middle, axis=0, keepdims=True)
    sums_ref[3:4, :] = jnp.sum(cotangent, axis=0, keepdims=True)


def attend_back_kernel(
    dims,
    picks,
    ranks,
    *refs,
):
    groups, slots, head_width, side, scale = dims
    group_width = slots * head_width
    rank = ranks[0]
    length = side * side
    if len(refs) == 11:
        branch_ref, out_ref, query_ref, key_ref, value_ref, probs_ref = refs[:6]
        packed_a, packed_b, grads, grad_mixed, sheared = refs[6:]
        fill = jnp.zeros((length, grad_mixed.shape[2] - group_width), BF16)
        product = mm_nt(branch_ref[...], out_ref[...]).astype(BF16)
        for group in range(groups):
            piece = product[:, group * group_width : (group + 1) * group_width]
            grad_mixed[group] = jnp.concatenate([piece, fill], axis=1)
        grad_mixed.send()
    else:
        grad_mixed, query_ref, key_ref, value_ref, probs_ref = refs[:5]
        packed_a, packed_b, grads, sheared = refs[5:]
        grad_mixed.ready()
    for ref in (query_ref, key_ref, value_ref, probs_ref):
        ref.ready()
    stride = 2 * side - 1
    span_lanes = sheared.shape[2]
    packed_lanes = packed_a.shape[1]
    table_lanes = round_up(stride * stride, LANES)

    def one_group(pick, carry):
        group = (picks[0] + pick) ^ rank
        wide = grad_mixed.shape[2] // LANES
        query_tiles, key_tiles, value_tiles = [None] * wide, [None] * wide, [None] * wide
        for slot in range(slots):
            head = group * slots + slot
            first, lanes, offset = head_window(slot, head_width)
            mask = head_mask(lanes, offset, head_width)
            span = slice(first, first + lanes)
            mixed_now = grad_mixed[group, :, span] * mask
            probs = probs_ref[head]
            grad_probs = mm_nt(value_ref[group, :, span], mixed_now)
            probs_wide = probs.astype(F32)
            weighted = probs_wide * grad_probs
            grad_scores = weighted - probs_wide * jnp.sum(weighted, axis=0, keepdims=True)
            rounded = grad_scores.astype(BF16)
            add_tiles(value_tiles, mm(probs, mixed_now), first)
            add_tiles(key_tiles, mm(rounded, query_ref[group, :, span] * mask), first)
            add_tiles(query_tiles, mm_tn(rounded, key_ref[group, :, span] * mask), first)
            steps = LANES // side
            shear = jnp.zeros((side, span_lanes), F32)
            for turn in range(steps):
                summed = None
                for jump in range(-(-side // steps)):
                    block = side - 1 - (jump * steps + turn)
                    if block >= 0:
                        piece = grad_scores[block * side : (block + 1) * side, :]
                        parts = []
                        if jump:
                            parts.append(jnp.zeros((side, jump * LANES), F32))
                        parts.append(piece)
                        rest = span_lanes - jump * LANES - length
                        if rest:
                            parts.append(jnp.zeros((side, rest), F32))
                        piece = jnp.concatenate(parts, axis=1)
                        summed = piece if summed is None else summed + piece
                shear = shear + (pltpu.roll(summed, turn * side, 1) if turn else summed)
            sheared[:, pl.ds(pick * slots + slot, 1), :] = shear[:, None, :]
        query = (jnp.concatenate(query_tiles, axis=1) * scale).astype(BF16)
        key = (jnp.concatenate(key_tiles, axis=1) * scale).astype(BF16)
        value = jnp.concatenate(value_tiles, axis=1).astype(BF16)
        grads[0, pick] = query
        grads[1, pick] = key
        grads[2, pick] = value
        return carry

    lax.fori_loop(0, len(picks), one_group, 0)
    selections = [squeeze_part(part, side, stride) for part in range(span_lanes // LANES)]
    heads = 2 * slots
    tall = table_lanes // LANES
    total = [jnp.zeros((heads, LANES), F32)] * tall
    for column in range(side):
        high, low = split_two(sheared[column])
        tiles = [None] * tall
        for part, (first, lanes, squeeze) in enumerate(selections):
            span = slice(part * LANES, (part + 1) * LANES)
            add_tiles(tiles, mm_nt(high[:, span], squeeze) + mm_nt(low[:, span], squeeze), first)
        spread = jnp.concatenate(
            [jnp.zeros((heads, LANES), F32) if tile is None else tile for tile in tiles], axis=1
        )
        turn = side - 1 - column
        turned = pltpu.roll(spread, turn, 1) if turn else spread
        total = [
            old + turned[:, place * LANES : (place + 1) * LANES] for place, old in enumerate(total)
        ]
    for pick, packed_ref in enumerate((packed_a, packed_b)):
        for place in range(tall):
            packed_ref[length + place * slots : length + (place + 1) * slots, :LANES] = total[place][
                pick * slots : (pick + 1) * slots
            ].astype(BF16)
        pieces = [grads[item, pick][:, :group_width] for item in range(3)]
        if packed_lanes > 3 * group_width:
            pieces.append(jnp.zeros((length, packed_lanes - 3 * group_width), BF16))
        packed_ref[:length, :] = jnp.concatenate(pieces, axis=1)


def tokens_kernel(
    dims,
    ranks,
    steps_ref,
    near_grads,
    far_grads,
    query_ref,
    key_ref,
    value_ref,
    relative_ref,
    params,
    middle_ref,
    middle_sums,
    embed_ref,
    up_bias_ref,
    tokens_hbm,
    image_ref,
    grad_ref,
    flat,
    own_tokens,
    sem,
):
    groups, slots, head_width, side, scale = dims
    group_width = slots * head_width
    rank = ranks[0]
    length = side * side
    own_copy = pltpu.make_async_copy(
        tokens_hbm.at[pl.ds(pl.multiple_of(rank * length, length), length)], own_tokens, sem
    )
    own_copy.start()
    for group in range(groups):
        away = group ^ rank
        for item in range(3):
            piece = jnp.where(away >= 2, far_grads[item, away & 1], near_grads[item, away & 1])
            flat[item, :, group * group_width : (group + 1) * group_width] = piece[:, :group_width]
    grad_normed = (
        mm_nt(flat[0], query_ref[...])
        + mm_nt(flat[1], key_ref[...])
        + mm_nt(flat[2], value_ref[...])
    )
    place = place_matrix(relative_ref[0:1, :], side)
    own_copy.wait()
    unit, inverse = unit_rows(mm(place, own_tokens[...]))
    total = middle_ref[...] + norm_back(grad_normed, unit, inverse, params[0:1, :])
    high, low = split_two(total)
    grad_ref[...] = mm_tn(place, high) + mm_tn(place, low)
    grad_ref.send()
    step = steps_ref[rank]
    sums = [
        jnp.sum(flat[0].astype(F32), axis=0, keepdims=True),
        jnp.sum(flat[2].astype(F32), axis=0, keepdims=True),
        embed_ref[0:1, :],
        jnp.full((1, embed_ref.shape[1]), (step // 8).astype(F32)),
        jnp.full((1, embed_ref.shape[1]), (step % 8).astype(F32)),
        middle_sums[0:4, :],
        jnp.sum(grad_normed * unit, axis=0, keepdims=True),
        jnp.sum(grad_normed, axis=0, keepdims=True),
        up_bias_ref[0:1, :],
        jnp.zeros((4, embed_ref.shape[1]), F32),
    ]
    image_ref[...] = jnp.concatenate(sums, axis=0).astype(BF16)
    image_ref.send()


def weights_kernel(dims, level, ranks, normed, *refs):
    groups, slots, head_width, side, scale = dims
    group_width = slots * head_width
    rows = side * side
    keep_first, keep_second, send_first, send_second, packed, branch, mixed = refs[3 * groups :]
    table = None
    for chunk in range(groups):
        span = slice(chunk * rows, (chunk + 1) * rows)
        source = refs[chunk]
        packed[span, :] = source[:rows, :]
        branch[span, :] = refs[groups + chunk][...]
        mixed[span, :] = refs[2 * groups + chunk][...]
        part = source[rows:, :LANES].astype(F32)
        table = part if table is None else table + part
    bit = (ranks[1] >> level) & 1
    left = mm_tn(packed[...], normed[...]).astype(BF16)
    right = mm_tn(mixed[...], branch[...]).astype(BF16)
    keep_first[...], send_first[...] = halves(left[: 2 * group_width], bit)
    value, out = left[2 * group_width : 3 * group_width], right[:group_width]
    low, high = halves(table.astype(BF16), bit)
    fill = jnp.zeros((low.shape[0], value.shape[1] - LANES), BF16)
    keep_second[:group_width, :] = jnp.where(bit == 0, value, out)
    keep_second[group_width:, :] = jnp.concatenate([low, fill], axis=1)
    send_second[:group_width, :] = jnp.where(bit == 0, out, value)
    send_second[group_width:, :] = jnp.concatenate([high, fill], axis=1)


def split_kernel(level, tail, ranks, kept, got, keep_ref, send_ref):
    total = (kept[...].astype(F32) + got[...].astype(F32)).astype(BF16)
    bit = (ranks[1] >> level) & 1
    body = total.shape[0] - tail
    keep, send = halves(total[:body], bit)
    send_ref[: body // 2, :] = send
    keep_ref[: body // 2, :] = keep
    if tail:
        keep, send = halves(total[body:], bit)
        send_ref[body // 2 :, :] = send
        keep_ref[body // 2 :, :] = keep


def join_kernel(level, tail, ranks, own, other, out_ref):
    body = own.shape[0] - tail
    bit = (ranks[1] >> level) & 1
    low = jnp.where(bit == 0, own[...], other[...])
    high = jnp.where(bit == 0, other[...], own[...])
    out_ref[:body, :] = low[:body]
    out_ref[body : 2 * body, :] = high[:body]
    if tail:
        out_ref[2 * body : 2 * body + tail, :] = low[body:]
        out_ref[2 * body + tail :, :] = high[body:]


def widen_kernel(level, ranks, own, other, out_ref):
    bit = (ranks[1] >> level) & 1
    first = (pl.program_id(0) < pl.num_programs(0) // 2) == (bit == 0)

    @pl.when(first)
    def _():
        out_ref[...] = own[...].astype(F32)

    @pl.when(jnp.logical_not(first))
    def _():
        out_ref[...] = other[...].astype(F32)


def widen_pair_kernel(level, tail, ranks, own, other, low_ref, high_ref, *refs):
    bit = (ranks[1] >> level) & 1
    body = own.shape[0] - tail
    low_ref[...] = jnp.where(bit == 0, own[:body, :], other[:body, :]).astype(F32)
    low_ref.send()
    high_ref[...] = jnp.where(bit == 0, other[:body, :], own[:body, :]).astype(F32)
    high_ref.send()
    if tail:
        table = refs[0]
        slots = table.shape[0]
        low = jnp.where(bit == 0, own[body:, :LANES], other[body:, :LANES]).astype(F32)
        high = jnp.where(bit == 0, other[body:, :LANES], own[body:, :LANES]).astype(F32)
        for part in range(table.shape[1] // LANES):
            source, row = (low, part * slots) if part * slots < tail else (high, part * slots - tail)
            table[:, part * LANES : (part + 1) * LANES] = source[row : row + slots]


def finish_kernel(
    dims, images, ranks, all_ref, query_hbm, value_hbm, query_ref, value_ref, table_ref, sums_ref,
    weights, sems,
):
    groups, slots, head_width, side, scale = dims
    group_width = slots * head_width
    rank = ranks[0]
    start = pl.multiple_of(rank * group_width, 16)
    copies = []
    for item, source in enumerate((query_hbm, value_hbm)):
        copy = pltpu.make_async_copy(
            source.at[pl.ds(start, group_width)], weights.at[item], sems.at[item]
        )
        copy.start()
        copies.append(copy)

    def own_columns(rows):
        chosen = rows[:, :group_width]
        for group in range(1, groups):
            piece = rows[:, group * group_width : (group + 1) * group_width]
            chosen = jnp.where(rank == group, piece, chosen)
        return chosen

    sums_ref[...] = jnp.zeros(sums_ref.shape, F32)
    embed = all_ref[2]
    totals = None
    for item, target in enumerate((query_ref, value_ref)):
        rows = all_ref[item]
        target[...] = mm_tn(own_columns(rows), embed)
        target.send()
        copies[item].wait()
        part = mm_nt(rows, weights[item])
        totals = part if totals is None else totals + part
    steps = all_ref[3][:, 0:1].astype(F32) * 8.0 + all_ref[4][:, 0:1].astype(F32)
    step = lax.broadcasted_iota(jnp.int32, (images, table_ref.shape[1]), 1)
    chosen = jnp.where(step == steps.astype(jnp.int32), 1.0, 0.0).astype(BF16)
    high, low = split_two(totals)
    table_ref[...] = mm_tn(high, chosen) + mm_tn(low, chosen)
    table_ref.send()
    for item in range(6):
        total = jnp.sum(all_ref[5 + item].astype(F32), axis=0, keepdims=True)
        sums_ref[item : item + 1, :group_width] = own_columns(total)
    image = lax.broadcasted_iota(jnp.int32, (images, 1), 0)
    mine = jnp.where(image % groups == rank, all_ref[11].astype(F32), 0.0)
    sums_ref[6:7, :] = jnp.sum(mine, axis=0, keepdims=True)


def block_kernel(side, relative_ref, own, near, far, middle_ref, params, out_ref):
    total = own[0].astype(F32) + near[0].astype(F32) + far[...].astype(F32)
    total = (middle_ref[...] + total + params[5:6, :]).astype(BF16)
    place = place_matrix(relative_ref[0:1, :], side)
    out_ref[...] = mm_tn(place, total).astype(BF16)


def shape_of(*sizes, dtype=BF16):
    return jax.ShapeDtypeStruct(sizes, dtype)


VMEM = pl.BlockSpec(memory_space=pltpu.VMEM)
HBM = pl.BlockSpec(memory_space=pl.ANY)
SMEM = pl.BlockSpec(memory_space=pltpu.SMEM)
MIB = 1024 * 1024
FEED = 20


def cost(us):
    return pl.CostEstimate(flops=int(us * 1.15e9), bytes_accessed=1000, transcendentals=0)


class Staged:
    def __init__(self, source, target, sem):
        self.ref, self.waited = target, False
        self.copy = pltpu.make_async_copy(source, target, sem)
        self.copy.start()
        self.shape = target.shape

    def ready(self):
        if not self.waited:
            self.waited = True
            self.copy.wait()
        return self.ref

    def __getitem__(self, place):
        return self.ready()[place]


class Result:
    def __init__(self, ref, target=None, sem=None):
        self.ref, self.sent = ref, target is None
        self.copy = None if self.sent else pltpu.make_async_copy(ref, target, sem)
        self.shape, self.dtype = ref.shape, ref.dtype

    def __getitem__(self, place):
        return self.ref[place]

    def __setitem__(self, place, value):
        self.ref[place] = value

    def send(self):
        if not self.sent:
            self.sent = True
            self.copy.start()


class Held:
    def __init__(self, ref):
        self.ref, self.shape = ref, ref.shape

    def ready(self):
        return self.ref

    def __getitem__(self, place):
        return self.ref[place]


def run(kernel, outs, inputs, kinds=None, scratch=(), deps=(), us=0.2, away=(), vmem=40):
    kinds = "v" * len(inputs) if kinds is None else kinds
    assert len(kinds) == len(inputs)
    single = not isinstance(outs, (list, tuple))
    outs = [outs] if single else list(outs)
    staged = [place for place, kind in enumerate(kinds) if kind == "w"]
    count, extra, results = len(inputs), len(deps), len(outs)
    buffers = [pltpu.VMEM(inputs[place].shape, inputs[place].dtype) for place in staged]
    buffers += [pltpu.VMEM(outs[place].shape, outs[place].dtype) for place in away]
    if buffers:
        buffers.append(pltpu.SemaphoreType.DMA((len(buffers),)))

    def body(*refs):
        given = list(refs[:count])
        targets = refs[count + extra : count + extra + results]
        rest = refs[count + extra + results :]
        for place, kind in enumerate(kinds):
            if kind == "v":
                given[place] = Held(given[place])
        for order, place in enumerate(staged):
            sem = rest[len(buffers) - 1].at[order]
            given[place] = Staged(given[place], rest[order], sem)
        made = []
        for place, target in enumerate(targets):
            if place in away:
                order = len(staged) + away.index(place)
                made.append(Result(rest[order], target, rest[len(buffers) - 1].at[order]))
            else:
                made.append(Result(target))
        kernel(*given, *made, *rest[len(buffers) :])
        for result in made:
            result.send()
        for place in staged:
            given[place].ready()
        for result in made:
            if result.copy is not None:
                result.copy.wait()

    space = {"s": SMEM, "h": HBM, "v": VMEM, "w": HBM}
    found = pl.pallas_call(
        body,
        out_shape=outs,
        in_specs=[space[kind] for kind in kinds] + [HBM] * extra,
        out_specs=[HBM if place in away else VMEM for place in range(results)],
        scratch_shapes=buffers + list(scratch),
        compiler_params=pltpu.CompilerParams(vmem_limit_bytes=vmem * MIB),
        cost_estimate=cost(us),
    )(*inputs, *deps)
    return found[0] if single else found


def quick(kernel, outs, inputs, deps=()):
    count = len(inputs)

    def body(*refs):
        kernel(*refs[:count], *refs[count + len(deps) :])

    specs = [SMEM if given.shape == (2,) else VMEM for given in inputs]
    return pl.pallas_call(
        body,
        out_shape=outs,
        in_specs=specs + [HBM] * len(deps),
        out_specs=jax.tree.map(lambda _: VMEM, outs),
        compiler_params=pltpu.CompilerParams(vmem_limit_bytes=4 * MIB),
        cost_estimate=cost(0.1),
    )(*inputs, *deps)


def widen(ranks, level, own, other):
    half, columns = own.shape
    parts = 2
    block = half // parts

    def own_map(i, me):
        bit = (me[1] >> level) & 1
        return (jnp.clip(i - parts * bit, 0, parts - 1), 0)

    def other_map(i, me):
        bit = (me[1] >> level) & 1
        return (jnp.clip(i - parts * (1 - bit), 0, parts - 1), 0)

    return pl.pallas_call(
        partial(widen_kernel, level),
        out_shape=shape_of(2 * half, columns, dtype=F32),
        grid_spec=pltpu.PrefetchScalarGridSpec(
            num_scalar_prefetch=1,
            grid=(2 * parts,),
            in_specs=[
                pl.BlockSpec((block, columns), own_map),
                pl.BlockSpec((block, columns), other_map),
            ],
            out_specs=pl.BlockSpec((block, columns), lambda i, me: (i, 0)),
        ),
        compiler_params=pltpu.CompilerParams(vmem_limit_bytes=16 * MIB),
        cost_estimate=cost(5.0),
    )(ranks, own, other)


def swap(array, axis, distance):
    size = lax.axis_size(axis)
    return lax.ppermute(array, axis, [(i, i ^ distance) for i in range(size)])


def after(array, *others):
    return lax.optimization_barrier((array, *others))[0]


class Total:
    def __init__(self, ranks, order, keep, send, tail=0):
        self.ranks, self.order, self.tail = ranks, order, tail
        self.keep = keep
        self.got = self.swap(0, send)

    def swap(self, place, array):
        return swap(array, "dp", 1 << self.order[place])

    def split(self, deps=()):
        half, columns = self.keep.shape
        part = shape_of(half // 2, columns)
        self.keep, send = quick(
            partial(split_kernel, self.order[1], self.tail),
            [part, part],
            [self.ranks, self.keep, self.got],
            deps,
        )
        self.got = self.swap(1, send)
        return self.keep

    def add(self, place, deps=()):
        self.keep = quick(add_kernel, shape_of(*self.keep.shape), [self.keep, self.got], deps)
        self.got = self.swap(place, self.keep)
        return self.keep

    def join(self, deps=()):
        half, columns = self.keep.shape
        self.keep = quick(
            partial(join_kernel, self.order[1], self.tail // 2),
            shape_of(2 * half, columns),
            [self.ranks, self.keep, self.got],
            deps,
        )
        self.got = self.swap(0, self.keep)
        return self.keep

    def advance(self, stage, deps=()):
        levels = len(self.order)
        if stage == 0:
            return self.split(deps)
        if stage < levels - 1:
            return self.add(stage + 1, deps)
        if stage == levels - 1:
            return self.add(1, deps)
        return self.join(deps)


def add_low(left, right):
    return (left.astype(F32) + right.astype(F32)).astype(BF16)


def on_device(
    tokens,
    timesteps,
    relative_index,
    time_table,
    query_weight,
    key_weight,
    value_weight,
    time_query_weight,
    time_value_weight,
    out_weight,
    out_bias,
    first_gain,
    first_shift,
    second_gain,
    second_shift,
    up_weight,
    up_bias,
    down_weight,
    down_bias,
    bias_table,
    cotangent,
):
    length = relative_index.shape[0]
    width = tokens.shape[1]
    heads = bias_table.shape[1]
    head_width = width // heads
    side = math.isqrt(length)
    stride = 2 * side - 1
    groups = lax.axis_size("mp")
    dp_size = lax.axis_size("dp")
    rank = lax.axis_index("mp")
    ranks = jnp.stack([rank, lax.axis_index("dp")]).astype(jnp.int32)
    slots = heads // groups
    group_width = slots * head_width
    group_lanes = round_up(group_width, LANES)
    packed_lanes = round_up(3 * group_width, LANES)
    table_lanes = round_up(stride * stride, LANES)
    span_lanes = round_up(stride * side, LANES)
    hidden_width = up_weight.shape[1]
    rows = groups * length
    dims = (groups, slots, head_width, side, head_width ** (-0.5))
    line = lambda vector: vector.reshape(1, -1)
    params = jnp.stack(
        [first_gain, first_shift, second_gain, second_shift, out_bias, down_bias]
        + [jnp.zeros_like(down_bias)] * 2
    )
    levels = list(range(dp_size.bit_length() - 1))
    other_order = levels[1::-1] + levels[2:]

    def grouped():
        return shape_of(groups, length, group_lanes)

    one_group = shape_of(length, group_lanes)

    cot_near = swap(cotangent, "mp", 1)
    cot_far = swap(cotangent, "mp", 2)
    steps = time_table.shape[0]
    outs = run(
        partial(attend_kernel, dims),
        [
            grouped(),
            grouped(),
            grouped(),
            shape_of(heads, length, length),
            one_group,
            one_group,
            one_group,
            one_group,
            shape_of(length, width, dtype=F32),
            shape_of(length, width),
            shape_of(8, width, dtype=F32),
        ],
        [
            ranks,
            timesteps,
            relative_index,
            bias_table.T,
            params,
            tokens,
            time_table.reshape(steps // 8, 8, width),
            query_weight,
            key_weight,
            value_weight,
            time_query_weight,
            time_value_weight,
            out_weight,
        ],
        "ssvvv" + "h" * 8,
        [
            pltpu.VMEM((6, width, width), BF16),
            pltpu.VMEM((length, width), BF16),
            pltpu.VMEM((8, width), BF16),
            pltpu.VMEM((heads, table_lanes), F32),
            pltpu.VMEM((heads * side, table_lanes), BF16),
            pltpu.VMEM((heads * side, table_lanes), BF16),
            pltpu.VMEM((heads, side, span_lanes), F32),
            pltpu.VMEM((length, width), BF16),
            pltpu.VMEM((groups, length, group_lanes), BF16),
            pltpu.SemaphoreType.DMA((8,)),
        ],
        us=16.0,
        vmem=54,
    )
    query_rows, key_rows, value_rows, probs = outs[:4]
    mixed = outs[4:8]
    middle, normed_own, embed = outs[8:]
    normed_near = swap(normed_own, "mp", 1)
    normed_far = swap(normed_own, "mp", 2)

    normed_first = pl.pallas_call(
        partial(normed_kernel, side),
        out_shape=shape_of(rows, width),
        grid_spec=pltpu.PrefetchScalarGridSpec(
            num_scalar_prefetch=1,
            grid=(groups,),
            in_specs=[
                pl.BlockSpec((8, length), lambda i, me: (0, 0)),
                pl.BlockSpec((length, width), lambda i, me: (i ^ me[0], 0)),
                pl.BlockSpec((8, width), lambda i, me: (0, 0)),
                HBM,
                HBM,
            ],
            out_specs=pl.BlockSpec((length, width), lambda i, me: (i, 0)),
        ),
        compiler_params=pltpu.CompilerParams(vmem_limit_bytes=40 * MIB),
        cost_estimate=cost(0.3),
    )(ranks, relative_index, tokens, params, normed_own, cot_far)

    cot_last = swap(cot_far, "mp", 1)
    pair = shape_of(2 * length, width)
    hidden_pair = shape_of(2 * length, hidden_width)
    chunk = shape_of(length, width)
    near_active, near_hidden, near_moved, grad_own, grad_near = run(
        partial(feed_near_kernel, side),
        [hidden_pair, hidden_pair, pair, chunk, chunk],
        [
            relative_index,
            normed_own,
            normed_near,
            cotangent,
            cot_near,
            up_weight,
            line(up_bias),
            down_weight,
        ],
        "vvvvvwvw",
        deps=[normed_first, cot_last],
        us=7.0,
        vmem=FEED,
    )
    near_got = swap(grad_near, "mp", 1)
    normed_last = swap(after(normed_far, grad_near), "mp", 1)
    mixed_got = [swap(mixed[away], "mp", away) for away in range(1, groups)]
    active, hidden, moved, grad_far, grad_last, up_bias_sum = run(
        partial(feed_far_kernel, side),
        [hidden_pair, hidden_pair, pair, chunk, chunk, shape_of(8, hidden_width, dtype=F32)],
        [
            relative_index,
            normed_far,
            normed_last,
            cot_far,
            cot_last,
            up_weight,
            line(up_bias),
            down_weight,
            near_hidden,
        ],
        "vvvvvwvwv",
        us=9.0,
        deps=[near_got],
        vmem=FEED,
    )
    last_got = swap(grad_last, "mp", 1)
    half = shape_of(hidden_width // 2, width)
    keep, send = run(
        partial(down_grad_kernel, levels[0]),
        [half, half],
        [ranks, near_active, near_moved, active, moved],
        "svvvv",
        deps=[up_bias_sum] + mixed_got,
        vmem=FEED,
    )
    down = Total(ranks, levels, keep, send)
    grad_sent = run(add_kernel, chunk, [grad_far, last_got], deps=[keep], vmem=4)
    far_got = swap(grad_sent, "mp", 2)
    half = shape_of(width // 2, hidden_width)
    keep, send = run(
        partial(up_grad_kernel, other_order[0]),
        [half, half],
        [ranks, normed_own, normed_near, normed_far, normed_last, near_hidden, hidden],
        "s" + "v" * 6,
        [pltpu.VMEM((rows, width), BF16)],
        deps=[grad_sent],
        us=0.4,
        vmem=FEED,
    )
    up = Total(ranks, other_order, keep, send)
    chunks = shape_of(2, length, width)
    out_keep, out_send = run(
        out_kernel, [chunks, chunks], [near_active, active, down_weight], "vvw", deps=[keep], us=0.4, vmem=FEED
    )
    out_got = swap(out_send, "mp", 1)
    grad_branch, grad_middle, middle_sums = run(
        middle_kernel,
        [chunk, shape_of(length, width, dtype=F32), shape_of(8, width, dtype=F32)],
        [grad_own, near_got, far_got, middle, near_moved, params],
        deps=[out_keep],
        vmem=8,
    )
    branch_near = swap(grad_branch, "mp", 1)
    branch_far = swap(grad_branch, "mp", 2)
    last = down.advance(0, deps=[middle_sums])

    tail = slots * table_lanes // LANES
    back_scratch = [pltpu.VMEM((side, 2 * slots, span_lanes), F32)]
    grads_shape = shape_of(3, 2, length, group_lanes)
    packed_shape = shape_of(length + tail, packed_lanes)
    heads_in = [query_rows, key_rows, value_rows, probs]
    packed_2, packed_3, far_grads, grad_mixed = run(
        partial(attend_back_kernel, dims, (2, 3)),
        [packed_shape, packed_shape, grads_shape, grouped()],
        [ranks, grad_branch, out_weight] + heads_in,
        "svwvvvv",
        back_scratch,
        deps=[last, branch_near],
        us=0.8,
    )
    packed_2 = swap(packed_2, "mp", 2)
    packed_3 = swap(packed_3, "mp", 3)
    last = up.advance(0, deps=[grad_mixed])
    last = down.advance(1, deps=[last])
    packed_0, packed_1, near_grads = run(
        partial(attend_back_kernel, dims, (0, 1)),
        [packed_shape, packed_shape, grads_shape],
        [ranks, grad_mixed] + heads_in,
        "svvvvv",
        back_scratch,
        deps=[last],
        us=0.8,
    )
    last = up.advance(1, deps=[packed_0, branch_far, packed_2])
    packed_1 = swap(packed_1, "mp", 1)
    branch_last = swap(branch_far, "mp", 1)
    half = shape_of(group_width, width)
    more = shape_of(group_width + tail // 2, width)
    keep_first, keep_second, send_first, send_second = run(
        partial(weights_kernel, dims, levels[0]),
        [half, more, half, more],
        [ranks, normed_first, packed_0, packed_1, packed_2, packed_3]
        + [grad_branch, branch_near, branch_far, branch_last]
        + [mixed[0]]
        + mixed_got,
        "s" + "v" * 13,
        [
            pltpu.VMEM((rows, packed_lanes), BF16),
            pltpu.VMEM((rows, width), BF16),
            pltpu.VMEM((rows, group_lanes), BF16),
        ],
        deps=[last],
        us=0.5,
    )
    first = Total(ranks, levels, keep_first, send_first)
    second = Total(ranks, levels, keep_second, send_second, tail // 2)
    last = keep_second
    image_rows, tokens_grad = run(
        partial(tokens_kernel, dims),
        [shape_of(16, width), shape_of(length, width, dtype=F32)],
        [
            ranks,
            timesteps,
            near_grads,
            far_grads,
            query_weight,
            key_weight,
            value_weight,
            relative_index,
            params,
            grad_middle,
            middle_sums,
            embed,
            jnp.pad(up_bias_sum, ((0, 0), (0, width - hidden_width))),
            tokens,
        ],
        "ssvvwwwvvvvvvh",
        [
            pltpu.VMEM((3, length, width), BF16),
            pltpu.VMEM((length, width), BF16),
            pltpu.SemaphoreType.DMA,
        ],
        deps=[last],
        us=0.7,
        away=(1,),
        vmem=24,
    )
    image_all = lax.all_gather(image_rows, ("dp", "mp"), axis=0, tiled=True)
    last = image_rows

    out_far = swap(add_low(out_keep[1], out_got[1]), "mp", 2)

    stages = len(levels) + 1
    todo = [(down, 2), (first, 0), (second, 0), (down, 3), (first, 1), (second, 1), (up, 2)]
    todo += [(up, 3), (first, 2), (second, 2), (first, 3), (second, 3)]
    for stage in range(4, stages):
        todo += [(total, stage) for total in (down, up, first, second)]
    for total, stage in todo:
        last = total.advance(stage, deps=[last])
    down_grad = widen(ranks, levels[0], down.keep, down.got)
    up_grad = widen(ranks, other_order[0], up.keep, up.got)
    wide = shape_of(group_width, width, dtype=F32)
    query_grad, key_grad = run(
        partial(widen_pair_kernel, levels[0], 0),
        [wide, wide],
        [ranks, first.keep, first.got],
        "svv",
        away=(0, 1),
    )
    value_grad, out_grad, table_grad = run(
        partial(widen_pair_kernel, levels[0], tail // 2),
        [wide, wide, shape_of(slots, table_lanes, dtype=F32)],
        [ranks, second.keep, second.got],
        "svv",
        away=(0, 1),
    )

    images = dp_size * groups
    image_all = image_all.reshape(images, 16, width)[:, :12].transpose(1, 0, 2)
    time_query_grad, time_value_grad, time_table_grad, sums = run(
        partial(finish_kernel, dims, images),
        [
            shape_of(group_width, width, dtype=F32),
            shape_of(group_width, width, dtype=F32),
            shape_of(group_width, steps, dtype=F32),
            shape_of(8, width, dtype=F32),
        ],
        [ranks, image_all, time_query_weight, time_value_weight],
        "svhh",
        [pltpu.VMEM((2, group_width, width), BF16), pltpu.SemaphoreType.DMA((2,))],
        away=(0, 1, 2),
        vmem=24,
    )
    parts = [sums[j, :group_width] for j in range(6)]
    second_gain_grad, second_shift_grad, out_bias_grad, down_bias_grad = parts[:4]
    first_gain_grad, first_shift_grad = parts[4:]
    bias_table_grad = table_grad[:, : stride * stride].T
    up_bias_grad = sums[6, :hidden_width]

    block_out = run(
        partial(block_kernel, side),
        shape_of(length, width),
        [relative_index, out_keep, out_got, out_far, middle, params],
    )
    return (
        block_out,
        tokens_grad,
        time_table_grad.T,
        query_grad.T,
        key_grad.T,
        value_grad.T,
        time_query_grad.T,
        time_value_grad.T,
        out_grad,
        out_bias_grad,
        first_gain_grad,
        first_shift_grad,
        second_gain_grad,
        second_shift_grad,
        up_grad,
        up_bias_grad,
        down_grad,
        down_bias_grad,
        bias_table_grad,
    )


def solution(mesh):
    whole = P()
    rows = P(("dp", "mp"), None)
    columns = P(None, "mp")
    split = P("mp")
    placed = (
        (P("dp", None), P("dp"))
        + (whole,) * 13
        + (columns, split, P("mp", None), whole, whole, rows)
    )
    return jax.shard_map(
        on_device,
        mesh=mesh,
        in_specs=placed,
        out_specs=(rows, rows)
        + (columns,) * 6
        + (P("mp", None),)
        + (split,) * 5
        + (columns, split, P("mp", None), split, columns),
        check_vma=False,
    )
```

profile of v0, /device:TPU:0, one launch (start us, length us, event | category | flops | bytes accessed | tf_op | source)
XLA Modules:
  0.0 310.6 jit_solution(13674470750189799475)
XLA Ops:
  7.8 2.6 collective-permute-start.2
  15.8 18.1 %shard_map.348 = (bf16[4,256,384]{2,1,0:T(8,128)(2,1)}, bf16[4,256,384]{2,1,0:T(8,128)(2,1)}, bf16[4,256,384]{2,1,0:T(8,128)(2,1)}, bf16[16,256,256]{2,1,0:T(8,1...) custom-call(s32[2]{0:T(128)} %pad_add_fusion.refs_0_.ranks, ...), custom_call_target="tpu_custom_call" | custom-call | flops 18400000000 | bytes 1000 | tf_op jit(solution)/shard_map/pallas_call | solution.py:812
  35.6 3.5 %shard_map.349.refs_8_.refs_1_ = bf16[1024,1152]{1,0:T(8,128)(2,1)S(1)} custom-call(s32[2]{0:T(128)S(1)} %copy-done.36, s32[256,256]{1,0:T(8,128)S(1)} %copy-done.16, bf16[1024,1152]{1,0:T(8,128)(2,1)S(1)} %copy-done, f32[8,1152]{1,0:T(8,128)S(1)} %copy-done.24, bf16[256,1152]{1,0:T(8,128)(2,1)S(1)} %copy-done.17, ...), custom_call_target="tpu_custom_call" | custom-call | flops 345000000 | bytes 1000 | tf_op jit(solution)/shard_map/pallas_call | solution.py:1042
  39.2 7.1 %shard_map.350 = (bf16[512,1152]{1,0:T(8,128)(2,1)S(1)}, bf16[512,1152]{1,0:T(8,128)(2,1)S(1)}, bf16[512,1152]{1,0:T(8,128)(2,1)S(1)}, bf16[256,1152]{1,0:T(8,128)(2,1)S(1)}, bf16[256,1152]{1,0:T(8,128)(2,1)S(1)}) custom-call(s32[256,256]{1,0:T(8,128)S(1)} %copy-done.16, bf16[256,1152]{1,0:T(8,128)(2,1)S(1)} %copy-done.17, ...), custom_call_target="tpu_custom_call" | custom-call | flops 8049999872 | bytes 1000 | tf_op jit(solution)/shard_map/pallas_call | solution.py:812
  46.2 3.7 %collective-permute-done.4.refs_1_.refs_3_ = bf16[256,1152]{1,0:T(8,128)(2,1)S(1)} collective-permute-done((bf16[256,1152]{1,0:T(8,128)(2,1)}, bf16[256,1152]{1,0:T(8,128)(2,1)S(1)}, u32[]{:S(2)}, u32[]{:S(2)}) %collective-permute-start.4) | collective-permute-done | bytes 589856 | tf_op jit(solution)/shard_map/ppermute | solution.py:873
  52.8 7.4 %shard_map.351 = (bf16[512,1152]{1,0:T(8,128)(2,1)S(1)}, bf16[512,1152]{1,0:T(8,128)(2,1)S(1)}, bf16[512,1152]{1,0:T(8,128)(2,1)S(1)}, bf16[256,1152]{1,0:T(8,12...) custom-call(s32[256,256]{1,0:T(8,128)S(1)} %copy-done.16, ...), custom_call_target="tpu_custom_call" | custom-call | flops 10350000128 | bytes 1000 | tf_op jit(solution)/shard_map/pallas_call | solution.py:812
  61.6 3.8 %shard_map.352 = (bf16[576,1152]{1,0:T(8,128)(2,1)S(1)}, bf16[576,1152]{1,0:T(8,128)(2,1)S(1)}) custom-call(s32[2]{0:T(128)S(1)} %copy-done.36, bf16[512,1152]{1,0:T(8,128)(2,1)S(1)} %get-tuple-element.82.refs_1_.refs_0_, bf16[512,1152]{1,0:T(8,128)(2,1)S(1)} %get-tuple-element.90.refs_2_.refs_4_, bf16[512,1152]{1,0:T(8,128)(2,1)S(1)} %get-tuple-element.86.refs_3_.refs_1_, ...), custom_call_target="tpu_custom_call" | custom-call | flops 230000000 | bytes 1000 | tf_op jit(solution)/shard_map/pallas_call | solution.py:812
  67.7 4.9 %shard_map.354 = (bf16[576,1152]{1,0:T(8,128)(2,1)S(1)}, bf16[576,1152]{1,0:T(8,128)(2,1)}) custom-call(s32[2]{0:T(128)S(1)} %copy-done.36, bf16[256,1152]{1,0:T(8,128)(2,1)S(1)} %copy-done.17, bf16[256,1152]{1,0:T(8,128)(2,1)S(1)} %collective-permute-done.refs_2_, bf16[256,1152]{1,0:T(8,128)(2,1)S(1)} %collective-permute-done.4.refs_1_.refs_3_, ...), custom_call_target="tpu_custom_call" | custom-call | flops 460000000 | bytes 1000 | tf_op jit(solution)/shard_map/pallas_call | solution.py:812
  74.3 5.0 %shard_map.355 = (bf16[2,256,1152]{2,1,0:T(8,128)(2,1)S(1)}, bf16[2,256,1152]{2,1,0:T(8,128)(2,1)}) custom-call(bf16[512,1152]{1,0:T(8,128)(2,1)S(1)} %get-tuple-element.82.refs_1_.refs_0_, bf16[512,1152]{1,0:T(8,128)(2,1)S(1)} %get-tuple-element.86.refs_3_.refs_1_, bf16[1152,1152]{1,0:T(8,128)(2,1)S(1)} %copy-done.14, ...), custom_call_target="tpu_custom_call" | custom-call | flops 460000000 | bytes 1000 | tf_op jit(solution)/shard_map/pallas_call | solution.py:812
  79.3 3.2 %collective-permute-done.13.refs_2_ = bf16[256,1152]{1,0:T(8,128)(2,1)S(1)} collective-permute-done((bf16[256,1152]{1,0:T(8,128)(2,1)S(1)}, bf16[256,1152]{1,0:T(8,128)(2,1)S(1)}, u32[]{:S(2)}, u32[]{:S(2)}) %collective-permute-start.13) | collective-permute-done | bytes 589856 | tf_op jit(solution)/shard_map/ppermute | solution.py:873
  83.8 13.0 %collective-permute-done.14.refs_2_ = bf16[576,1152]{1,0:T(8,128)(2,1)S(1)} collective-permute-done((bf16[576,1152]{1,0:T(8,128)(2,1)S(1)}, bf16[576,1152]{1,0:T(8,128)(2,1)S(1)}, u32[]{:S(2)}, u32[]{:S(2)}) %collective-permute-start.14) | collective-permute-done | bytes 1327136 | tf_op jit(solution)/shard_map/ppermute | solution.py:873
  100.8 9.1 %shard_map.359 = (bf16[288,896]{1,0:T(8,128)(2,1)}, bf16[288,896]{1,0:T(8,128)(2,1)S(1)}, bf16[3,2,256,384]{3,2,1,0:T(8,128)(2,1)S(1)}, bf16[4,256,384]{2,1,0:T(8,128)(2,1)S(1)}) custom-call(s32[2]{0:T(128)S(1)} %copy-done.36, bf16[256,1152]{1,0:T(8,128)(2,1)S(1)} %get-tuple-element.102.refs_1_.refs_6_, bf16[1152,1152]{1,0:T(8,128)(2,1)S(1)} %copy-done.15, ...), custom_call_target="tpu_custom_call" | custom-call | flops 920000000 | bytes 1000 | tf_op jit(solution)/shard_map/pallas_call | solution.py:812
  119.9 7.3 %shard_map.362 = (bf16[288,896]{1,0:T(8,128)(2,1)S(1)}, bf16[288,896]{1,0:T(8,128)(2,1)S(1)}, bf16[3,2,256,384]{3,2,1,0:T(8,128)(2,1)S(1)}) custom-call(s32[2]{0:T(128)S(1)} %copy-done.36, bf16[4,256,384]{2,1,0:T(8,128)(2,1)S(1)} %get-tuple-element.110.refs_3_.refs_1_, bf16[4,256,384]{2,1,0:T(8,128)(2,1)S(1)} %copy-done.4, ...), custom_call_target="tpu_custom_call" | custom-call | flops 920000000 | bytes 1000 | tf_op jit(solution)/shard_map/pallas_call | solution.py:812
  127.5 2.6 collective-permute-start.25
  130.3 4.7 %collective-permute-done.20.refs_5_ = bf16[288,896]{1,0:T(8,128)(2,1)S(1)} collective-permute-done((bf16[288,896]{1,0:T(8,128)(2,1)S(1)}, bf16[288,896]{1,0:T(8,128)(2,1)S(1)}, u32[]{:S(2)}, u32[]{:S(2)}) %collective-permute-start.20) | collective-permute-done | bytes 516128 | tf_op jit(solution)/shard_map/ppermute | solution.py:873
  138.8 5.1 %shard_map.364 = (bf16[288,1152]{1,0:T(8,128)(2,1)S(1)}, bf16[304,1152]{1,0:T(8,128)(2,1)S(1)}, bf16[288,1152]{1,0:T(8,128)(2,1)}, bf16[304,1152]{1,0:T(8,128)(2,1)}) custom-call(s32[2]{0:T(128)S(1)} %copy-done.36, bf16[1024,1152]{1,0:T(8,128)(2,1)S(1)} %shard_map.349.refs_8_.refs_1_, bf16[288,896]{1,0:T(8,128)(2,1)S(1)} %get-tuple-element.118.refs_2_, ...), custom_call_target="tpu_custom_call" | custom-call | flops 575000000 | bytes 1000 | tf_op jit(solution)/shard_map/pallas_call | solution.py:812
  149.5 9.3 %shard_map.365 = (bf16[16,1152]{1,0:T(8,128)(2,1)}, f32[256,1152]{1,0:T(8,128)}) custom-call(s32[2]{0:T(128)S(1)} %copy-done.36, s32[4]{0:T(128)S(1)} %copy-done.38, bf16[3,2,256,384]{3,2,1,0:T(8,128)(2,1)S(1)} %get-tuple-element.114.refs_2_, bf16[3,2,256,384]{3,2,1,0:T(8,128)(2,1)S(1)} %copy-done.23, bf16[1152,1152]{1,0:T(8,128)(2,1)S(1)} %copy-done.9, ...), custom_call_target="tpu_custom_call" | custom-call | flops 805000000 | bytes 1000 | tf_op jit(solution)/shard_map/pallas_call | solution.py:812
  162.6 3.4 %collective-permute-start.30 = (bf16[288,1152]{1,0:T(8,128)(2,1)S(1)}, bf16[288,1152]{1,0:T(8,128)(2,1)}, u32[]{:S(2)}, u32[]{:S(2)}) collective-permute-start(bf16[288,1152]{1,0:T(8,128)(2,1)S(1)} %shard_map.363.refs_14_.refs_0_), channel_id=1, source_target_pairs={{0,16},{4,20},{8,24},{12,28},{16,0},{20,4},{24,8},{28,12},{1,17},{... | collective-permute-start | bytes 1990664 | tf_op jit(solution)/shard_map/ppermute | solution.py:873
  166.0 10.4 %collective-permute-done.24.refs_2_ = bf16[288,1152]{1,0:T(8,128)(2,1)} collective-permute-done((bf16[288,1152]{1,0:T(8,128)(2,1)}, bf16[288,1152]{1,0:T(8,128)(2,1)}, u32[]{:S(2)}, u32[]{:S(2)}) %collective-permute-start.24) | collective-permute-done | bytes 663584 | tf_op jit(solution)/shard_map/ppermute | solution.py:873
  183.4 11.4 %collective-permute-done.27.refs_2_ = bf16[288,1152]{1,0:T(8,128)(2,1)} collective-permute-done((bf16[288,1152]{1,0:T(8,128)(2,1)S(1)}, bf16[288,1152]{1,0:T(8,128)(2,1)}, u32[]{:S(2)}, u32[]{:S(2)}) %collective-permute-start.27) | collective-permute-done | bytes 663584 | tf_op jit(solution)/shard_map/ppermute | solution.py:873
  196.7 13.1 %collective-permute-done.26.refs_1_ = bf16[144,1152]{1,0:T(8,128)(2,1)S(1)} collective-permute-done((bf16[144,1152]{1,0:T(8,128)(2,1)S(1)}, bf16[144,1152]{1,0:T(8,128)(2,1)S(1)}, u32[]{:S(2)}, u32[]{:S(2)}) %collective-permute-start.26) | collective-permute-done | bytes 331808 | tf_op jit(solution)/shard_map/ppermute | solution.py:873
  209.8 3.0 collective-permute-start.29
  217.6 25.4 %collective-permute-done.32.refs_2_ = bf16[288,1152]{1,0:T(8,128)(2,1)S(1)} collective-permute-done((bf16[288,1152]{1,0:T(8,128)(2,1)S(1)}, bf16[288,1152]{1,0:T(8,128)(2,1)S(1)}, u32[]{:S(2)}, u32[]{:S(2)}) %collective-permute-start.32) | collective-permute-done | bytes 663584 | tf_op jit(solution)/shard_map/ppermute | solution.py:873
  243.8 2.1 collective-permute-done.34.refs_1_
  248.1 2.7 shard_map.356
  250.8 13.4 %collective-permute-done.33.refs_2_ = bf16[144,1152]{1,0:T(8,128)(2,1)S(1)} collective-permute-done((bf16[144,1152]{1,0:T(8,128)(2,1)S(1)}, bf16[144,1152]{1,0:T(8,128)(2,1)S(1)}, u32[]{:S(2)}, u32[]{:S(2)}) %collective-permute-start.33) | collective-permute-done | bytes 331808 | tf_op jit(solution)/shard_map/ppermute | solution.py:873
  267.6 3.3 %shard_map.382 = f32[1152,1152]{1,0:T(8,128)} custom-call(s32[2]{0:T(128)S(1)} %copy-done.36, bf16[576,1152]{1,0:T(8,128)(2,1)S(1)} %shard_map.370.refs_2_.own, bf16[576,1152]{1,0:T(8,128)(2,1)S(1)} %collective-permute-done.39.other), custom_call_target="tpu_custom_call" | custom-call | flops 5750000128 | bytes 1000 | tf_op jit(solution)/shard_map/pallas_call | solution.py:854
  275.8 5.1 %shard_map.366 = (f32[288,1152]{1,0:T(8,128)}, f32[288,1152]{1,0:T(8,128)}, f32[288,1000]{1,0:T(8,128)}, f32[8,1152]{1,0:T(8,128)S(1)}) custom-call(s32[2]{0:T(128)S(1)} %copy-done.36, bf16[12,32,1152]{2,1,0:T(8,128)(2,1)S(1)} %bitcast.19, bf16[1152,1152]{1,0:T(8,128)(2,1)S(1)} %copy-done.12, bf16[1152,1152]{1,0:T(8,128)(2,1)S(1)} %copy-done.13), custom_call_target="tpu_custom_call" | custom-call | flops 230000000 | bytes 1000 | tf_op jit(solution)/shard_map/pallas_call | solution.py:812
  282.8 2.7 shard_map.378
  285.5 9.4 %collective-permute-done.37.refs_2_ = bf16[304,1152]{1,0:T(8,128)(2,1)} collective-permute-done((bf16[304,1152]{1,0:T(8,128)(2,1)S(1)}, bf16[304,1152]{1,0:T(8,128)(2,1)}, u32[]{:S(2)}, u32[]{:S(2)}) %collective-permute-start.37) | collective-permute-done | bytes 700448 | tf_op jit(solution)/shard_map/ppermute | solution.py:873
  295.0 2.7 shard_map.380
  298.3 5.3 %shard_map.381 = f32[1152,1152]{1,0:T(8,128)} custom-call(s32[2]{0:T(128)S(1)} %copy-done.36, bf16[576,1152]{1,0:T(8,128)(2,1)S(1)} %shard_map.374.refs_2_.own, bf16[576,1152]{1,0:T(8,128)(2,1)} %collective-permute-done.38.other), custom_call_target="tpu_custom_call" | custom-call | flops 5750000128 | bytes 1000 | tf_op jit(solution)/shard_map/pallas_call | solution.py:854
  (191 shorter events, 72.1 us)
Async XLA Ops:
  7.2 263.7 %all-gather.2.cloned.1.call-start = ((), (), s32[]{:S(2)}) async-start(), calls=%async_computation | async-start | bytes 1216512 | tf_op jit(solution)/shard_map/all_gather | solution.py:1227
  7.2 31.9 %collective-permute-start.1 = (bf16[256,1152]{1,0:T(8,128)(2,1)}, bf16[256,1152]{1,0:T(8,128)(2,1)S(1)}, u32[]{:S(2)}, u32[]{:S(2)}) collective-permute-start(bf16[256,1152]{1,0:T(8,128)(2,1)} %refs_3_.2), channel_id=1, source_target_pairs={{0,1},{1,0},{2,3},{3,2},{4,5},{5,4},{6,7},{7,6},{8,9},{9,8},{10,11... | collective-permute-start | bytes 1769480 | tf_op jit(solution)/shard_map/ppermute | solution.py:873
  7.8 26.3 %collective-permute-start.2 = (bf16[256,1152]{1,0:T(8,128)(2,1)}, bf16[256,1152]{1,0:T(8,128)(2,1)S(1)}, u32[]{:S(2)}, u32[]{:S(2)}) collective-permute-start(bf16[256,1152]{1,0:T(8,128)(2,1)} %refs_3_.2), channel_id=1, source_target_pairs={{0,2},{1,3},{2,0},{3,1},{4,6},{5,7},{6,4},{7,5},{8,10},{9,11},{10,... | collective-permute-start | bytes 1769480 | tf_op jit(solution)/shard_map/ppermute | solution.py:873
  34.4 15.5 %collective-permute-start.4 = (bf16[256,1152]{1,0:T(8,128)(2,1)}, bf16[256,1152]{1,0:T(8,128)(2,1)S(1)}, u32[]{:S(2)}, u32[]{:S(2)}) collective-permute-start(bf16[256,1152]{1,0:T(8,128)(2,1)} %get-tuple-element.81.dep.refs_1_), channel_id=1, source_target_pairs={{0,2},{1,3},{2,0},{3,1},{4,6},{5,7},{6,4},{7,5},{8,10},{9,11},{10,... | collective-permute-start | bytes 1769480 | tf_op jit(solution)/shard_map/ppermute | solution.py:873
  65.4 31.4 %collective-permute-start.14 = (bf16[576,1152]{1,0:T(8,128)(2,1)S(1)}, bf16[576,1152]{1,0:T(8,128)(2,1)S(1)}, u32[]{:S(2)}, u32[]{:S(2)}) collective-permute-start(bf16[576,1152]{1,0:T(8,128)(2,1)S(1)} %get-tuple-element.107), channel_id=1, source_target_pairs={{0,4},{4,0},{8,12},{12,8},{16,20},{20,16},{24,28},{28,24},{1,5},{5... | collective-permute-start | bytes 3981320 | tf_op jit(solution)/shard_map/ppermute | solution.py:873
  67.2 15.3 %collective-permute-start.13 = (bf16[256,1152]{1,0:T(8,128)(2,1)S(1)}, bf16[256,1152]{1,0:T(8,128)(2,1)S(1)}, u32[]{:S(2)}, u32[]{:S(2)}) collective-permute-start(bf16[256,1152]{1,0:T(8,128)(2,1)S(1)} %shard_map.353.refs_7_), channel_id=1, source_target_pairs={{0,2},{1,3},{2,0},{3,1},{4,6},{5,7},{6,4},{7,5},{8,10},{9,11},{10,... | collective-permute-start | bytes 1769480 | tf_op jit(solution)/shard_map/ppermute | solution.py:873
  72.7 38.8 %collective-permute-start.17 = (bf16[576,1152]{1,0:T(8,128)(2,1)}, bf16[576,1152]{1,0:T(8,128)(2,1)}, u32[]{:S(2)}, u32[]{:S(2)}) collective-permute-start(bf16[576,1152]{1,0:T(8,128)(2,1)} %get-tuple-element.112), channel_id=1, source_target_pairs={{0,8},{4,12},{8,0},{12,4},{16,24},{20,28},{24,16},{28,20},{1,9},{5... | collective-permute-start | bytes 3981320 | tf_op jit(solution)/shard_map/ppermute | solution.py:873
  83.7 17.1 %collective-permute-start.15 = (bf16[256,1152]{1,0:T(8,128)(2,1)S(1)}, bf16[256,1152]{1,0:T(8,128)(2,1)S(1)}, u32[]{:S(2)}, u32[]{:S(2)}) collective-permute-start(bf16[256,1152]{1,0:T(8,128)(2,1)S(1)} %get-tuple-element.102.refs_1_.refs_6_), channel_id=1, source_target_pairs={{0,1},{1,0},{2,3},{3,2},{4,5},{5,4},{6,7},{7,6},{8,9},{9,8},{10,11... | collective-permute-start | bytes 1769480 | tf_op jit(solution)/shard_map/ppermute | solution.py:873
  98.5 19.3 %collective-permute-start.16 = (bf16[288,1152]{1,0:T(8,128)(2,1)}, bf16[288,1152]{1,0:T(8,128)(2,1)S(1)}, u32[]{:S(2)}, u32[]{:S(2)}) collective-permute-start(bf16[288,1152]{1,0:T(8,128)(2,1)} %get-tuple-element.111), channel_id=1, source_target_pairs={{0,8},{4,12},{8,0},{12,4},{16,24},{20,28},{24,16},{28,20},{1,9},{5... | collective-permute-start | bytes 1990664 | tf_op jit(solution)/shard_map/ppermute | solution.py:873
  100.2 16.3 %collective-permute-start.21 = (bf16[256,1152]{1,0:T(8,128)(2,1)S(1)}, bf16[256,1152]{1,0:T(8,128)(2,1)S(1)}, u32[]{:S(2)}, u32[]{:S(2)}) collective-permute-start(bf16[256,1152]{1,0:T(8,128)(2,1)S(1)} %get-tuple-element.102.refs_1_.refs_6_), channel_id=1, source_target_pairs={{0,2},{1,3},{2,0},{3,1},{4,6},{5,7},{6,4},{7,5},{8,10},{9,11},{10,... | collective-permute-start | bytes 1769480 | tf_op jit(solution)/shard_map/ppermute | solution.py:873
  110.0 17.5 %collective-permute-start.19 = (bf16[288,896]{1,0:T(8,128)(2,1)}, bf16[288,896]{1,0:T(8,128)(2,1)S(1)}, u32[]{:S(2)}, u32[]{:S(2)}) collective-permute-start(bf16[288,896]{1,0:T(8,128)(2,1)} %get-tuple-element.120), channel_id=1, source_target_pairs={{0,2},{1,3},{2,0},{3,1},{4,6},{5,7},{6,4},{7,5},{8,10},{9,11},{10,... | collective-permute-start | bytes 1548296 | tf_op jit(solution)/shard_map/ppermute | solution.py:873
  113.2 16.9 %collective-permute-start.23 = (bf16[288,1152]{1,0:T(8,128)(2,1)S(1)}, bf16[288,1152]{1,0:T(8,128)(2,1)S(1)}, u32[]{:S(2)}, u32[]{:S(2)}) collective-permute-start(bf16[288,1152]{1,0:T(8,128)(2,1)S(1)} %get-tuple-element.123), channel_id=1, source_target_pairs={{0,4},{4,0},{8,12},{12,8},{16,20},{20,16},{24,28},{28,24},{1,5},{5... | collective-permute-start | bytes 1990664 | tf_op jit(solution)/shard_map/ppermute | solution.py:873
  114.9 20.2 %collective-permute-start.20 = (bf16[288,896]{1,0:T(8,128)(2,1)S(1)}, bf16[288,896]{1,0:T(8,128)(2,1)S(1)}, u32[]{:S(2)}, u32[]{:S(2)}) collective-permute-start(bf16[288,896]{1,0:T(8,128)(2,1)S(1)} %get-tuple-element.121), channel_id=1, source_target_pairs={{0,3},{1,2},{2,1},{3,0},{4,7},{5,6},{6,5},{7,4},{8,11},{9,10},{10,... | collective-permute-start | bytes 1548296 | tf_op jit(solution)/shard_map/ppermute | solution.py:873
  116.4 19.4 %collective-permute-start.22 = (bf16[256,1152]{1,0:T(8,128)(2,1)S(1)}, bf16[256,1152]{1,0:T(8,128)(2,1)S(1)}, u32[]{:S(2)}, u32[]{:S(2)}) collective-permute-start(bf16[256,1152]{1,0:T(8,128)(2,1)S(1)} %collective-permute-done.21.refs_3_.refs_8_), channel_id=1, source_target_pairs={{0,1},{1,0},{2,3},{3,2},{4,5},{5,4},{6,7},{7,6},{8,9},{9,8},{10,11... | collective-permute-start | bytes 1769480 | tf_op jit(solution)/shard_map/ppermute | solution.py:873
  127.5 32.3 %collective-permute-start.25 = (bf16[288,1152]{1,0:T(8,128)(2,1)S(1)}, bf16[288,1152]{1,0:T(8,128)(2,1)S(1)}, u32[]{:S(2)}, u32[]{:S(2)}) collective-permute-start(bf16[288,1152]{1,0:T(8,128)(2,1)S(1)} %shard_map.361.refs_6_.refs_0_), channel_id=1, source_target_pairs={{0,16},{4,20},{8,24},{12,28},{16,0},{20,4},{24,8},{28,12},{1,17},{... | collective-permute-start | bytes 1990664 | tf_op jit(solution)/shard_map/ppermute | solution.py:873
  130.1 85.5 %collective-permute-start.11 = (bf16[2,256,1152]{2,1,0:T(8,128)(2,1)}, bf16[2,256,1152]{2,1,0:T(8,128)(2,1)}, u32[]{:S(2)}, u32[]{:S(2)}) collective-permute-start(bf16[2,256,1152]{2,1,0:T(8,128)(2,1)} %get-tuple-element.99), channel_id=1, source_target_pairs={{0,1},{1,0},{2,3},{3,2},{4,5},{5,4},{6,7},{7,6},{8,9},{9,8},{10,11... | collective-permute-start | bytes 3538952 | tf_op jit(solution)/shard_map/ppermute | solution.py:873
  143.9 34.9 %collective-permute-start.28 = (bf16[304,1152]{1,0:T(8,128)(2,1)}, bf16[304,1152]{1,0:T(8,128)(2,1)}, u32[]{:S(2)}, u32[]{:S(2)}) collective-permute-start(bf16[304,1152]{1,0:T(8,128)(2,1)} %get-tuple-element.132), channel_id=1, source_target_pairs={{0,4},{4,0},{8,12},{12,8},{16,20},{20,16},{24,28},{28,24},{1,5},{5... | collective-permute-start | bytes 2101256 | tf_op jit(solution)/shard_map/ppermute | solution.py:873
  145.5 30.9 %collective-permute-start.24 = (bf16[288,1152]{1,0:T(8,128)(2,1)}, bf16[288,1152]{1,0:T(8,128)(2,1)}, u32[]{:S(2)}, u32[]{:S(2)}) collective-permute-start(bf16[288,1152]{1,0:T(8,128)(2,1)} %get-tuple-element.129), channel_id=1, source_target_pairs={{0,4},{4,0},{8,12},{12,8},{16,20},{20,16},{24,28},{28,24},{1,5},{5... | collective-permute-start | bytes 1990664 | tf_op jit(solution)/shard_map/ppermute | solution.py:873
  161.9 32.9 %collective-permute-start.27 = (bf16[288,1152]{1,0:T(8,128)(2,1)S(1)}, bf16[288,1152]{1,0:T(8,128)(2,1)}, u32[]{:S(2)}, u32[]{:S(2)}) collective-permute-start(bf16[288,1152]{1,0:T(8,128)(2,1)S(1)} %shard_map.367.refs_3_.refs_1_), channel_id=1, source_target_pairs={{0,8},{4,12},{8,0},{12,4},{16,24},{20,28},{24,16},{28,20},{1,9},{5... | collective-permute-start | bytes 1990664 | tf_op jit(solution)/shard_map/ppermute | solution.py:873
  162.6 50.4 %collective-permute-start.30 = (bf16[288,1152]{1,0:T(8,128)(2,1)S(1)}, bf16[288,1152]{1,0:T(8,128)(2,1)}, u32[]{:S(2)}, u32[]{:S(2)}) collective-permute-start(bf16[288,1152]{1,0:T(8,128)(2,1)S(1)} %shard_map.363.refs_14_.refs_0_), channel_id=1, source_target_pairs={{0,16},{4,20},{8,24},{12,28},{16,0},{20,4},{24,8},{28,12},{1,17},{... | collective-permute-start | bytes 1990664 | tf_op jit(solution)/shard_map/ppermute | solution.py:873
  181.3 31.6 %collective-permute-start.31 = (bf16[152,1152]{1,0:T(8,128)(2,1)S(1)}, bf16[152,1152]{1,0:T(8,128)(2,1)S(1)}, u32[]{:S(2)}, u32[]{:S(2)}) collective-permute-start(bf16[152,1152]{1,0:T(8,128)(2,1)S(1)} %get-tuple-element.134), channel_id=1, source_target_pairs={{0,8},{4,12},{8,0},{12,4},{16,24},{20,28},{24,16},{28,20},{1,9},{5... | collective-permute-start | bytes 1050632 | tf_op jit(solution)/shard_map/ppermute | solution.py:873
  181.5 28.3 %collective-permute-start.26 = (bf16[144,1152]{1,0:T(8,128)(2,1)S(1)}, bf16[144,1152]{1,0:T(8,128)(2,1)S(1)}, u32[]{:S(2)}, u32[]{:S(2)}) collective-permute-start(bf16[144,1152]{1,0:T(8,128)(2,1)S(1)} %get-tuple-element.131), channel_id=1, source_target_pairs={{0,8},{4,12},{8,0},{12,4},{16,24},{20,28},{24,16},{28,20},{1,9},{5... | collective-permute-start | bytes 995336 | tf_op jit(solution)/shard_map/ppermute | solution.py:873
  196.0 71.6 %collective-permute-start.39 = (bf16[576,1152]{1,0:T(8,128)(2,1)S(1)}, bf16[576,1152]{1,0:T(8,128)(2,1)S(1)}, u32[]{:S(2)}, u32[]{:S(2)}) collective-permute-start(bf16[576,1152]{1,0:T(8,128)(2,1)S(1)} %shard_map.370.refs_2_.own), channel_id=1, source_target_pairs={{0,4},{4,0},{8,12},{12,8},{16,20},{20,16},{24,28},{28,24},{1,5},{5... | collective-permute-start | bytes 3981320 | tf_op jit(solution)/shard_map/ppermute | solution.py:873
  209.8 33.8 %collective-permute-start.29 = (bf16[144,1152]{1,0:T(8,128)(2,1)S(1)}, bf16[144,1152]{1,0:T(8,128)(2,1)S(1)}, u32[]{:S(2)}, u32[]{:S(2)}) collective-permute-start(bf16[144,1152]{1,0:T(8,128)(2,1)S(1)} %shard_map.371.refs_2_.refs_0_), channel_id=1, source_target_pairs={{0,16},{4,20},{8,24},{12,28},{16,0},{20,4},{24,8},{28,12},{1,17},{... | collective-permute-start | bytes 995336 | tf_op jit(solution)/shard_map/ppermute | solution.py:873
  212.9 32.9 %collective-permute-start.34 = (bf16[152,1152]{1,0:T(8,128)(2,1)S(1)}, bf16[152,1152]{1,0:T(8,128)(2,1)S(1)}, u32[]{:S(2)}, u32[]{:S(2)}) collective-permute-start(bf16[152,1152]{1,0:T(8,128)(2,1)S(1)} %shard_map.372.refs_2_.refs_0_), channel_id=1, source_target_pairs={{0,16},{4,20},{8,24},{12,28},{16,0},{20,4},{24,8},{28,12},{1,17},{... | collective-permute-start | bytes 1050632 | tf_op jit(solution)/shard_map/ppermute | solution.py:873
  214.3 28.7 %collective-permute-start.32 = (bf16[288,1152]{1,0:T(8,128)(2,1)S(1)}, bf16[288,1152]{1,0:T(8,128)(2,1)S(1)}, u32[]{:S(2)}, u32[]{:S(2)}) collective-permute-start(bf16[288,1152]{1,0:T(8,128)(2,1)S(1)} %shard_map.373.refs_1_.refs_3_), channel_id=1, source_target_pairs={{0,4},{4,0},{8,12},{12,8},{16,20},{20,16},{24,28},{28,24},{1,5},{5... | collective-permute-start | bytes 1990664 | tf_op jit(solution)/shard_map/ppermute | solution.py:873
  216.8 31.3 %collective-permute-start.12 = (bf16[256,1152]{1,0:T(8,128)(2,1)S(1)}, bf16[256,1152]{1,0:T(8,128)(2,1)S(1)}, u32[]{:S(2)}, u32[]{:S(2)}) collective-permute-start(bf16[256,1152]{1,0:T(8,128)(2,1)S(1)} %fusion), channel_id=1, source_target_pairs={{0,2},{1,3},{2,0},{3,1},{4,6},{5,7},{6,4},{7,5},{8,10},{9,11},{10,... | collective-permute-start | bytes 1769480 | tf_op jit(solution)/shard_map/ppermute | solution.py:873
  246.0 20.5 %collective-permute-start.36 = (bf16[152,1152]{1,0:T(8,128)(2,1)S(1)}, bf16[152,1152]{1,0:T(8,128)(2,1)S(1)}, u32[]{:S(2)}, u32[]{:S(2)}) collective-permute-start(bf16[152,1152]{1,0:T(8,128)(2,1)S(1)} %shard_map.376.refs_3_.refs_1_), channel_id=1, source_target_pairs={{0,8},{4,12},{8,0},{12,4},{16,24},{20,28},{24,16},{28,20},{1,9},{5... | collective-permute-start | bytes 1050632 | tf_op jit(solution)/shard_map/ppermute | solution.py:873
  246.0 18.2 %collective-permute-start.33 = (bf16[144,1152]{1,0:T(8,128)(2,1)S(1)}, bf16[144,1152]{1,0:T(8,128)(2,1)S(1)}, u32[]{:S(2)}, u32[]{:S(2)}) collective-permute-start(bf16[144,1152]{1,0:T(8,128)(2,1)S(1)} %shard_map.375.refs_2_.refs_1_), channel_id=1, source_target_pairs={{0,8},{4,12},{8,0},{12,4},{16,24},{20,28},{24,16},{28,20},{1,9},{5... | collective-permute-start | bytes 995336 | tf_op jit(solution)/shard_map/ppermute | solution.py:873
  248.1 50.3 %collective-permute-start.38 = (bf16[576,1152]{1,0:T(8,128)(2,1)S(1)}, bf16[576,1152]{1,0:T(8,128)(2,1)}, u32[]{:S(2)}, u32[]{:S(2)}) collective-permute-start(bf16[576,1152]{1,0:T(8,128)(2,1)S(1)} %shard_map.374.refs_2_.own), channel_id=1, source_target_pairs={{0,8},{4,12},{8,0},{12,4},{16,24},{20,28},{24,16},{28,20},{1,9},{5... | collective-permute-start | bytes 3981320 | tf_op jit(solution)/shard_map/ppermute | solution.py:873
  264.8 18.0 %collective-permute-start.35 = (bf16[288,1152]{1,0:T(8,128)(2,1)S(1)}, bf16[288,1152]{1,0:T(8,128)(2,1)}, u32[]{:S(2)}, u32[]{:S(2)}) collective-permute-start(bf16[288,1152]{1,0:T(8,128)(2,1)S(1)} %shard_map.377.refs_1_.refs_3_), channel_id=1, source_target_pairs={{0,4},{4,0},{8,12},{12,8},{16,20},{20,16},{24,28},{28,24},{1,5},{5... | collective-permute-start | bytes 1990664 | tf_op jit(solution)/shard_map/ppermute | solution.py:873
  267.0 27.9 %collective-permute-start.37 = (bf16[304,1152]{1,0:T(8,128)(2,1)S(1)}, bf16[304,1152]{1,0:T(8,128)(2,1)}, u32[]{:S(2)}, u32[]{:S(2)}) collective-permute-start(bf16[304,1152]{1,0:T(8,128)(2,1)S(1)} %shard_map.379.refs_1_), channel_id=1, source_target_pairs={{0,4},{4,0},{8,12},{12,8},{16,20},{20,16},{24,28},{28,24},{1,5},{5... | collective-permute-start | bytes 2101256 | tf_op jit(solution)/shard_map/ppermute | solution.py:873
  (54 other events, 414.5 us)
Sparse Core Ops, SparseCore 0:
  166.2 81.5 all-gather.1
where the time goes:
time: 316 us; the launch traced here: 311 us
  waiting for transfers between devices  116 us (37%)
  Pallas kernels  115 us (36%)
  starting transfers between devices  36.8 us (12%)
  local copies, waits for them, and re-layouts  26.1 us (8%)
  between operations  14.8 us (5%)
    ppermute x40, waiting for transfers between devices, swap(): return lax.ppermute(array, axis, [(i, i ^ distance) for i in range(size)])  116 us
    pallas_call x16, Pallas kernels, run(): pl.pallas_call(body, out_shape=outs, in_specs=[space[kind] for kind in ki...  91.6 us
    ppermute x40, starting transfers between devices, swap(): return lax.ppermute(array, axis, [(i, i ^ distance) for i in range(size)])  36.8 us
    unnamed x91, local copies, waits for them, and re-layouts  19.4 us
    pallas_call x16, Pallas kernels, quick(): pl.pallas_call(body, out_shape=outs, in_specs=specs + [HBM] * len(deps),...  11.2 us
    pallas_call x2, Pallas kernels, widen(): pl.pallas_call(partial(widen_kernel, level), out_shape=shape_of(2 * half,...  8.58 us
  transfers between devices with their start and end apart: 41, of which 18 were waited for; matrix products, arithmetic and copies ran while one was open for 3% of the time, Pallas kernels for 35%

commit v1 on v0

--- a/solution.py
+++ b/solution.py
@@ -13,6 +13,7 @@
 F32 = jnp.float32
 BF16 = jnp.bfloat16
 LANES = 128
+PACE = 0.3
 
 
 def mm(left, right):
@@ -40,6 +41,10 @@
 def head_mask(lanes, offset, head_width):
     lane = lax.broadcasted_iota(jnp.int32, (1, lanes), 1)
     return jnp.where((lane >= offset) & (lane < offset + head_width), 1.0, 0.0).astype(BF16)
+
+
+def row_of(ref):
+    return ref[...].reshape(1, ref.shape[0])
 
 
 def unit_rows(values):
@@ -96,7 +101,11 @@
     steps_ref,
     relative_ref,
     table_ref,
-    params,
+    first_gain,
+    first_shift,
+    second_gain,
+    second_shift,
+    out_bias,
     tokens_hbm,
     times_hbm,
     query_hbm,
@@ -111,8 +120,7 @@
     probs_ref,
     mixed_0,
     mixed_1,
-    mixed_2,
-    mixed_3,
+    mixed_far,
     middle_ref,
     normed_ref,
     embed_ref,
@@ -164,7 +172,7 @@
     own_copy.wait()
     own = mm(place, own_tokens[...])
     unit, _ = unit_rows(own)
-    normed = (unit * params[0:1, :] + params[1:2, :]).astype(BF16)
+    normed = (unit * row_of(first_gain) + row_of(first_shift)).astype(BF16)
 
     def into_groups(rows, target):
         fill = jnp.zeros((rows.shape[0], target.shape[2] - group_width), rows.dtype)
@@ -220,26 +228,30 @@
             values = value_ref[group, :, first : first + lanes] * mask
             add_tiles(tiles, mm_tn(probs, values), first)
         mixed_ref[group] = jnp.concatenate(tiles, axis=1).astype(BF16)
+        probs_ref.send_rows(group * slots, slots)
         return carry
 
     lax.fori_loop(0, groups, one_group, 0)
-    probs_ref.send()
     for group in range(groups):
         flat[:, group * group_width : (group + 1) * group_width] = mixed_ref[group][:, :group_width]
-    for away, target in enumerate((mixed_0, mixed_1, mixed_2, mixed_3)):
-        target[...] = mixed_ref[rank ^ away]
-        target.send()
+    for away in (2, 3):
+        mixed_far[away - 2] = mixed_ref[rank ^ away]
+    mixed_far.send()
+    mixed_1[...] = mixed_ref[rank ^ 1]
+    mixed_1.send()
+    mixed_0[...] = mixed_ref[rank]
+    mixed_0.send()
     copies[5].wait()
-    middle = own + mm(flat[...], weights[5]) + params[4:5, :]
+    middle = own + mm(flat[...], weights[5]) + row_of(out_bias)
     middle_ref[...] = middle
     middle_ref.send()
     unit, _ = unit_rows(middle)
-    normed_ref[...] = (unit * params[2:3, :] + params[3:4, :]).astype(BF16)
-
-
-def normed_kernel(side, ranks, relative_ref, tokens_ref, params, dep, other, normed_ref):
+    normed_ref[...] = (unit * row_of(second_gain) + row_of(second_shift)).astype(BF16)
+
+
+def normed_kernel(side, ranks, relative_ref, tokens_ref, gain, shift, normed_ref):
     unit, _ = unit_rows(mm(place_matrix(relative_ref[0:1, :], side), tokens_ref[...]))
-    normed_ref[...] = (unit * params[0:1, :] + params[1:2, :]).astype(BF16)
+    normed_ref[...] = (unit * row_of(gain) + row_of(shift)).astype(BF16)
 
 
 def gelu_pair(hidden):
@@ -258,7 +270,7 @@
         span = slice(chunk * rows, (chunk + 1) * rows)
         turned = mm(place, cotangent[chunk][...]).astype(BF16)
         moved[span, :] = turned
-        gelu_out, slope = gelu_pair(mm(normed[chunk][...], up_ref[...]) + up_bias[...])
+        gelu_out, slope = gelu_pair(mm(normed[chunk][...], up_ref[...]) + row_of(up_bias))
         active[span, :] = gelu_out.astype(BF16)
         hidden[span, :] = (mm_nt(turned, down_ref[...]) * slope).astype(BF16)
 
@@ -382,7 +394,7 @@
     far_ref,
     middle_ref,
     moved_ref,
-    params,
+    gain,
     branch_ref,
     grad_ref,
     sums_ref,
@@ -391,7 +403,7 @@
     grad_normed = own_ref[...].astype(F32) + near_ref[...].astype(F32) + far_ref[...].astype(F32)
     unit, inverse = unit_rows(middle_ref[...])
     cotangent = moved_ref[:rows, :].astype(F32)
-    grad_middle = cotangent + norm_back(grad_normed, unit, inverse, params[2:3, :])
+    grad_middle = cotangent + norm_back(grad_normed, unit, inverse, row_of(gain))
     branch_ref[...] = grad_middle.astype(BF16)
     branch_ref.send()
     grad_ref[...] = grad_middle
@@ -413,9 +425,21 @@
     group_width = slots * head_width
     rank = ranks[0]
     length = side * side
-    if len(refs) == 11:
-        branch_ref, out_ref, query_ref, key_ref, value_ref, probs_ref = refs[:6]
-        packed_a, packed_b, grads, grad_mixed, sheared = refs[6:]
+    hbm = refs[1:5] if len(refs) == 14 else refs[2:6]
+    nows = refs[-5:-1]
+
+    def fetch(pick, item):
+        group = (picks[0] + pick) ^ rank
+        source = hbm[item].at[pl.ds(group * slots, slots)] if item == 3 else hbm[item].at[group]
+        return pltpu.make_async_copy(source, nows[item].at[pick], refs[-1].at[pick, item])
+
+    for pick in range(2):
+        for item in (3, 2, 0, 1):
+            fetch(pick, item).start()
+    if len(refs) == 15:
+        branch_ref, out_ref = refs[:2]
+        packed_far, grads, grad_mixed, sheared, query_now, key_now, value_now, probs_now, _ = refs[6:]
+        packed_all = [packed_far.ref.at[0], packed_far.ref.at[1]]
         fill = jnp.zeros((length, grad_mixed.shape[2] - group_width), BF16)
         product = mm_nt(branch_ref[...], out_ref[...]).astype(BF16)
         for group in range(groups):
@@ -423,35 +447,35 @@
             grad_mixed[group] = jnp.concatenate([piece, fill], axis=1)
         grad_mixed.send()
     else:
-        grad_mixed, query_ref, key_ref, value_ref, probs_ref = refs[:5]
-        packed_a, packed_b, grads, sheared = refs[5:]
+        grad_mixed = refs[0]
+        packed_a, packed_b, grads, sheared, query_now, key_now, value_now, probs_now, _ = refs[5:]
+        packed_all = [packed_a.ref, packed_b.ref]
         grad_mixed.ready()
-    for ref in (query_ref, key_ref, value_ref, probs_ref):
-        ref.ready()
     stride = 2 * side - 1
     span_lanes = sheared.shape[2]
-    packed_lanes = packed_a.shape[1]
+    packed_lanes = packed_all[0].shape[1]
     table_lanes = round_up(stride * stride, LANES)
 
     def one_group(pick, carry):
         group = (picks[0] + pick) ^ rank
+        for item in range(4):
+            fetch(pick, item).wait()
         wide = grad_mixed.shape[2] // LANES
         query_tiles, key_tiles, value_tiles = [None] * wide, [None] * wide, [None] * wide
         for slot in range(slots):
-            head = group * slots + slot
             first, lanes, offset = head_window(slot, head_width)
             mask = head_mask(lanes, offset, head_width)
             span = slice(first, first + lanes)
             mixed_now = grad_mixed[group, :, span] * mask
-            probs = probs_ref[head]
-            grad_probs = mm_nt(value_ref[group, :, span], mixed_now)
+            probs = probs_now[pick, slot]
+            grad_probs = mm_nt(value_now[pick, :, span], mixed_now)
             probs_wide = probs.astype(F32)
             weighted = probs_wide * grad_probs
             grad_scores = weighted - probs_wide * jnp.sum(weighted, axis=0, keepdims=True)
             rounded = grad_scores.astype(BF16)
             add_tiles(value_tiles, mm(probs, mixed_now), first)
-            add_tiles(key_tiles, mm(rounded, query_ref[group, :, span] * mask), first)
-            add_tiles(query_tiles, mm_tn(rounded, key_ref[group, :, span] * mask), first)
+            add_tiles(key_tiles, mm(rounded, query_now[pick, :, span] * mask), first)
+            add_tiles(query_tiles, mm_tn(rounded, key_now[pick, :, span] * mask), first)
             steps = LANES // side
             shear = jnp.zeros((side, span_lanes), F32)
             for turn in range(steps):
@@ -498,7 +522,7 @@
         total = [
             old + turned[:, place * LANES : (place + 1) * LANES] for place, old in enumerate(total)
         ]
-    for pick, packed_ref in enumerate((packed_a, packed_b)):
+    for pick, packed_ref in enumerate(packed_all):
         for place in range(tall):
             packed_ref[length + place * slots : length + (place + 1) * slots, :LANES] = total[place][
                 pick * slots : (pick + 1) * slots
@@ -512,18 +536,15 @@
 def tokens_kernel(
     dims,
     ranks,
-    steps_ref,
     near_grads,
     far_grads,
     query_ref,
     key_ref,
     value_ref,
     relative_ref,
-    params,
+    gain,
     middle_ref,
     middle_sums,
-    embed_ref,
-    up_bias_ref,
     tokens_hbm,
     image_ref,
     grad_ref,
@@ -552,52 +573,110 @@
     place = place_matrix(relative_ref[0:1, :], side)
     own_copy.wait()
     unit, inverse = unit_rows(mm(place, own_tokens[...]))
-    total = middle_ref[...] + norm_back(grad_normed, unit, inverse, params[0:1, :])
+    total = middle_ref[...] + norm_back(grad_normed, unit, inverse, row_of(gain))
     high, low = split_two(total)
     grad_ref[...] = mm_tn(place, high) + mm_tn(place, low)
     grad_ref.send()
-    step = steps_ref[rank]
     sums = [
         jnp.sum(flat[0].astype(F32), axis=0, keepdims=True),
         jnp.sum(flat[2].astype(F32), axis=0, keepdims=True),
-        embed_ref[0:1, :],
-        jnp.full((1, embed_ref.shape[1]), (step // 8).astype(F32)),
-        jnp.full((1, embed_ref.shape[1]), (step % 8).astype(F32)),
-        middle_sums[0:4, :],
         jnp.sum(grad_normed * unit, axis=0, keepdims=True),
         jnp.sum(grad_normed, axis=0, keepdims=True),
-        up_bias_ref[0:1, :],
-        jnp.zeros((4, embed_ref.shape[1]), F32),
+        middle_sums[0:4, :],
     ]
-    image_ref[...] = jnp.concatenate(sums, axis=0).astype(BF16)
+    image_ref[...] = jnp.concatenate(sums, axis=0)
     image_ref.send()
 
 
-def weights_kernel(dims, level, ranks, normed, *refs):
+def own_columns(rows, rank, groups):
+    columns = rows.shape[1] // groups
+    chosen = rows[:, :columns]
+    for group in range(1, groups):
+        chosen = jnp.where(rank == group, rows[:, group * columns : (group + 1) * columns], chosen)
+    return chosen
+
+
+def weights_kernel(dims, level, ranks, steps_ref, normed, *refs):
     groups, slots, head_width, side, scale = dims
     group_width = slots * head_width
     rows = side * side
-    keep_first, keep_second, send_first, send_second, packed, branch, mixed = refs[3 * groups :]
+    rank = ranks[0]
+    lines_own, lines_far, lines_near, up_bias_ref, query_hbm, value_hbm = refs[
+        3 * groups : 3 * groups + 6
+    ]
+    keep_first, keep_second, send_first, send_second = refs[3 * groups + 6 : 3 * groups + 10]
+    packed, branch, mixed, tail, times, sems = refs[3 * groups + 10 :]
+    start = pl.multiple_of(rank * group_width, 16)
+    copies = []
+    for item, source in enumerate((query_hbm, value_hbm)):
+        copies.append(
+            pltpu.make_async_copy(
+                source.at[pl.ds(start, group_width)], times.at[item], sems.at[item]
+            )
+        )
+        copies[item].start()
     table = None
     for chunk in range(groups):
         span = slice(chunk * rows, (chunk + 1) * rows)
-        source = refs[chunk]
+        source, other = refs[chunk].ref, refs[2 * groups + chunk].ref
+        if chunk >= 2:
+            source, other = source.at[chunk - 2], other.at[chunk - 2]
         packed[span, :] = source[:rows, :]
         branch[span, :] = refs[groups + chunk][...]
-        mixed[span, :] = refs[2 * groups + chunk][...]
+        mixed[span, :] = other[...]
         part = source[rows:, :LANES].astype(F32)
         table = part if table is None else table + part
     bit = (ranks[1] >> level) & 1
     left = mm_tn(packed[...], normed[...]).astype(BF16)
     right = mm_tn(mixed[...], branch[...]).astype(BF16)
-    keep_first[...], send_first[...] = halves(left[: 2 * group_width], bit)
     value, out = left[2 * group_width : 3 * group_width], right[:group_width]
-    low, high = halves(table.astype(BF16), bit)
-    fill = jnp.zeros((low.shape[0], value.shape[1] - LANES), BF16)
-    keep_second[:group_width, :] = jnp.where(bit == 0, value, out)
-    keep_second[group_width:, :] = jnp.concatenate([low, fill], axis=1)
-    send_second[:group_width, :] = jnp.where(bit == 0, out, value)
-    send_second[group_width:, :] = jnp.concatenate([high, fill], axis=1)
+    keep_second[...] = jnp.where(bit == 0, value, out)
+    send_second[...] = jnp.where(bit == 0, out, value)
+
+    lines = [lines_own[...], lines_near[:8, :], lines_far[...], lines_near[8:, :]]
+    embed = None
+    for item in range(2):
+        both = jnp.concatenate([line[item : item + 1, :] for line in lines] * 2, axis=0)
+        high = both.astype(BF16).astype(F32)
+        place = lax.broadcasted_iota(jnp.int32, both.shape, 0)
+        both = jnp.where(place < groups, high, both - high).astype(BF16)
+        copies[item].wait()
+        product = mm_nt(both, times[item])
+        product = product[:groups] + product[groups:]
+        embed = product if embed is None else embed + product
+    tail[...] = jnp.zeros_like(tail)
+    tail[: table.shape[0], :LANES] = table
+    each = group_width // 2
+    for chunk in range(groups):
+        total = jnp.sum(packed[chunk * rows : (chunk + 1) * rows, :].astype(F32), axis=0, keepdims=True)
+        step = steps_ref[rank ^ chunk]
+        fill = tail.shape[1] - LANES - 3 * group_width - 16
+        line = [
+            total[:, :group_width],
+            total[:, 2 * group_width : 3 * group_width],
+            embed[chunk : chunk + 1, :],
+            jnp.zeros((1, fill), F32),
+            jnp.full((1, 8), (step // 8).astype(F32)),
+            jnp.full((1, 8), (step % 8).astype(F32)),
+        ]
+        image = ranks[1] * groups + (rank ^ chunk)
+        tail[pl.ds(image, 1), LANES:] = jnp.concatenate(line, axis=1)
+    vectors = lines[0] + lines[1] + lines[2] + lines[3]
+    vectors = [own_columns(vectors[item : item + 1, :], rank, groups) for item in range(2, 8)]
+    vectors += [
+        up_bias_ref[0:1, part * group_width : (part + 1) * group_width]
+        for part in range(up_bias_ref.shape[1] // group_width)
+    ]
+    first = LANES + 3 * group_width
+    for item, vector in enumerate(vectors):
+        tail[2 * item : 2 * item + 1, first : first + each] = vector[:, :each]
+        tail[2 * item + 1 : 2 * item + 2, first : first + each] = vector[:, each:]
+    keep, send = halves(left[: 2 * group_width], bit)
+    keep_first[:group_width, :] = keep
+    send_first[:group_width, :] = send
+    keep, send = halves(tail[...].astype(BF16), bit)
+    keep_first[group_width:, :] = keep
+    send_first[group_width:, :] = send
 
 
 def split_kernel(level, tail, ranks, kept, got, keep_ref, send_ref):
@@ -625,9 +704,10 @@
         out_ref[2 * body + tail :, :] = high[body:]
 
 
-def widen_kernel(level, ranks, own, other, out_ref):
+def widen_kernel(level, cross, each, ranks, own, other, out_ref):
     bit = (ranks[1] >> level) & 1
-    first = (pl.program_id(0) < pl.num_programs(0) // 2) == (bit == 0)
+    block = pl.program_id(0) // each
+    first = (block % 2 if cross else block // 2) == bit
 
     @pl.when(first)
     def _():
@@ -638,73 +718,65 @@
         out_ref[...] = other[...].astype(F32)
 
 
-def widen_pair_kernel(level, tail, ranks, own, other, low_ref, high_ref, *refs):
+def widen_pair_kernel(level, ranks, own, other, low_ref, high_ref, tail_ref):
     bit = (ranks[1] >> level) & 1
-    body = own.shape[0] - tail
-    low_ref[...] = jnp.where(bit == 0, own[:body, :], other[:body, :]).astype(F32)
+    low = jnp.where(bit == 0, own[...], other[...]).astype(F32)
+    high = jnp.where(bit == 0, other[...], own[...]).astype(F32)
+    body, half = low_ref.shape[0], tail_ref.shape[0] // 2
+    tail_ref[:half, :] = low[body:]
+    tail_ref[half:, :] = high[body:]
+    low_ref[...] = low[:body]
     low_ref.send()
-    high_ref[...] = jnp.where(bit == 0, other[:body, :], own[:body, :]).astype(F32)
-    high_ref.send()
-    if tail:
-        table = refs[0]
-        slots = table.shape[0]
-        low = jnp.where(bit == 0, own[body:, :LANES], other[body:, :LANES]).astype(F32)
-        high = jnp.where(bit == 0, other[body:, :LANES], own[body:, :LANES]).astype(F32)
-        for part in range(table.shape[1] // LANES):
-            source, row = (low, part * slots) if part * slots < tail else (high, part * slots - tail)
-            table[:, part * LANES : (part + 1) * LANES] = source[row : row + slots]
+    high_ref[...] = high[:body]
+
+
+def widen_cross_kernel(level, ranks, own, other, low_ref, high_ref):
+    bit = (ranks[1] >> level) & 1
+    body = own.shape[0] // 2
+    even = jnp.where(bit == 0, own[...], other[...]).astype(F32)
+    odd = jnp.where(bit == 0, other[...], own[...]).astype(F32)
+    low_ref[:body, :] = even[:body]
+    low_ref[body:, :] = odd[:body]
+    low_ref.send()
+    high_ref[:body, :] = even[body:]
+    high_ref[body:, :] = odd[body:]
 
 
 def finish_kernel(
-    dims, images, ranks, all_ref, query_hbm, value_hbm, query_ref, value_ref, table_ref, sums_ref,
-    weights, sems,
+    dims, images, tail, times, query_ref, value_ref, table_ref, bias_ref, sums_ref
 ):
     groups, slots, head_width, side, scale = dims
     group_width = slots * head_width
-    rank = ranks[0]
-    start = pl.multiple_of(rank * group_width, 16)
-    copies = []
-    for item, source in enumerate((query_hbm, value_hbm)):
-        copy = pltpu.make_async_copy(
-            source.at[pl.ds(start, group_width)], weights.at[item], sems.at[item]
-        )
-        copy.start()
-        copies.append(copy)
-
-    def own_columns(rows):
-        chosen = rows[:, :group_width]
-        for group in range(1, groups):
-            piece = rows[:, group * group_width : (group + 1) * group_width]
-            chosen = jnp.where(rank == group, piece, chosen)
-        return chosen
-
+    for part in range(bias_ref.shape[1] // LANES):
+        bias_ref[:, part * LANES : (part + 1) * LANES] = tail[
+            part * slots : (part + 1) * slots, :LANES
+        ]
+    each = group_width // 2
+    first = LANES + 3 * group_width
     sums_ref[...] = jnp.zeros(sums_ref.shape, F32)
-    embed = all_ref[2]
-    totals = None
-    for item, target in enumerate((query_ref, value_ref)):
-        rows = all_ref[item]
-        target[...] = mm_tn(own_columns(rows), embed)
-        target.send()
-        copies[item].wait()
-        part = mm_nt(rows, weights[item])
-        totals = part if totals is None else totals + part
-    steps = all_ref[3][:, 0:1].astype(F32) * 8.0 + all_ref[4][:, 0:1].astype(F32)
+    for item in range(10):
+        for part in range(2):
+            row = 2 * item + part
+            sums_ref[item : item + 1, part * each : (part + 1) * each] = tail[
+                row : row + 1, first : first + each
+            ]
+    last = tail.shape[1]
+    steps = tail[:images, last - 16 : last - 15] * 8.0 + tail[:images, last - 8 : last - 7]
     step = lax.broadcasted_iota(jnp.int32, (images, table_ref.shape[1]), 1)
     chosen = jnp.where(step == steps.astype(jnp.int32), 1.0, 0.0).astype(BF16)
-    high, low = split_two(totals)
-    table_ref[...] = mm_tn(high, chosen) + mm_tn(low, chosen)
+    total = tail[:images, LANES + 2 * group_width : LANES + 3 * group_width].astype(BF16)
+    table_ref[...] = mm_tn(total, chosen)
     table_ref.send()
-    for item in range(6):
-        total = jnp.sum(all_ref[5 + item].astype(F32), axis=0, keepdims=True)
-        sums_ref[item : item + 1, :group_width] = own_columns(total)
-    image = lax.broadcasted_iota(jnp.int32, (images, 1), 0)
-    mine = jnp.where(image % groups == rank, all_ref[11].astype(F32), 0.0)
-    sums_ref[6:7, :] = jnp.sum(mine, axis=0, keepdims=True)
-
-
-def block_kernel(side, relative_ref, own, near, far, middle_ref, params, out_ref):
+    embed = mm(chosen, times[...]).astype(BF16)
+    for item, target in enumerate((query_ref, value_ref)):
+        rows = tail[:images, LANES + item * group_width : LANES + (item + 1) * group_width]
+        target[...] = mm_tn(rows.astype(BF16), embed)
+        target.send()
+
+
+def block_kernel(side, relative_ref, own, near, far, middle_ref, bias, out_ref):
     total = own[0].astype(F32) + near[0].astype(F32) + far[...].astype(F32)
-    total = (middle_ref[...] + total + params[5:6, :]).astype(BF16)
+    total = (middle_ref[...] + total + row_of(bias)).astype(BF16)
     place = place_matrix(relative_ref[0:1, :], side)
     out_ref[...] = mm_tn(place, total).astype(BF16)
 
@@ -717,11 +789,11 @@
 HBM = pl.BlockSpec(memory_space=pl.ANY)
 SMEM = pl.BlockSpec(memory_space=pltpu.SMEM)
 MIB = 1024 * 1024
-FEED = 20
+FEED = 16
 
 
 def cost(us):
-    return pl.CostEstimate(flops=int(us * 1.15e9), bytes_accessed=1000, transcendentals=0)
+    return pl.CostEstimate(flops=int(us * PACE * 1.15e9), bytes_accessed=1000, transcendentals=0)
 
 
 class Staged:
@@ -746,6 +818,12 @@
         self.ref, self.sent = ref, target is None
         self.copy = None if self.sent else pltpu.make_async_copy(ref, target, sem)
         self.shape, self.dtype = ref.shape, ref.dtype
+        self.target, self.sem = target, sem
+
+    def send_rows(self, start, count):
+        self.sent = True
+        rows = pl.ds(start, count)
+        pltpu.make_async_copy(self.ref.at[rows], self.target.at[rows], self.sem).start()
 
     def __getitem__(self, place):
         return self.ref[place]
@@ -770,13 +848,15 @@
         return self.ref[place]
 
 
-def run(kernel, outs, inputs, kinds=None, scratch=(), deps=(), us=0.2, away=(), vmem=40):
+def run(kernel, outs, inputs, kinds=None, scratch=(), deps=(), us=2.5, away=(), vmem=16):
     kinds = "v" * len(inputs) if kinds is None else kinds
     assert len(kinds) == len(inputs)
     single = not isinstance(outs, (list, tuple))
     outs = [outs] if single else list(outs)
     staged = [place for place, kind in enumerate(kinds) if kind == "w"]
-    count, extra, results = len(inputs), len(deps), len(outs)
+    count, results = len(inputs), len(outs)
+    if deps:
+        inputs = [after(inputs[0], *deps), *inputs[1:]]
     buffers = [pltpu.VMEM(inputs[place].shape, inputs[place].dtype) for place in staged]
     buffers += [pltpu.VMEM(outs[place].shape, outs[place].dtype) for place in away]
     if buffers:
@@ -784,8 +864,8 @@
 
     def body(*refs):
         given = list(refs[:count])
-        targets = refs[count + extra : count + extra + results]
-        rest = refs[count + extra + results :]
+        targets = refs[count : count + results]
+        rest = refs[count + results :]
         for place, kind in enumerate(kinds):
             if kind == "v":
                 given[place] = Held(given[place])
@@ -812,51 +892,52 @@
     found = pl.pallas_call(
         body,
         out_shape=outs,
-        in_specs=[space[kind] for kind in kinds] + [HBM] * extra,
+        in_specs=[space[kind] for kind in kinds],
         out_specs=[HBM if place in away else VMEM for place in range(results)],
         scratch_shapes=buffers + list(scratch),
         compiler_params=pltpu.CompilerParams(vmem_limit_bytes=vmem * MIB),
         cost_estimate=cost(us),
-    )(*inputs, *deps)
+    )(*inputs)
     return found[0] if single else found
 
 
 def quick(kernel, outs, inputs, deps=()):
-    count = len(inputs)
-
-    def body(*refs):
-        kernel(*refs[:count], *refs[count + len(deps) :])
-
-    specs = [SMEM if given.shape == (2,) else VMEM for given in inputs]
+    if deps:
+        inputs = [after(inputs[0], *deps), *inputs[1:]]
     return pl.pallas_call(
-        body,
+        kernel,
         out_shape=outs,
-        in_specs=specs + [HBM] * len(deps),
+        in_specs=[SMEM if given.shape == (2,) else VMEM for given in inputs],
         out_specs=jax.tree.map(lambda _: VMEM, outs),
         compiler_params=pltpu.CompilerParams(vmem_limit_bytes=4 * MIB),
-        cost_estimate=cost(0.1),
-    )(*inputs, *deps)
-
-
-def widen(ranks, level, own, other):
+        cost_estimate=cost(1.2),
+    )(*inputs)
+
+
+def widen(ranks, level, own, other, last, cross=False):
     half, columns = own.shape
-    parts = 2
-    block = half // parts
+    each = 2
+    block = half // (2 * each)
+    parts = 4 * each
+
+    def place_of(i, bit):
+        quarter, inner = i // each, i % each
+        if cross:
+            return ((quarter // 2) * each + inner, 0)
+        return (jnp.clip(i - 2 * each * bit, 0, 2 * each - 1), 0)
 
     def own_map(i, me):
-        bit = (me[1] >> level) & 1
-        return (jnp.clip(i - parts * bit, 0, parts - 1), 0)
+        return place_of(i, (me[1] >> level) & 1)
 
     def other_map(i, me):
-        bit = (me[1] >> level) & 1
-        return (jnp.clip(i - parts * (1 - bit), 0, parts - 1), 0)
+        return place_of(i, 1 - ((me[1] >> level) & 1))
 
     return pl.pallas_call(
-        partial(widen_kernel, level),
+        partial(widen_kernel, level, cross, each),
         out_shape=shape_of(2 * half, columns, dtype=F32),
         grid_spec=pltpu.PrefetchScalarGridSpec(
             num_scalar_prefetch=1,
-            grid=(2 * parts,),
+            grid=(parts,),
             in_specs=[
                 pl.BlockSpec((block, columns), own_map),
                 pl.BlockSpec((block, columns), other_map),
@@ -864,8 +945,8 @@
             out_specs=pl.BlockSpec((block, columns), lambda i, me: (i, 0)),
         ),
         compiler_params=pltpu.CompilerParams(vmem_limit_bytes=16 * MIB),
-        cost_estimate=cost(5.0),
-    )(ranks, own, other)
+        cost_estimate=cost(3.5),
+    )(after(ranks, last), own, other)
 
 
 def swap(array, axis, distance):
@@ -878,8 +959,9 @@
 
 
 class Total:
-    def __init__(self, ranks, order, keep, send, tail=0):
+    def __init__(self, ranks, order, keep, send, tail=0, cross=False):
         self.ranks, self.order, self.tail = ranks, order, tail
+        self.back = (0, 1) if cross else (1, 0)
         self.keep = keep
         self.got = self.swap(0, send)
 
@@ -906,23 +988,21 @@
     def join(self, deps=()):
         half, columns = self.keep.shape
         self.keep = quick(
-            partial(join_kernel, self.order[1], self.tail // 2),
+            partial(join_kernel, self.order[self.back[0]], self.tail // 2),
             shape_of(2 * half, columns),
             [self.ranks, self.keep, self.got],
             deps,
         )
-        self.got = self.swap(0, self.keep)
+        self.got = self.swap(self.back[1], self.keep)
         return self.keep
 
-    def advance(self, stage, deps=()):
-        levels = len(self.order)
-        if stage == 0:
-            return self.split(deps)
-        if stage < levels - 1:
-            return self.add(stage + 1, deps)
-        if stage == levels - 1:
-            return self.add(1, deps)
-        return self.join(deps)
+    def exchange(self, deps=()):
+        for place in range(2, len(self.order)):
+            self.add(place, deps)
+        return self.keep
+
+    def finish(self, deps=()):
+        return self.add(self.back[0], deps)
 
 
 def add_low(left, right):
@@ -971,11 +1051,6 @@
     hidden_width = up_weight.shape[1]
     rows = groups * length
     dims = (groups, slots, head_width, side, head_width ** (-0.5))
-    line = lambda vector: vector.reshape(1, -1)
-    params = jnp.stack(
-        [first_gain, first_shift, second_gain, second_shift, out_bias, down_bias]
-        + [jnp.zeros_like(down_bias)] * 2
-    )
     levels = list(range(dp_size.bit_length() - 1))
     other_order = levels[1::-1] + levels[2:]
 
@@ -996,8 +1071,7 @@
             shape_of(heads, length, length),
             one_group,
             one_group,
-            one_group,
-            one_group,
+            shape_of(2, length, group_lanes),
             shape_of(length, width, dtype=F32),
             shape_of(length, width),
             shape_of(8, width, dtype=F32),
@@ -1007,7 +1081,11 @@
             timesteps,
             relative_index,
             bias_table.T,
-            params,
+            first_gain,
+            first_shift,
+            second_gain,
+            second_shift,
+            out_bias,
             tokens,
             time_table.reshape(steps // 8, 8, width),
             query_weight,
@@ -1017,7 +1095,7 @@
             time_value_weight,
             out_weight,
         ],
-        "ssvvv" + "h" * 8,
+        "sswwwwwww" + "h" * 8,
         [
             pltpu.VMEM((6, width, width), BF16),
             pltpu.VMEM((length, width), BF16),
@@ -1030,12 +1108,12 @@
             pltpu.VMEM((groups, length, group_lanes), BF16),
             pltpu.SemaphoreType.DMA((8,)),
         ],
-        us=16.0,
-        vmem=54,
+        us=60.0,
+        away=(0, 1, 2, 3, 4, 5, 6, 7),
+        vmem=56,
     )
     query_rows, key_rows, value_rows, probs = outs[:4]
-    mixed = outs[4:8]
-    middle, normed_own, embed = outs[8:]
+    mixed_own, mixed_near, mixed_far, middle, normed_own, embed = outs[4:]
     normed_near = swap(normed_own, "mp", 1)
     normed_far = swap(normed_own, "mp", 2)
 
@@ -1048,17 +1126,16 @@
             in_specs=[
                 pl.BlockSpec((8, length), lambda i, me: (0, 0)),
                 pl.BlockSpec((length, width), lambda i, me: (i ^ me[0], 0)),
-                pl.BlockSpec((8, width), lambda i, me: (0, 0)),
-                HBM,
-                HBM,
+                VMEM,
+                VMEM,
             ],
             out_specs=pl.BlockSpec((length, width), lambda i, me: (i, 0)),
         ),
         compiler_params=pltpu.CompilerParams(vmem_limit_bytes=40 * MIB),
-        cost_estimate=cost(0.3),
-    )(ranks, relative_index, tokens, params, normed_own, cot_far)
-
-    cot_last = swap(cot_far, "mp", 1)
+        cost_estimate=cost(4.0),
+    )(after(ranks, normed_own, cot_far), relative_index, tokens, first_gain, first_shift)
+
+    cot_last = swap(after(cot_far, normed_own), "mp", 1)
     pair = shape_of(2 * length, width)
     hidden_pair = shape_of(2 * length, hidden_width)
     chunk = shape_of(length, width)
@@ -1072,17 +1149,17 @@
             cotangent,
             cot_near,
             up_weight,
-            line(up_bias),
+            up_bias,
             down_weight,
         ],
         "vvvvvwvw",
         deps=[normed_first, cot_last],
-        us=7.0,
+        us=7.2,
         vmem=FEED,
     )
     near_got = swap(grad_near, "mp", 1)
     normed_last = swap(after(normed_far, grad_near), "mp", 1)
-    mixed_got = [swap(mixed[away], "mp", away) for away in range(1, groups)]
+    mixed_far = swap(mixed_far, "mp", 2)
     active, hidden, moved, grad_far, grad_last, up_bias_sum = run(
         partial(feed_far_kernel, side),
         [hidden_pair, hidden_pair, pair, chunk, chunk, shape_of(8, hidden_width, dtype=F32)],
@@ -1093,12 +1170,12 @@
             cot_far,
             cot_last,
             up_weight,
-            line(up_bias),
+            up_bias,
             down_weight,
             near_hidden,
         ],
         "vvvvvwvwv",
-        us=9.0,
+        us=7.5,
         deps=[near_got],
         vmem=FEED,
     )
@@ -1109,12 +1186,15 @@
         [half, half],
         [ranks, near_active, near_moved, active, moved],
         "svvvv",
-        deps=[up_bias_sum] + mixed_got,
+        deps=[up_bias_sum, mixed_far],
+        us=14.0,
         vmem=FEED,
     )
     down = Total(ranks, levels, keep, send)
     grad_sent = run(add_kernel, chunk, [grad_far, last_got], deps=[keep], vmem=4)
     far_got = swap(grad_sent, "mp", 2)
+    mixed_last = swap(after(mixed_far, grad_sent), "mp", 1)
+    mixed_near = swap(after(mixed_near, grad_sent), "mp", 1)
     half = shape_of(width // 2, hidden_width)
     keep, send = run(
         partial(up_grad_kernel, other_order[0]),
@@ -1123,163 +1203,179 @@
         "s" + "v" * 6,
         [pltpu.VMEM((rows, width), BF16)],
         deps=[grad_sent],
-        us=0.4,
+        us=4.9,
         vmem=FEED,
     )
-    up = Total(ranks, other_order, keep, send)
+    up = Total(ranks, other_order, keep, send, cross=True)
     chunks = shape_of(2, length, width)
     out_keep, out_send = run(
-        out_kernel, [chunks, chunks], [near_active, active, down_weight], "vvw", deps=[keep], us=0.4, vmem=FEED
+        out_kernel, [chunks, chunks], [near_active, active, down_weight], "vvw", deps=[keep], us=5.0, vmem=FEED
     )
     out_got = swap(out_send, "mp", 1)
     grad_branch, grad_middle, middle_sums = run(
         middle_kernel,
         [chunk, shape_of(length, width, dtype=F32), shape_of(8, width, dtype=F32)],
-        [grad_own, near_got, far_got, middle, near_moved, params],
+        [grad_own, near_got, far_got, middle, near_moved, second_gain],
+        "vvvvvw",
         deps=[out_keep],
         vmem=8,
     )
     branch_near = swap(grad_branch, "mp", 1)
     branch_far = swap(grad_branch, "mp", 2)
-    last = down.advance(0, deps=[middle_sums])
+    last = middle_sums
 
     tail = slots * table_lanes // LANES
-    back_scratch = [pltpu.VMEM((side, 2 * slots, span_lanes), F32)]
+    two_groups = pltpu.VMEM((2, length, group_lanes), BF16)
+    back_scratch = [
+        pltpu.VMEM((side, 2 * slots, span_lanes), F32),
+        two_groups,
+        two_groups,
+        two_groups,
+        pltpu.VMEM((2, slots, length, length), BF16),
+        pltpu.SemaphoreType.DMA((2, 4)),
+    ]
     grads_shape = shape_of(3, 2, length, group_lanes)
     packed_shape = shape_of(length + tail, packed_lanes)
+    packed_pair = shape_of(2, length + tail, packed_lanes)
     heads_in = [query_rows, key_rows, value_rows, probs]
-    packed_2, packed_3, far_grads, grad_mixed = run(
+    packed_far, far_grads, grad_mixed = run(
         partial(attend_back_kernel, dims, (2, 3)),
-        [packed_shape, packed_shape, grads_shape, grouped()],
+        [packed_pair, grads_shape, grouped()],
         [ranks, grad_branch, out_weight] + heads_in,
-        "svwvvvv",
+        "svwhhhh",
         back_scratch,
-        deps=[last, branch_near],
-        us=0.8,
-    )
-    packed_2 = swap(packed_2, "mp", 2)
-    packed_3 = swap(packed_3, "mp", 3)
-    last = up.advance(0, deps=[grad_mixed])
-    last = down.advance(1, deps=[last])
+        deps=[last, mixed_last, mixed_near],
+        us=8.3,
+    )
+    packed_far = swap(packed_far, "mp", 2)
+    last = grad_mixed
     packed_0, packed_1, near_grads = run(
         partial(attend_back_kernel, dims, (0, 1)),
         [packed_shape, packed_shape, grads_shape],
         [ranks, grad_mixed] + heads_in,
-        "svvvvv",
+        "svhhhh",
         back_scratch,
         deps=[last],
-        us=0.8,
-    )
-    last = up.advance(1, deps=[packed_0, branch_far, packed_2])
-    packed_1 = swap(packed_1, "mp", 1)
-    branch_last = swap(branch_far, "mp", 1)
-    half = shape_of(group_width, width)
-    more = shape_of(group_width + tail // 2, width)
-    keep_first, keep_second, send_first, send_second = run(
-        partial(weights_kernel, dims, levels[0]),
-        [half, more, half, more],
-        [ranks, normed_first, packed_0, packed_1, packed_2, packed_3]
-        + [grad_branch, branch_near, branch_far, branch_last]
-        + [mixed[0]]
-        + mixed_got,
-        "s" + "v" * 13,
-        [
-            pltpu.VMEM((rows, packed_lanes), BF16),
-            pltpu.VMEM((rows, width), BF16),
-            pltpu.VMEM((rows, group_lanes), BF16),
-        ],
-        deps=[last],
-        us=0.5,
-    )
-    first = Total(ranks, levels, keep_first, send_first)
-    second = Total(ranks, levels, keep_second, send_second, tail // 2)
-    last = keep_second
+        us=8.3,
+    )
+    last = down.split([packed_0, branch_far])
+    branch_last = swap(after(branch_far, last), "mp", 1)
+    last = up.split([last])
     image_rows, tokens_grad = run(
         partial(tokens_kernel, dims),
-        [shape_of(16, width), shape_of(length, width, dtype=F32)],
+        [shape_of(8, width, dtype=F32), shape_of(length, width, dtype=F32)],
         [
             ranks,
-            timesteps,
             near_grads,
             far_grads,
             query_weight,
             key_weight,
             value_weight,
             relative_index,
-            params,
+            first_gain,
             grad_middle,
             middle_sums,
-            embed,
-            jnp.pad(up_bias_sum, ((0, 0), (0, width - hidden_width))),
             tokens,
         ],
-        "ssvvwwwvvvvvvh",
+        "svvwwwwwvvh",
         [
             pltpu.VMEM((3, length, width), BF16),
             pltpu.VMEM((length, width), BF16),
             pltpu.SemaphoreType.DMA,
         ],
-        deps=[last],
-        us=0.7,
+        deps=[last, branch_last],
+        us=8.6,
         away=(1,),
         vmem=24,
     )
-    image_all = lax.all_gather(image_rows, ("dp", "mp"), axis=0, tiled=True)
-    last = image_rows
-
+    lines_far = swap(image_rows, "mp", 2)
+    last = down.exchange([image_rows, packed_far, lines_far])
+    lines_near = swap(jnp.concatenate([image_rows, lines_far], axis=0), "mp", 1)
+    packed_last = swap(after(packed_far, last), "mp", 1)
+    packed_1 = swap(after(packed_1, last), "mp", 1)
+    half = shape_of(group_width, width)
+    images = dp_size * groups
+    tail_rows = max(tail, images)
+    more = shape_of(group_width + tail_rows // 2, width)
+    keep_first, keep_second, send_first, send_second = run(
+        partial(weights_kernel, dims, levels[0]),
+        [more, half, more, half],
+        [ranks, timesteps, normed_first, packed_0, packed_1, packed_far, packed_last]
+        + [grad_branch, branch_near, branch_far, branch_last]
+        + [mixed_own, mixed_near, mixed_far, mixed_last]
+        + [image_rows, lines_far, lines_near, up_bias_sum, time_query_weight, time_value_weight],
+        "ss" + "v" * 17 + "hh",
+        [
+            pltpu.VMEM((rows, packed_lanes), BF16),
+            pltpu.VMEM((rows, width), BF16),
+            pltpu.VMEM((rows, group_lanes), BF16),
+            pltpu.VMEM((tail_rows, width), F32),
+            pltpu.VMEM((2, group_width, width), BF16),
+            pltpu.SemaphoreType.DMA((2,)),
+        ],
+        deps=[last],
+        us=5.2,
+    )
+    first = Total(ranks, levels, keep_first, send_first, tail_rows // 2)
+    last = first.split([keep_second])
+    second = Total(ranks, levels, keep_second, after(send_second, last), cross=True)
+    last = down.finish([last])
+    last = up.exchange([last])
     out_far = swap(add_low(out_keep[1], out_got[1]), "mp", 2)
-
-    stages = len(levels) + 1
-    todo = [(down, 2), (first, 0), (second, 0), (down, 3), (first, 1), (second, 1), (up, 2)]
-    todo += [(up, 3), (first, 2), (second, 2), (first, 3), (second, 3)]
-    for stage in range(4, stages):
-        todo += [(total, stage) for total in (down, up, first, second)]
-    for total, stage in todo:
-        last = total.advance(stage, deps=[last])
-    down_grad = widen(ranks, levels[0], down.keep, down.got)
-    up_grad = widen(ranks, other_order[0], up.keep, up.got)
+    last = second.split([last])
+    last = down.join([last])
+    last = up.finish([last])
+    last = first.exchange([last])
+    last = up.join([last])
+    last = first.finish([last])
+    last = second.exchange([last])
+    last = first.join([last])
+    down_grad = widen(ranks, levels[0], down.keep, down.got, last)
+    last = second.finish([down_grad])
+    last = second.join([last])
+    up_grad = widen(ranks, other_order[1], up.keep, up.got, last, cross=True)
     wide = shape_of(group_width, width, dtype=F32)
-    query_grad, key_grad = run(
-        partial(widen_pair_kernel, levels[0], 0),
-        [wide, wide],
+    query_grad, key_grad, tail_sums = run(
+        partial(widen_pair_kernel, levels[0]),
+        [wide, wide, shape_of(tail_rows, width, dtype=F32)],
         [ranks, first.keep, first.got],
         "svv",
         away=(0, 1),
-    )
-    value_grad, out_grad, table_grad = run(
-        partial(widen_pair_kernel, levels[0], tail // 2),
-        [wide, wide, shape_of(slots, table_lanes, dtype=F32)],
+        deps=[up_grad],
+    )
+    value_grad, out_grad = run(
+        partial(widen_cross_kernel, levels[1]),
+        [wide, wide],
         [ranks, second.keep, second.got],
         "svv",
         away=(0, 1),
-    )
-
-    images = dp_size * groups
-    image_all = image_all.reshape(images, 16, width)[:, :12].transpose(1, 0, 2)
-    time_query_grad, time_value_grad, time_table_grad, sums = run(
+        deps=[query_grad],
+    )
+
+    time_query_grad, time_value_grad, time_table_grad, table_grad, sums = run(
         partial(finish_kernel, dims, images),
         [
             shape_of(group_width, width, dtype=F32),
             shape_of(group_width, width, dtype=F32),
             shape_of(group_width, steps, dtype=F32),
-            shape_of(8, width, dtype=F32),
+            shape_of(slots, table_lanes, dtype=F32),
+            shape_of(16, group_width, dtype=F32),
         ],
-        [ranks, image_all, time_query_weight, time_value_weight],
-        "svhh",
-        [pltpu.VMEM((2, group_width, width), BF16), pltpu.SemaphoreType.DMA((2,))],
+        [tail_sums, time_table],
+        "vw",
         away=(0, 1, 2),
-        vmem=24,
-    )
-    parts = [sums[j, :group_width] for j in range(6)]
-    second_gain_grad, second_shift_grad, out_bias_grad, down_bias_grad = parts[:4]
-    first_gain_grad, first_shift_grad = parts[4:]
+        vmem=52,
+    )
+    first_gain_grad, first_shift_grad, second_gain_grad, second_shift_grad = sums[:4]
+    out_bias_grad, down_bias_grad = sums[4], sums[5]
+    up_bias_grad = sums[6 : 6 + hidden_width // group_width].reshape(-1)
     bias_table_grad = table_grad[:, : stride * stride].T
-    up_bias_grad = sums[6, :hidden_width]
 
     block_out = run(
         partial(block_kernel, side),
         shape_of(length, width),
-        [relative_index, out_keep, out_got, out_far, middle, params],
+        [relative_index, out_keep, out_got, out_far, middle, down_bias],
+        "wvvvvw",
     )
     return (
         block_out,

time: 316 us -> 294 us (0.930)
  local copies, waits for them, and re-layouts: 26.1 us -> 3.06 us
  waiting for transfers between devices: 116 us -> 132 us
  between operations: 14.8 us -> 1.49 us
  starting transfers between devices: 36.8 us -> 42.4 us
  Pallas kernels: 115 us -> 111 us
    unnamed x91 -> x58, local copies, waits for them, and re-layouts: 19.4 us -> 1.15 us
    ppermute x40 -> x42, waiting for transfers between devices: 116 us -> 132 us  [swap(): return lax.ppermute(array, axis, [(i, i ^ distance) for i in range(size)])]
    ppermute x40 -> x42, starting transfers between devices: 36.8 us -> 42.4 us  [swap(): return lax.ppermute(array, axis, [(i, i ^ distance) for i in range(size)])]
    another operation x8 -> x0, local copies, waits for them, and re-layouts: 4.87 us -> none  [on_device(): jnp.stack([first_gain, first_shift, second_gain, second_shift, out_bias,...]
    pallas_call x18, Pallas kernels: 19.8 us -> 15.6 us  [the longest x2 8.67 us: widen(): pl.pallas_call(partial(widen_kernel, level, cross, each), out_shape=shape...]
  transfers between devices with their start and end apart: 41 -> 42, of which waited for: 18 -> 18; matrix products, arithmetic and copies ran while one was open for 3% -> 1% of each run, Pallas kernels for 35% -> 35%
where the time goes in v1:
time: 294 us; the launch traced here: 290 us
  waiting for transfers between devices  132 us (45%)
  Pallas kernels  111 us (38%)
  starting transfers between devices  42.4 us (14%)
  local copies, waits for them, and re-layouts  3.06 us (1%)
    ppermute x42, waiting for transfers between devices, swap(): return lax.ppermute(array, axis, [(i, i ^ distance) for i in range(size)])  132 us
    pallas_call x16, Pallas kernels, run(): pl.pallas_call(body, out_shape=outs, in_specs=[space[kind] for kind in ki...  91.7 us
    ppermute x42, starting transfers between devices, swap(): return lax.ppermute(array, axis, [(i, i ^ distance) for i in range(size)])  42.4 us
    pallas_call x2, Pallas kernels, widen(): pl.pallas_call(partial(widen_kernel, level, cross, each), out_shape=shape...  8.67 us
    pallas_call x16, Pallas kernels, quick(): pl.pallas_call(kernel, out_shape=outs, in_specs=[SMEM if given.shape == (...  6.89 us
  transfers between devices with their start and end apart: 42, of which 18 were waited for; matrix products, arithmetic and copies ran while one was open for 1% of the time, Pallas kernels for 35%

profile of v1, /device:TPU:0, one launch (start us, length us, event | category | flops | bytes accessed | tf_op | source)
XLA Modules:
  0.0 290.4 jit_solution(11083875896472871331)
XLA Ops:
  0.7 3.0 %collective-permute-start = (bf16[256,1152]{1,0:T(8,128)(2,1)}, bf16[256,1152]{1,0:T(8,128)(2,1)S(1)}, u32[]{:S(2)}, u32[]{:S(2)}) collective-permute-start(bf16[256,1152]{1,0:T(8,128)(2,1)} %refs_3_.2), channel_id=1, source_target_pairs={{0,2},{1,3},{2,0},{3,1},{4,6},{5,7},{6,4},{7,5},{8,10},{9,11},{10,... | collective-permute-start | bytes 1769480 | tf_op jit(solution)/shard_map/ppermute | solution.py:954
  4.3 19.2 %shard_map.348 = (bf16[4,256,384]{2,1,0:T(8,128)(2,1)}, bf16[4,256,384]{2,1,0:T(8,128)(2,1)}, bf16[4,256,384]{2,1,0:T(8,128)(2,1)}, bf16[16,256,256]{2,1,0:T(8,1...) custom-call(s32[2]{0:T(128)} %pad_add_fusion.refs_0_.ranks, ...), custom_call_target="tpu_custom_call" | custom-call | flops 20700000256 | bytes 1000 | tf_op jit(solution)/shard_map/pallas_call | solution.py:892
  24.3 3.5 %shard_map.349.refs_2_ = bf16[1024,1152]{1,0:T(8,128)(2,1)S(1)} custom-call(s32[2]{0:T(128)S(1)} %copy-done.9, s32[256,256]{1,0:T(8,128)S(1)} %copy-done.7, bf16[1024,1152]{1,0:T(8,128)(2,1)S(1)} %copy-done.6, f32[1152]{0:T(1024)S(1)} %copy-done.11, f32[1152]{0:T(1024)S(1)} %copy-done.21), custom_call_target="tpu_custom_call" | custom-call | flops 1380000000 | bytes 1000 | tf_op jit(solution)/shard_map/pallas_call | solution.py:1120
  27.8 7.2 %shard_map.350 = (bf16[512,1152]{1,0:T(8,128)(2,1)S(1)}, bf16[512,1152]{1,0:T(8,128)(2,1)S(1)}, bf16[512,1152]{1,0:T(8,128)(2,1)S(1)}, bf16[256,1152]{1,0:T(8,128)(2,1)S(1)}, bf16[256,1152]{1,0:T(8,128)(2,1)S(1)}) custom-call(s32[256,256]{1,0:T(8,128)S(1)} %copy-done.7, bf16[256,1152]{1,0:T(8,128)(2,1)S(1)} %copy-done.20, ...), custom_call_target="tpu_custom_call" | custom-call | flops 2484000000 | bytes 1000 | tf_op jit(solution)/shard_map/pallas_call | solution.py:892
  35.4 4.6 %collective-permute-done.5.refs_1_.refs_3_ = bf16[256,1152]{1,0:T(8,128)(2,1)S(1)} collective-permute-done((bf16[256,1152]{1,0:T(8,128)(2,1)}, bf16[256,1152]{1,0:T(8,128)(2,1)S(1)}, u32[]{:S(2)}, u32[]{:S(2)}) %collective-permute-start.5) | collective-permute-done | bytes 589856 | tf_op jit(solution)/shard_map/ppermute | solution.py:954
  42.1 7.4 %shard_map.351 = (bf16[512,1152]{1,0:T(8,128)(2,1)S(1)}, bf16[512,1152]{1,0:T(8,128)(2,1)S(1)}, bf16[512,1152]{1,0:T(8,128)(2,1)S(1)}, bf16[256,1152]{1,0:T(8,12...) custom-call(s32[256,256]{1,0:T(8,128)S(1)} %copy-done.7, ...), custom_call_target="tpu_custom_call" | custom-call | flops 2587500032 | bytes 1000 | tf_op jit(solution)/shard_map/pallas_call | solution.py:892
  51.6 3.8 %shard_map.352 = (bf16[576,1152]{1,0:T(8,128)(2,1)S(1)}, bf16[576,1152]{1,0:T(8,128)(2,1)S(1)}) custom-call(s32[2]{0:T(128)S(1)} %copy-done.9, bf16[512,1152]{1,0:T(8,128)(2,1)S(1)} %get-tuple-element.140.refs_1_.refs_0_, bf16[512,1152]{1,0:T(8,128)(2,1)S(1)} %get-tuple-element.131.refs_2_.refs_4_, bf16[512,1152]{1,0:T(8,128)(2,1)S(1)} %get-tuple-element.132.refs_3_.refs_1_, ...), custom_call_target="tpu_custom_call" | custom-call | flops 4830000128 | bytes 1000 | tf_op jit(solution)/shard_map/pallas_call | solution.py:892
  57.8 3.9 %shard_map.354 = (bf16[576,1152]{1,0:T(8,128)(2,1)S(1)}, bf16[576,1152]{1,0:T(8,128)(2,1)S(1)}) custom-call(s32[2]{0:T(128)S(1)} %copy-done.9, bf16[256,1152]{1,0:T(8,128)(2,1)S(1)} %copy-done.20, bf16[256,1152]{1,0:T(8,128)(2,1)S(1)} %collective-permute-done.2.refs_2_, bf16[256,1152]{1,0:T(8,128)(2,1)S(1)} %collective-permute-done.5.refs_1_.refs_3_, ...), custom_call_target="tpu_custom_call" | custom-call | flops 1690499968 | bytes 1000 | tf_op jit(solution)/shard_map/pallas_call | solution.py:892
  63.9 4.0 %shard_map.355 = (bf16[2,256,1152]{2,1,0:T(8,128)(2,1)S(1)}, bf16[2,256,1152]{2,1,0:T(8,128)(2,1)S(1)}) custom-call(bf16[512,1152]{1,0:T(8,128)(2,1)S(1)} %get-tuple-element.140.refs_1_.refs_0_, bf16[512,1152]{1,0:T(8,128)(2,1)S(1)} %get-tuple-element.132.refs_3_.refs_1_, bf16[1152,1152]{1,0:T(8,128)(2,1)S(1)} %copy-done.15), custom_call_target="tpu_custom_call" | custom-call | flops 1724999936 | bytes 1000 | tf_op jit(solution)/shard_map/pallas_call | solution.py:892
  68.9 3.0 %collective-permute-done.11.refs_2_ = bf16[256,1152]{1,0:T(8,128)(2,1)S(1)} collective-permute-done((bf16[256,1152]{1,0:T(8,128)(2,1)S(1)}, bf16[256,1152]{1,0:T(8,128)(2,1)S(1)}, u32[]{:S(2)}, u32[]{:S(2)}) %collective-permute-start.11) | collective-permute-done | bytes 589856 | tf_op jit(solution)/shard_map/ppermute | solution.py:954
  74.2 10.0 %shard_map.358 = (bf16[2,288,896]{2,1,0:T(8,128)(2,1)S(1)}, bf16[3,2,256,384]{3,2,1,0:T(8,128)(2,1)S(1)}, bf16[4,256,384]{2,1,0:T(8,128)(2,1)S(1)}) custom-call(s32[2]{0:T(128)S(1)} %copy-done.9, bf16[256,1152]{1,0:T(8,128)(2,1)S(1)} %get-tuple-element.151.refs_1_.refs_7_, bf16[1152,1152]{1,0:T(8,128)(2,1)S(1)} %copy-done.16, ...), custom_call_target="tpu_custom_call" | custom-call | flops 2863500032 | bytes 1000 | tf_op jit(solution)/shard_map/pallas_call | solution.py:892
  85.7 9.0 %shard_map.359 = (bf16[288,896]{1,0:T(8,128)(2,1)S(1)}, bf16[288,896]{1,0:T(8,128)(2,1)S(1)}, bf16[3,2,256,384]{3,2,1,0:T(8,128)(2,1)S(1)}) custom-call(s32[2]{0:T(128)S(1)} %copy-done.9, bf16[4,256,384]{2,1,0:T(8,128)(2,1)S(1)} %get-tuple-element.156.refs_1_, bf16[4,256,384]{2,1,0:T(8,128)(2,1)S(1)} %copy-done.24, bf16[4,256,384]{2,1,0:T(8,128)(2,1)S(1)} %copy-done.25, ...), custom_call_target="tpu_custom_call" | custom-call | flops 2863500032 | bytes 1000 | tf_op jit(solution)/shard_map/pallas_call | solution.py:892
  98.5 8.8 %shard_map.362 = (f32[8,1152]{1,0:T(8,128)S(1)}, f32[256,1152]{1,0:T(8,128)}) custom-call(s32[2]{0:T(128)S(1)} %copy-done.9, bf16[3,2,256,384]{3,2,1,0:T(8,128)(2,1)S(1)} %get-tuple-element.167.refs_1_, bf16[3,2,256,384]{3,2,1,0:T(8,128)(2,1)S(1)} %get-tuple-element.168.refs_2_, bf16[1152,1152]{1,0:T(8,128)(2,1)S(1)} %copy-done.1, ...), custom_call_target="tpu_custom_call" | custom-call | flops 2967000064 | bytes 1000 | tf_op jit(solution)/shard_map/pallas_call | solution.py:892
  114.4 2.5 collective-permute-done.23.refs_8_
  117.8 6.1 %shard_map.364 = (bf16[304,1152]{1,0:T(8,128)(2,1)S(1)}, bf16[288,1152]{1,0:T(8,128)(2,1)S(1)}, bf16[304,1152]{1,0:T(8,128)(2,1)S(1)}, bf16[288,1152]{1,0:T(8,128)(2,1)S(1)}) custom-call(s32[2]{0:T(128)S(1)} %copy-done.9, s32[4]{0:T(128)S(1)} %copy-done.13, bf16[1024,1152]{1,0:T(8,128)(2,1)S(1)} %shard_map.349.refs_2_, ...), custom_call_target="tpu_custom_call" | custom-call | flops 1794000000 | bytes 1000 | tf_op jit(solution)/shard_map/pallas_call | solution.py:892
  124.4 2.6 collective-permute-start.26
  128.5 13.9 %collective-permute-done.25.got = bf16[304,1152]{1,0:T(8,128)(2,1)S(1)} collective-permute-done((bf16[304,1152]{1,0:T(8,128)(2,1)S(1)}, bf16[304,1152]{1,0:T(8,128)(2,1)S(1)}, u32[]{:S(2)}, u32[]{:S(2)}) %collective-permute-start.25) | collective-permute-done | bytes 700448 | tf_op jit(solution)/shard_map/ppermute | solution.py:954
  143.8 12.4 %collective-permute-done.26.right = bf16[288,1152]{1,0:T(8,128)(2,1)S(1)} collective-permute-done((bf16[288,1152]{1,0:T(8,128)(2,1)S(1)}, bf16[288,1152]{1,0:T(8,128)(2,1)S(1)}, u32[]{:S(2)}, u32[]{:S(2)}) %collective-permute-start.26) | collective-permute-done | bytes 663584 | tf_op jit(solution)/shard_map/ppermute | solution.py:954
  157.3 3.4 %collective-permute-start.30 = (bf16[288,1152]{1,0:T(8,128)(2,1)S(1)}, bf16[288,1152]{1,0:T(8,128)(2,1)S(1)}, u32[]{:S(2)}, u32[]{:S(2)}) collective-permute-start(bf16[288,1152]{1,0:T(8,128)(2,1)S(1)} %shard_map.367.left), channel_id=1, source_target_pairs={{0,16},{4,20},{8,24},{12,28},{16,0},{20,4},{24,8},{28,12},{1,17},{... | collective-permute-start | bytes 1990664 | tf_op jit(solution)/shard_map/ppermute | solution.py:954
  160.7 9.4 %collective-permute-done.28.got = bf16[288,1152]{1,0:T(8,128)(2,1)S(1)} collective-permute-done((bf16[288,1152]{1,0:T(8,128)(2,1)S(1)}, bf16[288,1152]{1,0:T(8,128)(2,1)S(1)}, u32[]{:S(2)}, u32[]{:S(2)}) %collective-permute-start.28) | collective-permute-done | bytes 663584 | tf_op jit(solution)/shard_map/ppermute | solution.py:954
  170.8 15.1 %collective-permute-done.29.other = bf16[288,1152]{1,0:T(8,128)(2,1)S(1)} collective-permute-done((bf16[288,1152]{1,0:T(8,128)(2,1)S(1)}, bf16[288,1152]{1,0:T(8,128)(2,1)S(1)}, u32[]{:S(2)}, u32[]{:S(2)}) %collective-permute-start.29) | collective-permute-done | bytes 663584 | tf_op jit(solution)/shard_map/ppermute | solution.py:954
  186.6 3.2 %collective-permute-done.30.right = bf16[288,1152]{1,0:T(8,128)(2,1)S(1)} collective-permute-done((bf16[288,1152]{1,0:T(8,128)(2,1)S(1)}, bf16[288,1152]{1,0:T(8,128)(2,1)S(1)}, u32[]{:S(2)}, u32[]{:S(2)}) %collective-permute-start.30) | collective-permute-done | bytes 663584 | tf_op jit(solution)/shard_map/ppermute | solution.py:954
  193.6 18.6 %collective-permute-done.31.right = bf16[152,1152]{1,0:T(8,128)(2,1)S(1)} collective-permute-done((bf16[152,1152]{1,0:T(8,128)(2,1)S(1)}, bf16[152,1152]{1,0:T(8,128)(2,1)S(1)}, u32[]{:S(2)}, u32[]{:S(2)}) %collective-permute-start.31) | collective-permute-done | bytes 350240 | tf_op jit(solution)/shard_map/ppermute | solution.py:954
  212.2 2.3 collective-permute-start.33
  218.8 9.8 %collective-permute-done.33.right = bf16[152,1152]{1,0:T(8,128)(2,1)S(1)} collective-permute-done((bf16[152,1152]{1,0:T(8,128)(2,1)S(1)}, bf16[152,1152]{1,0:T(8,128)(2,1)S(1)}, u32[]{:S(2)}, u32[]{:S(2)}) %collective-permute-start.33) | collective-permute-done | bytes 350240 | tf_op jit(solution)/shard_map/ppermute | solution.py:954
  229.6 3.4 %collective-permute-start.37 = (bf16[144,1152]{1,0:T(8,128)(2,1)S(1)}, bf16[144,1152]{1,0:T(8,128)(2,1)S(1)}, u32[]{:S(2)}, u32[]{:S(2)}) collective-permute-start(bf16[144,1152]{1,0:T(8,128)(2,1)S(1)} %shard_map.374.left), channel_id=1, source_target_pairs={{0,16},{4,20},{8,24},{12,28},{16,0},{20,4},{24,8},{28,12},{1,17},{... | collective-permute-start | bytes 995336 | tf_op jit(solution)/shard_map/ppermute | solution.py:954
  233.8 11.1 %collective-permute-done.35.other = bf16[152,1152]{1,0:T(8,128)(2,1)S(1)} collective-permute-done((bf16[152,1152]{1,0:T(8,128)(2,1)S(1)}, bf16[152,1152]{1,0:T(8,128)(2,1)S(1)}, u32[]{:S(2)}, u32[]{:S(2)}) %collective-permute-start.35) | collective-permute-done | bytes 350240 | tf_op jit(solution)/shard_map/ppermute | solution.py:954
  245.6 2.2 collective-permute-start.40
  247.8 4.3 %shard_map.376 = f32[1152,1152]{1,0:T(8,128)} custom-call(s32[2]{0:T(128)S(1)} %copy-done.9, bf16[576,1152]{1,0:T(8,128)(2,1)S(1)} %shard_map.369.own, bf16[576,1152]{1,0:T(8,128)(2,1)S(1)} %collective-permute-done.36.other), custom_call_target="tpu_custom_call" | custom-call | flops 1207500032 | bytes 1000 | tf_op jit(solution)/shard_map/pallas_call | solution.py:935
  252.3 18.6 %collective-permute-done.38.other = bf16[144,1152]{1,0:T(8,128)(2,1)S(1)} collective-permute-done((bf16[144,1152]{1,0:T(8,128)(2,1)S(1)}, bf16[144,1152]{1,0:T(8,128)(2,1)S(1)}, u32[]{:S(2)}, u32[]{:S(2)}) %collective-permute-start.38) | collective-permute-done | bytes 331808 | tf_op jit(solution)/shard_map/ppermute | solution.py:954
  275.2 4.3 %shard_map.379 = f32[1152,1152]{1,0:T(8,128)} custom-call(s32[2]{0:T(128)S(1)} %copy-done.9, bf16[576,1152]{1,0:T(8,128)(2,1)S(1)} %shard_map.372.own, bf16[576,1152]{1,0:T(8,128)(2,1)S(1)} %collective-permute-done.39.other), custom_call_target="tpu_custom_call" | custom-call | flops 1207500032 | bytes 1000 | tf_op jit(solution)/shard_map/pallas_call | solution.py:935
  281.7 4.3 %shard_map.381 = (f32[288,1152]{1,0:T(8,128)}, f32[288,1152]{1,0:T(8,128)}, f32[288,1000]{1,0:T(8,128)}, f32[4,1024]{1,0:T(4,128)S(1)}, f32[16,288]{1,0:T(8,128)S(1)}) custom-call(f32[32,1152]{1,0:T(8,128)S(1)} %get-tuple-element.206.refs_0_, bf16[1000,1152]{1,0:T(8,128)(2,1)} %refs_1_.5), custom_call_target="tpu_custom_call" | custom-call | flops 862499968 | bytes 1000 | tf_op jit(solution)/shard_map/pallas_call | solution.py:892
  (152 shorter events, 53.8 us)
Async XLA Ops:
  0.7 22.8 %collective-permute-start = (bf16[256,1152]{1,0:T(8,128)(2,1)}, bf16[256,1152]{1,0:T(8,128)(2,1)S(1)}, u32[]{:S(2)}, u32[]{:S(2)}) collective-permute-start(bf16[256,1152]{1,0:T(8,128)(2,1)} %refs_3_.2), channel_id=1, source_target_pairs={{0,2},{1,3},{2,0},{3,1},{4,6},{5,7},{6,4},{7,5},{8,10},{9,11},{10,... | collective-permute-start | bytes 1769480 | tf_op jit(solution)/shard_map/ppermute | solution.py:954
  24.2 15.9 %collective-permute-start.5 = (bf16[256,1152]{1,0:T(8,128)(2,1)}, bf16[256,1152]{1,0:T(8,128)(2,1)S(1)}, u32[]{:S(2)}, u32[]{:S(2)}) collective-permute-start(bf16[256,1152]{1,0:T(8,128)(2,1)} %get-tuple-element.118.refs_1_), channel_id=1, source_target_pairs={{0,2},{1,3},{2,0},{3,1},{4,6},{5,7},{6,4},{7,5},{8,10},{9,11},{10,... | collective-permute-start | bytes 1769480 | tf_op jit(solution)/shard_map/ppermute | solution.py:954
  35.0 5.4 %collective-permute-start.4 = (bf16[256,1152]{1,0:T(8,128)(2,1)S(1)}, bf16[256,1152]{1,0:T(8,128)(2,1)S(1)}, u32[]{:S(2)}, u32[]{:S(2)}) collective-permute-start(bf16[256,1152]{1,0:T(8,128)(2,1)S(1)} %get-tuple-element.123), channel_id=1, source_target_pairs={{0,1},{1,0},{2,3},{3,2},{4,5},{5,4},{6,7},{7,6},{8,9},{9,8},{10,11... | collective-permute-start | bytes 1769480 | tf_op jit(solution)/shard_map/ppermute | solution.py:954
  40.1 11.5 %collective-permute-start.7 = (bf16[2,256,384]{2,1,0:T(8,128)(2,1)S(1)}, bf16[2,256,384]{2,1,0:T(8,128)(2,1)S(1)}, u32[]{:S(2)}, u32[]{:S(2)}) collective-permute-start(bf16[2,256,384]{2,1,0:T(8,128)(2,1)S(1)} %copy-done.27), channel_id=1, source_target_pairs={{0,2},{1,3},{2,0},{3,1},{4,6},{5,7},{6,4},{7,5},{8,10},{9,11},{10,... | collective-permute-start | bytes 1179656 | tf_op jit(solution)/shard_map/ppermute | solution.py:954
  49.5 7.5 %collective-permute-start.8 = (bf16[256,1152]{1,0:T(8,128)(2,1)S(1)}, bf16[256,1152]{1,0:T(8,128)(2,1)S(1)}, u32[]{:S(2)}, u32[]{:S(2)}) collective-permute-start(bf16[256,1152]{1,0:T(8,128)(2,1)S(1)} %get-tuple-element.136), channel_id=1, source_target_pairs={{0,1},{1,0},{2,3},{3,2},{4,5},{5,4},{6,7},{7,6},{8,9},{9,8},{10,11... | collective-permute-start | bytes 1769480 | tf_op jit(solution)/shard_map/ppermute | solution.py:954
  55.4 39.3 %collective-permute-start.15 = (bf16[576,1152]{1,0:T(8,128)(2,1)S(1)}, bf16[576,1152]{1,0:T(8,128)(2,1)S(1)}, u32[]{:S(2)}, u32[]{:S(2)}) collective-permute-start(bf16[576,1152]{1,0:T(8,128)(2,1)S(1)} %get-tuple-element.160), channel_id=1, source_target_pairs={{0,4},{4,0},{8,12},{12,8},{16,20},{20,16},{24,28},{28,24},{1,5},{5... | collective-permute-start | bytes 3981320 | tf_op jit(solution)/shard_map/ppermute | solution.py:954
  57.2 14.7 %collective-permute-start.11 = (bf16[256,1152]{1,0:T(8,128)(2,1)S(1)}, bf16[256,1152]{1,0:T(8,128)(2,1)S(1)}, u32[]{:S(2)}, u32[]{:S(2)}) collective-permute-start(bf16[256,1152]{1,0:T(8,128)(2,1)S(1)} %shard_map.353), channel_id=1, source_target_pairs={{0,2},{1,3},{2,0},{3,1},{4,6},{5,7},{6,4},{7,5},{8,10},{9,11},{10,... | collective-permute-start | bytes 1769480 | tf_op jit(solution)/shard_map/ppermute | solution.py:954
  57.8 16.4 %collective-permute-start.12 = (bf16[2,256,384]{2,1,0:T(8,128)(2,1)S(1)}, bf16[2,256,384]{2,1,0:T(8,128)(2,1)S(1)}, u32[]{:S(2)}, u32[]{:S(2)}) collective-permute-start(bf16[2,256,384]{2,1,0:T(8,128)(2,1)S(1)} %collective-permute-done.7.refs_13_), channel_id=1, source_target_pairs={{0,1},{1,0},{2,3},{3,2},{4,5},{5,4},{6,7},{7,6},{8,9},{9,8},{10,11... | collective-permute-start | bytes 1179656 | tf_op jit(solution)/shard_map/ppermute | solution.py:954
  61.7 12.5 %collective-permute-start.13 = (bf16[256,384]{1,0:T(8,128)(2,1)S(1)}, bf16[256,384]{1,0:T(8,128)(2,1)S(1)}, u32[]{:S(2)}, u32[]{:S(2)}) collective-permute-start(bf16[256,384]{1,0:T(8,128)(2,1)S(1)} %copy-done.28), channel_id=1, source_target_pairs={{0,1},{1,0},{2,3},{3,2},{4,5},{5,4},{6,7},{7,6},{8,9},{9,8},{10,11... | collective-permute-start | bytes 589832 | tf_op jit(solution)/shard_map/ppermute | solution.py:954
  62.3 35.2 %collective-permute-start.16 = (bf16[576,1152]{1,0:T(8,128)(2,1)S(1)}, bf16[576,1152]{1,0:T(8,128)(2,1)S(1)}, u32[]{:S(2)}, u32[]{:S(2)}) collective-permute-start(bf16[576,1152]{1,0:T(8,128)(2,1)S(1)} %get-tuple-element.163), channel_id=1, source_target_pairs={{0,8},{4,12},{8,0},{12,4},{16,24},{20,28},{24,16},{28,20},{1,9},{5... | collective-permute-start | bytes 3981320 | tf_op jit(solution)/shard_map/ppermute | solution.py:954
  73.5 21.2 %collective-permute-start.14 = (bf16[256,1152]{1,0:T(8,128)(2,1)S(1)}, bf16[256,1152]{1,0:T(8,128)(2,1)S(1)}, u32[]{:S(2)}, u32[]{:S(2)}) collective-permute-start(bf16[256,1152]{1,0:T(8,128)(2,1)S(1)} %get-tuple-element.151.refs_1_.refs_7_), channel_id=1, source_target_pairs={{0,2},{1,3},{2,0},{3,1},{4,6},{5,7},{6,4},{7,5},{8,10},{9,11},{10,... | collective-permute-start | bytes 1769480 | tf_op jit(solution)/shard_map/ppermute | solution.py:954
  84.2 25.3 %collective-permute-start.18 = (bf16[2,288,896]{2,1,0:T(8,128)(2,1)S(1)}, bf16[2,288,896]{2,1,0:T(8,128)(2,1)S(1)}, u32[]{:S(2)}, u32[]{:S(2)}) collective-permute-start(bf16[2,288,896]{2,1,0:T(8,128)(2,1)S(1)} %get-tuple-element.172), channel_id=1, source_target_pairs={{0,2},{1,3},{2,0},{3,1},{4,6},{5,7},{6,4},{7,5},{8,10},{9,11},{10,... | collective-permute-start | bytes 3096584 | tf_op jit(solution)/shard_map/ppermute | solution.py:954
  95.9 17.3 %collective-permute-start.20 = (bf16[288,1152]{1,0:T(8,128)(2,1)S(1)}, bf16[288,1152]{1,0:T(8,128)(2,1)S(1)}, u32[]{:S(2)}, u32[]{:S(2)}) collective-permute-start(bf16[288,1152]{1,0:T(8,128)(2,1)S(1)} %get-tuple-element.174), channel_id=1, source_target_pairs={{0,8},{4,12},{8,0},{12,4},{16,24},{20,28},{24,16},{28,20},{1,9},{5... | collective-permute-start | bytes 1990664 | tf_op jit(solution)/shard_map/ppermute | solution.py:954
  123.8 18.6 %collective-permute-start.25 = (bf16[304,1152]{1,0:T(8,128)(2,1)S(1)}, bf16[304,1152]{1,0:T(8,128)(2,1)S(1)}, u32[]{:S(2)}, u32[]{:S(2)}) collective-permute-start(bf16[304,1152]{1,0:T(8,128)(2,1)S(1)} %get-tuple-element.183), channel_id=1, source_target_pairs={{0,4},{4,0},{8,12},{12,8},{16,20},{20,16},{24,28},{28,24},{1,5},{5... | collective-permute-start | bytes 2101256 | tf_op jit(solution)/shard_map/ppermute | solution.py:954
  124.4 31.8 %collective-permute-start.26 = (bf16[288,1152]{1,0:T(8,128)(2,1)S(1)}, bf16[288,1152]{1,0:T(8,128)(2,1)S(1)}, u32[]{:S(2)}, u32[]{:S(2)}) collective-permute-start(bf16[288,1152]{1,0:T(8,128)(2,1)S(1)} %shard_map.363.left), channel_id=1, source_target_pairs={{0,16},{4,20},{8,24},{12,28},{16,0},{20,4},{24,8},{28,12},{1,17},{... | collective-permute-start | bytes 1990664 | tf_op jit(solution)/shard_map/ppermute | solution.py:954
  127.0 30.1 %collective-permute-start.27 = (bf16[288,1152]{1,0:T(8,128)(2,1)S(1)}, bf16[288,1152]{1,0:T(8,128)(2,1)S(1)}, u32[]{:S(2)}, u32[]{:S(2)}) collective-permute-start(bf16[288,1152]{1,0:T(8,128)(2,1)S(1)} %get-tuple-element.187), channel_id=1, source_target_pairs={{0,4},{4,0},{8,12},{12,8},{16,20},{20,16},{24,28},{28,24},{1,5},{5... | collective-permute-start | bytes 1990664 | tf_op jit(solution)/shard_map/ppermute | solution.py:954
  143.2 26.9 %collective-permute-start.28 = (bf16[288,1152]{1,0:T(8,128)(2,1)S(1)}, bf16[288,1152]{1,0:T(8,128)(2,1)S(1)}, u32[]{:S(2)}, u32[]{:S(2)}) collective-permute-start(bf16[288,1152]{1,0:T(8,128)(2,1)S(1)} %get-tuple-element.190), channel_id=1, source_target_pairs={{0,4},{4,0},{8,12},{12,8},{16,20},{20,16},{24,28},{28,24},{1,5},{5... | collective-permute-start | bytes 1990664 | tf_op jit(solution)/shard_map/ppermute | solution.py:954
  156.4 29.6 %collective-permute-start.29 = (bf16[288,1152]{1,0:T(8,128)(2,1)S(1)}, bf16[288,1152]{1,0:T(8,128)(2,1)S(1)}, u32[]{:S(2)}, u32[]{:S(2)}) collective-permute-start(bf16[288,1152]{1,0:T(8,128)(2,1)S(1)} %shard_map.366.own), channel_id=1, source_target_pairs={{0,8},{4,12},{8,0},{12,4},{16,24},{20,28},{24,16},{28,20},{1,9},{5... | collective-permute-start | bytes 1990664 | tf_op jit(solution)/shard_map/ppermute | solution.py:954
  157.3 32.5 %collective-permute-start.30 = (bf16[288,1152]{1,0:T(8,128)(2,1)S(1)}, bf16[288,1152]{1,0:T(8,128)(2,1)S(1)}, u32[]{:S(2)}, u32[]{:S(2)}) collective-permute-start(bf16[288,1152]{1,0:T(8,128)(2,1)S(1)} %shard_map.367.left), channel_id=1, source_target_pairs={{0,16},{4,20},{8,24},{12,28},{16,0},{20,4},{24,8},{28,12},{1,17},{... | collective-permute-start | bytes 1990664 | tf_op jit(solution)/shard_map/ppermute | solution.py:954
  160.7 72.3 %collective-permute-start.9 = (bf16[2,256,1152]{2,1,0:T(8,128)(2,1)S(1)}, bf16[2,256,1152]{2,1,0:T(8,128)(2,1)S(1)}, u32[]{:S(2)}, u32[]{:S(2)}) collective-permute-start(bf16[2,256,1152]{2,1,0:T(8,128)(2,1)S(1)} %copy-done.18), channel_id=1, source_target_pairs={{0,1},{1,0},{2,3},{3,2},{4,5},{5,4},{6,7},{7,6},{8,9},{9,8},{10,11... | collective-permute-start | bytes 3538952 | tf_op jit(solution)/shard_map/ppermute | solution.py:954
  189.9 26.3 %collective-permute-start.32 = (bf16[288,1152]{1,0:T(8,128)(2,1)S(1)}, bf16[288,1152]{1,0:T(8,128)(2,1)S(1)}, u32[]{:S(2)}, u32[]{:S(2)}) collective-permute-start(bf16[288,1152]{1,0:T(8,128)(2,1)S(1)} %shard_map.370.own), channel_id=1, source_target_pairs={{0,8},{4,12},{8,0},{12,4},{16,24},{20,28},{24,16},{28,20},{1,9},{5... | collective-permute-start | bytes 1990664 | tf_op jit(solution)/shard_map/ppermute | solution.py:954
  190.1 22.0 %collective-permute-start.31 = (bf16[152,1152]{1,0:T(8,128)(2,1)S(1)}, bf16[152,1152]{1,0:T(8,128)(2,1)S(1)}, u32[]{:S(2)}, u32[]{:S(2)}) collective-permute-start(bf16[152,1152]{1,0:T(8,128)(2,1)S(1)} %get-tuple-element.195), channel_id=1, source_target_pairs={{0,8},{4,12},{8,0},{12,4},{16,24},{20,28},{24,16},{28,20},{1,9},{5... | collective-permute-start | bytes 1050632 | tf_op jit(solution)/shard_map/ppermute | solution.py:954
  192.0 55.8 %collective-permute-start.36 = (bf16[576,1152]{1,0:T(8,128)(2,1)S(1)}, bf16[576,1152]{1,0:T(8,128)(2,1)S(1)}, u32[]{:S(2)}, u32[]{:S(2)}) collective-permute-start(bf16[576,1152]{1,0:T(8,128)(2,1)S(1)} %shard_map.369.own), channel_id=1, source_target_pairs={{0,4},{4,0},{8,12},{12,8},{16,20},{20,16},{24,28},{28,24},{1,5},{5... | collective-permute-start | bytes 3981320 | tf_op jit(solution)/shard_map/ppermute | solution.py:954
  212.2 16.4 %collective-permute-start.33 = (bf16[152,1152]{1,0:T(8,128)(2,1)S(1)}, bf16[152,1152]{1,0:T(8,128)(2,1)S(1)}, u32[]{:S(2)}, u32[]{:S(2)}) collective-permute-start(bf16[152,1152]{1,0:T(8,128)(2,1)S(1)} %shard_map.371.left), channel_id=1, source_target_pairs={{0,16},{4,20},{8,24},{12,28},{16,0},{20,4},{24,8},{28,12},{1,17},{... | collective-permute-start | bytes 1050632 | tf_op jit(solution)/shard_map/ppermute | solution.py:954
  214.5 14.9 %collective-permute-start.34 = (bf16[144,1152]{1,0:T(8,128)(2,1)S(1)}, bf16[144,1152]{1,0:T(8,128)(2,1)S(1)}, u32[]{:S(2)}, u32[]{:S(2)}) collective-permute-start(bf16[144,1152]{1,0:T(8,128)(2,1)S(1)} %get-tuple-element.199), channel_id=1, source_target_pairs={{0,8},{4,12},{8,0},{12,4},{16,24},{20,28},{24,16},{28,20},{1,9},{5... | collective-permute-start | bytes 995336 | tf_op jit(solution)/shard_map/ppermute | solution.py:954
  216.9 58.3 %collective-permute-start.39 = (bf16[576,1152]{1,0:T(8,128)(2,1)S(1)}, bf16[576,1152]{1,0:T(8,128)(2,1)S(1)}, u32[]{:S(2)}, u32[]{:S(2)}) collective-permute-start(bf16[576,1152]{1,0:T(8,128)(2,1)S(1)} %shard_map.372.own), channel_id=1, source_target_pairs={{0,4},{4,0},{8,12},{12,8},{16,20},{20,16},{24,28},{28,24},{1,5},{5... | collective-permute-start | bytes 3981320 | tf_op jit(solution)/shard_map/ppermute | solution.py:954
  228.7 16.3 %collective-permute-start.35 = (bf16[152,1152]{1,0:T(8,128)(2,1)S(1)}, bf16[152,1152]{1,0:T(8,128)(2,1)S(1)}, u32[]{:S(2)}, u32[]{:S(2)}) collective-permute-start(bf16[152,1152]{1,0:T(8,128)(2,1)S(1)} %shard_map.373.own), channel_id=1, source_target_pairs={{0,8},{4,12},{8,0},{12,4},{16,24},{20,28},{24,16},{28,20},{1,9},{5... | collective-permute-start | bytes 1050632 | tf_op jit(solution)/shard_map/ppermute | solution.py:954
  229.6 22.6 %collective-permute-start.37 = (bf16[144,1152]{1,0:T(8,128)(2,1)S(1)}, bf16[144,1152]{1,0:T(8,128)(2,1)S(1)}, u32[]{:S(2)}, u32[]{:S(2)}) collective-permute-start(bf16[144,1152]{1,0:T(8,128)(2,1)S(1)} %shard_map.374.left), channel_id=1, source_target_pairs={{0,16},{4,20},{8,24},{12,28},{16,0},{20,4},{24,8},{28,12},{1,17},{... | collective-permute-start | bytes 995336 | tf_op jit(solution)/shard_map/ppermute | solution.py:954
  233.2 40.1 %collective-permute-start.10 = (bf16[256,1152]{1,0:T(8,128)(2,1)S(1)}, bf16[256,1152]{1,0:T(8,128)(2,1)S(1)}, u32[]{:S(2)}, u32[]{:S(2)}) collective-permute-start(bf16[256,1152]{1,0:T(8,128)(2,1)S(1)} %fusion), channel_id=1, source_target_pairs={{0,2},{1,3},{2,0},{3,1},{4,6},{5,7},{6,4},{7,5},{8,10},{9,11},{10,... | collective-permute-start | bytes 1769480 | tf_op jit(solution)/shard_map/ppermute | solution.py:954
  245.6 34.0 %collective-permute-start.40 = (bf16[304,1152]{1,0:T(8,128)(2,1)S(1)}, bf16[304,1152]{1,0:T(8,128)(2,1)S(1)}, u32[]{:S(2)}, u32[]{:S(2)}) collective-permute-start(bf16[304,1152]{1,0:T(8,128)(2,1)S(1)} %shard_map.375.refs_1_), channel_id=1, source_target_pairs={{0,4},{4,0},{8,12},{12,8},{16,20},{20,16},{24,28},{28,24},{1,5},{5... | collective-permute-start | bytes 2101256 | tf_op jit(solution)/shard_map/ppermute | solution.py:954
  252.2 18.7 %collective-permute-start.38 = (bf16[144,1152]{1,0:T(8,128)(2,1)S(1)}, bf16[144,1152]{1,0:T(8,128)(2,1)S(1)}, u32[]{:S(2)}, u32[]{:S(2)}) collective-permute-start(bf16[144,1152]{1,0:T(8,128)(2,1)S(1)} %shard_map.377.own), channel_id=1, source_target_pairs={{0,4},{4,0},{8,12},{12,8},{16,20},{20,16},{24,28},{28,24},{1,5},{5... | collective-permute-start | bytes 995336 | tf_op jit(solution)/shard_map/ppermute | solution.py:954
  271.5 16.5 %collective-permute-start.41 = (bf16[288,1152]{1,0:T(8,128)(2,1)S(1)}, bf16[288,1152]{1,0:T(8,128)(2,1)S(1)}, u32[]{:S(2)}, u32[]{:S(2)}) collective-permute-start(bf16[288,1152]{1,0:T(8,128)(2,1)S(1)} %shard_map.378.refs_1_), channel_id=1, source_target_pairs={{0,8},{4,12},{8,0},{12,4},{16,24},{20,28},{24,16},{28,20},{1,9},{5... | collective-permute-start | bytes 1990664 | tf_op jit(solution)/shard_map/ppermute | solution.py:954
  (39 other events, 367.8 us)

commit v2 on v1

--- a/solution.py
+++ b/solution.py
@@ -901,7 +901,7 @@
     return found[0] if single else found
 
 
-def quick(kernel, outs, inputs, deps=()):
+def quick(kernel, outs, inputs, deps=(), us=1.2):
     if deps:
         inputs = [after(inputs[0], *deps), *inputs[1:]]
     return pl.pallas_call(
@@ -910,7 +910,7 @@
         in_specs=[SMEM if given.shape == (2,) else VMEM for given in inputs],
         out_specs=jax.tree.map(lambda _: VMEM, outs),
         compiler_params=pltpu.CompilerParams(vmem_limit_bytes=4 * MIB),
-        cost_estimate=cost(1.2),
+        cost_estimate=cost(us),
     )(*inputs)
 
 
@@ -968,7 +968,7 @@
     def swap(self, place, array):
         return swap(array, "dp", 1 << self.order[place])
 
-    def split(self, deps=()):
+    def split(self, deps=(), us=1.2):
         half, columns = self.keep.shape
         part = shape_of(half // 2, columns)
         self.keep, send = quick(
@@ -976,6 +976,7 @@
             [part, part],
             [self.ranks, self.keep, self.got],
             deps,
+            us,
         )
         self.got = self.swap(1, send)
         return self.keep
@@ -1289,8 +1290,8 @@
         vmem=24,
     )
     lines_far = swap(image_rows, "mp", 2)
-    last = down.exchange([image_rows, packed_far, lines_far])
-    lines_near = swap(jnp.concatenate([image_rows, lines_far], axis=0), "mp", 1)
+    last = down.exchange([image_rows, packed_far, lines_far, up.got])
+    lines_near = swap(after(jnp.concatenate([image_rows, lines_far], axis=0), last), "mp", 1)
     packed_last = swap(after(packed_far, last), "mp", 1)
     packed_1 = swap(after(packed_1, last), "mp", 1)
     half = shape_of(group_width, width)
@@ -1317,12 +1318,12 @@
         us=5.2,
     )
     first = Total(ranks, levels, keep_first, send_first, tail_rows // 2)
-    last = first.split([keep_second])
-    second = Total(ranks, levels, keep_second, after(send_second, last), cross=True)
-    last = down.finish([last])
+    last = down.finish([keep_second])
+    last = first.split([last], 8.0)
+    second = Total(ranks, levels, keep_second, send_second, cross=True)
     last = up.exchange([last])
     out_far = swap(add_low(out_keep[1], out_got[1]), "mp", 2)
-    last = second.split([last])
+    last = second.split([last], 8.0)
     last = down.join([last])
     last = up.finish([last])
     last = first.exchange([last])

time: 294 us -> 288 us (0.980)
  starting transfers between devices: 42.4 us -> 37.5 us
    ppermute x42, starting transfers between devices: 42.4 us -> 37.5 us  [swap(): return lax.ppermute(array, axis, [(i, i ^ distance) for i in range(size)])]
  transfers between devices with their start and end apart: 42 -> 42, of which waited for: 18 -> 18; matrix products, arithmetic and copies ran while one was open for 1% -> 1% of each run, Pallas kernels for 35% -> 38%
where the time goes in v2:
time: 288 us; the launch traced here: 284 us
  waiting for transfers between devices  131 us (45%)
  Pallas kernels  111 us (39%)
  starting transfers between devices  37.5 us (13%)
    ppermute x42, waiting for transfers between devices, swap(): return lax.ppermute(array, axis, [(i, i ^ distance) for i in range(size)])  131 us
    pallas_call x16, Pallas kernels, run(): pl.pallas_call(body, out_shape=outs, in_specs=[space[kind] for kind in ki...  91.7 us
    ppermute x42, starting transfers between devices, swap(): return lax.ppermute(array, axis, [(i, i ^ distance) for i in range(size)])  37.5 us
    pallas_call x2, Pallas kernels, widen(): pl.pallas_call(partial(widen_kernel, level, cross, each), out_shape=shape...  8.67 us
    pallas_call x16, Pallas kernels, quick(): pl.pallas_call(kernel, out_shape=outs, in_specs=[SMEM if given.shape == (...  6.89 us
  transfers between devices with their start and end apart: 42, of which 18 were waited for; matrix products, arithmetic and copies ran while one was open for 1% of the time, Pallas kernels for 38%

profile of v2, /device:TPU:0, one launch (start us, length us, event | category | flops | bytes accessed | tf_op | source)
XLA Modules:
  0.0 283.8 jit_solution(12757363018941897778)
XLA Ops:
  0.7 3.0 %collective-permute-start = (bf16[256,1152]{1,0:T(8,128)(2,1)}, bf16[256,1152]{1,0:T(8,128)(2,1)S(1)}, u32[]{:S(2)}, u32[]{:S(2)}) collective-permute-start(bf16[256,1152]{1,0:T(8,128)(2,1)} %refs_3_.2), channel_id=1, source_target_pairs={{0,2},{1,3},{2,0},{3,1},{4,6},{5,7},{6,4},{7,5},{8,10},{9,11},{10,... | collective-permute-start | bytes 1769480 | tf_op jit(solution)/shard_map/ppermute | solution.py:954
  4.3 19.2 %shard_map.348 = (bf16[4,256,384]{2,1,0:T(8,128)(2,1)}, bf16[4,256,384]{2,1,0:T(8,128)(2,1)}, bf16[4,256,384]{2,1,0:T(8,128)(2,1)}, bf16[16,256,256]{2,1,0:T(8,1...) custom-call(s32[2]{0:T(128)} %pad_add_fusion.refs_0_.ranks, ...), custom_call_target="tpu_custom_call" | custom-call | flops 20700000256 | bytes 1000 | tf_op jit(solution)/shard_map/pallas_call | solution.py:892
  24.3 3.5 %shard_map.349.refs_2_ = bf16[1024,1152]{1,0:T(8,128)(2,1)S(1)} custom-call(s32[2]{0:T(128)S(1)} %copy-done.9, s32[256,256]{1,0:T(8,128)S(1)} %copy-done.7, bf16[1024,1152]{1,0:T(8,128)(2,1)S(1)} %copy-done.6, f32[1152]{0:T(1024)S(1)} %copy-done.11, f32[1152]{0:T(1024)S(1)} %copy-done.19), custom_call_target="tpu_custom_call" | custom-call | flops 1380000000 | bytes 1000 | tf_op jit(solution)/shard_map/pallas_call | solution.py:1121
  27.8 7.2 %shard_map.350 = (bf16[512,1152]{1,0:T(8,128)(2,1)S(1)}, bf16[512,1152]{1,0:T(8,128)(2,1)S(1)}, bf16[512,1152]{1,0:T(8,128)(2,1)S(1)}, bf16[256,1152]{1,0:T(8,128)(2,1)S(1)}, bf16[256,1152]{1,0:T(8,128)(2,1)S(1)}) custom-call(s32[256,256]{1,0:T(8,128)S(1)} %copy-done.7, bf16[256,1152]{1,0:T(8,128)(2,1)S(1)} %copy-done.18, ...), custom_call_target="tpu_custom_call" | custom-call | flops 2484000000 | bytes 1000 | tf_op jit(solution)/shard_map/pallas_call | solution.py:892
  35.4 4.6 %collective-permute-done.5.refs_1_.refs_3_ = bf16[256,1152]{1,0:T(8,128)(2,1)S(1)} collective-permute-done((bf16[256,1152]{1,0:T(8,128)(2,1)}, bf16[256,1152]{1,0:T(8,128)(2,1)S(1)}, u32[]{:S(2)}, u32[]{:S(2)}) %collective-permute-start.5) | collective-permute-done | bytes 589856 | tf_op jit(solution)/shard_map/ppermute | solution.py:954
  42.1 7.4 %shard_map.351 = (bf16[512,1152]{1,0:T(8,128)(2,1)S(1)}, bf16[512,1152]{1,0:T(8,128)(2,1)S(1)}, bf16[512,1152]{1,0:T(8,128)(2,1)S(1)}, bf16[256,1152]{1,0:T(8,12...) custom-call(s32[256,256]{1,0:T(8,128)S(1)} %copy-done.7, ...), custom_call_target="tpu_custom_call" | custom-call | flops 2587500032 | bytes 1000 | tf_op jit(solution)/shard_map/pallas_call | solution.py:892
  51.6 3.8 %shard_map.352 = (bf16[576,1152]{1,0:T(8,128)(2,1)S(1)}, bf16[576,1152]{1,0:T(8,128)(2,1)S(1)}) custom-call(s32[2]{0:T(128)S(1)} %copy-done.9, bf16[512,1152]{1,0:T(8,128)(2,1)S(1)} %get-tuple-element.140.refs_1_.refs_0_, bf16[512,1152]{1,0:T(8,128)(2,1)S(1)} %get-tuple-element.131.refs_2_.refs_4_, bf16[512,1152]{1,0:T(8,128)(2,1)S(1)} %get-tuple-element.132.refs_3_.refs_1_, ...), custom_call_target="tpu_custom_call" | custom-call | flops 4830000128 | bytes 1000 | tf_op jit(solution)/shard_map/pallas_call | solution.py:892
  57.8 3.9 %shard_map.354 = (bf16[576,1152]{1,0:T(8,128)(2,1)S(1)}, bf16[576,1152]{1,0:T(8,128)(2,1)S(1)}) custom-call(s32[2]{0:T(128)S(1)} %copy-done.9, bf16[256,1152]{1,0:T(8,128)(2,1)S(1)} %copy-done.18, bf16[256,1152]{1,0:T(8,128)(2,1)S(1)} %collective-permute-done.2.refs_2_, bf16[256,1152]{1,0:T(8,128)(2,1)S(1)} %collective-permute-done.5.refs_1_.refs_3_, ...), custom_call_target="tpu_custom_call" | custom-call | flops 1690499968 | bytes 1000 | tf_op jit(solution)/shard_map/pallas_call | solution.py:892
  63.9 4.0 %shard_map.355 = (bf16[2,256,1152]{2,1,0:T(8,128)(2,1)S(1)}, bf16[2,256,1152]{2,1,0:T(8,128)(2,1)S(1)}) custom-call(bf16[512,1152]{1,0:T(8,128)(2,1)S(1)} %get-tuple-element.140.refs_1_.refs_0_, bf16[512,1152]{1,0:T(8,128)(2,1)S(1)} %get-tuple-element.132.refs_3_.refs_1_, bf16[1152,1152]{1,0:T(8,128)(2,1)S(1)} %copy-done.15), custom_call_target="tpu_custom_call" | custom-call | flops 1724999936 | bytes 1000 | tf_op jit(solution)/shard_map/pallas_call | solution.py:892
  67.9 4.0 %collective-permute-done.11.refs_2_ = bf16[256,1152]{1,0:T(8,128)(2,1)S(1)} collective-permute-done((bf16[256,1152]{1,0:T(8,128)(2,1)S(1)}, bf16[256,1152]{1,0:T(8,128)(2,1)S(1)}, u32[]{:S(2)}, u32[]{:S(2)}) %collective-permute-start.11) | collective-permute-done | bytes 589856 | tf_op jit(solution)/shard_map/ppermute | solution.py:954
  74.2 10.0 %shard_map.358 = (bf16[2,288,896]{2,1,0:T(8,128)(2,1)S(1)}, bf16[3,2,256,384]{3,2,1,0:T(8,128)(2,1)S(1)}, bf16[4,256,384]{2,1,0:T(8,128)(2,1)S(1)}) custom-call(s32[2]{0:T(128)S(1)} %copy-done.9, bf16[256,1152]{1,0:T(8,128)(2,1)S(1)} %get-tuple-element.151.refs_1_.refs_7_, bf16[1152,1152]{1,0:T(8,128)(2,1)S(1)} %copy-done.16, ...), custom_call_target="tpu_custom_call" | custom-call | flops 2863500032 | bytes 1000 | tf_op jit(solution)/shard_map/pallas_call | solution.py:892
  85.7 9.0 %shard_map.359 = (bf16[288,896]{1,0:T(8,128)(2,1)S(1)}, bf16[288,896]{1,0:T(8,128)(2,1)S(1)}, bf16[3,2,256,384]{3,2,1,0:T(8,128)(2,1)S(1)}) custom-call(s32[2]{0:T(128)S(1)} %copy-done.9, bf16[4,256,384]{2,1,0:T(8,128)(2,1)S(1)} %get-tuple-element.156.refs_1_, bf16[4,256,384]{2,1,0:T(8,128)(2,1)S(1)} %copy-done.22, bf16[4,256,384]{2,1,0:T(8,128)(2,1)S(1)} %copy-done.23, ...), custom_call_target="tpu_custom_call" | custom-call | flops 2863500032 | bytes 1000 | tf_op jit(solution)/shard_map/pallas_call | solution.py:892
  99.0 8.9 %shard_map.362 = (f32[8,1152]{1,0:T(8,128)S(1)}, f32[256,1152]{1,0:T(8,128)}) custom-call(s32[2]{0:T(128)S(1)} %copy-done.9, bf16[3,2,256,384]{3,2,1,0:T(8,128)(2,1)S(1)} %get-tuple-element.167.refs_1_, bf16[3,2,256,384]{3,2,1,0:T(8,128)(2,1)S(1)} %get-tuple-element.168.refs_2_, bf16[1152,1152]{1,0:T(8,128)(2,1)S(1)} %copy-done.1, ...), custom_call_target="tpu_custom_call" | custom-call | flops 2967000064 | bytes 1000 | tf_op jit(solution)/shard_map/pallas_call | solution.py:892
  109.5 2.4 collective-permute-done.19.refs_16_
  111.9 2.3 collective-permute-done.20.right
  115.7 2.6 collective-permute-start.26
  119.0 6.1 %shard_map.364 = (bf16[304,1152]{1,0:T(8,128)(2,1)S(1)}, bf16[288,1152]{1,0:T(8,128)(2,1)S(1)}, bf16[304,1152]{1,0:T(8,128)(2,1)S(1)}, bf16[288,1152]{1,0:T(8,128)(2,1)S(1)}) custom-call(s32[2]{0:T(128)S(1)} %copy-done.9, s32[4]{0:T(128)S(1)} %copy-done.13, bf16[1024,1152]{1,0:T(8,128)(2,1)S(1)} %shard_map.349.refs_2_, ...), custom_call_target="tpu_custom_call" | custom-call | flops 1794000000 | bytes 1000 | tf_op jit(solution)/shard_map/pallas_call | solution.py:892
  126.6 21.0 %collective-permute-done.26.right = bf16[288,1152]{1,0:T(8,128)(2,1)S(1)} collective-permute-done((bf16[288,1152]{1,0:T(8,128)(2,1)S(1)}, bf16[288,1152]{1,0:T(8,128)(2,1)S(1)}, u32[]{:S(2)}, u32[]{:S(2)}) %collective-permute-start.26) | collective-permute-done | bytes 663584 | tf_op jit(solution)/shard_map/ppermute | solution.py:954
  151.0 3.4 %collective-permute-start.30 = (bf16[288,1152]{1,0:T(8,128)(2,1)S(1)}, bf16[288,1152]{1,0:T(8,128)(2,1)S(1)}, u32[]{:S(2)}, u32[]{:S(2)}) collective-permute-start(bf16[288,1152]{1,0:T(8,128)(2,1)S(1)} %shard_map.367.left), channel_id=1, source_target_pairs={{0,16},{4,20},{8,24},{12,28},{16,0},{20,4},{24,8},{28,12},{1,17},{... | collective-permute-start | bytes 1990664 | tf_op jit(solution)/shard_map/ppermute | solution.py:954
  154.5 10.7 %collective-permute-done.28.got = bf16[288,1152]{1,0:T(8,128)(2,1)S(1)} collective-permute-done((bf16[288,1152]{1,0:T(8,128)(2,1)S(1)}, bf16[288,1152]{1,0:T(8,128)(2,1)S(1)}, u32[]{:S(2)}, u32[]{:S(2)}) %collective-permute-start.28) | collective-permute-done | bytes 663584 | tf_op jit(solution)/shard_map/ppermute | solution.py:954
  165.9 9.8 %collective-permute-done.29.other = bf16[288,1152]{1,0:T(8,128)(2,1)S(1)} collective-permute-done((bf16[288,1152]{1,0:T(8,128)(2,1)S(1)}, bf16[288,1152]{1,0:T(8,128)(2,1)S(1)}, u32[]{:S(2)}, u32[]{:S(2)}) %collective-permute-start.29) | collective-permute-done | bytes 663584 | tf_op jit(solution)/shard_map/ppermute | solution.py:954
  176.4 6.9 %collective-permute-done.30.right = bf16[288,1152]{1,0:T(8,128)(2,1)S(1)} collective-permute-done((bf16[288,1152]{1,0:T(8,128)(2,1)S(1)}, bf16[288,1152]{1,0:T(8,128)(2,1)S(1)}, u32[]{:S(2)}, u32[]{:S(2)}) %collective-permute-start.30) | collective-permute-done | bytes 663584 | tf_op jit(solution)/shard_map/ppermute | solution.py:954
  186.1 20.7 %collective-permute-done.31.right = bf16[152,1152]{1,0:T(8,128)(2,1)S(1)} collective-permute-done((bf16[152,1152]{1,0:T(8,128)(2,1)S(1)}, bf16[152,1152]{1,0:T(8,128)(2,1)S(1)}, u32[]{:S(2)}, u32[]{:S(2)}) %collective-permute-start.31) | collective-permute-done | bytes 350240 | tf_op jit(solution)/shard_map/ppermute | solution.py:954
  211.1 12.3 %collective-permute-done.33.right = bf16[152,1152]{1,0:T(8,128)(2,1)S(1)} collective-permute-done((bf16[152,1152]{1,0:T(8,128)(2,1)S(1)}, bf16[152,1152]{1,0:T(8,128)(2,1)S(1)}, u32[]{:S(2)}, u32[]{:S(2)}) %collective-permute-start.33) | collective-permute-done | bytes 350240 | tf_op jit(solution)/shard_map/ppermute | solution.py:954
  223.7 3.0 %collective-permute-start.37 = (bf16[144,1152]{1,0:T(8,128)(2,1)S(1)}, bf16[144,1152]{1,0:T(8,128)(2,1)S(1)}, u32[]{:S(2)}, u32[]{:S(2)}) collective-permute-start(bf16[144,1152]{1,0:T(8,128)(2,1)S(1)} %shard_map.374.left), channel_id=1, source_target_pairs={{0,16},{4,20},{8,24},{12,28},{16,0},{20,4},{24,8},{28,12},{1,17},{... | collective-permute-start | bytes 995336 | tf_op jit(solution)/shard_map/ppermute | solution.py:954
  227.5 13.3 %collective-permute-done.35.other = bf16[152,1152]{1,0:T(8,128)(2,1)S(1)} collective-permute-done((bf16[152,1152]{1,0:T(8,128)(2,1)S(1)}, bf16[152,1152]{1,0:T(8,128)(2,1)S(1)}, u32[]{:S(2)}, u32[]{:S(2)}) %collective-permute-start.35) | collective-permute-done | bytes 350240 | tf_op jit(solution)/shard_map/ppermute | solution.py:954
  242.0 4.3 %shard_map.376 = f32[1152,1152]{1,0:T(8,128)} custom-call(s32[2]{0:T(128)S(1)} %copy-done.9, bf16[576,1152]{1,0:T(8,128)(2,1)S(1)} %shard_map.369.own, bf16[576,1152]{1,0:T(8,128)(2,1)S(1)} %collective-permute-done.36.other), custom_call_target="tpu_custom_call" | custom-call | flops 1207500032 | bytes 1000 | tf_op jit(solution)/shard_map/pallas_call | solution.py:935
  248.0 17.5 %collective-permute-done.38.other = bf16[144,1152]{1,0:T(8,128)(2,1)S(1)} collective-permute-done((bf16[144,1152]{1,0:T(8,128)(2,1)S(1)}, bf16[144,1152]{1,0:T(8,128)(2,1)S(1)}, u32[]{:S(2)}, u32[]{:S(2)}) %collective-permute-start.38) | collective-permute-done | bytes 331808 | tf_op jit(solution)/shard_map/ppermute | solution.py:954
  268.5 4.3 %shard_map.379 = f32[1152,1152]{1,0:T(8,128)} custom-call(s32[2]{0:T(128)S(1)} %copy-done.9, bf16[576,1152]{1,0:T(8,128)(2,1)S(1)} %shard_map.372.own, bf16[576,1152]{1,0:T(8,128)(2,1)S(1)} %collective-permute-done.39.other), custom_call_target="tpu_custom_call" | custom-call | flops 1207500032 | bytes 1000 | tf_op jit(solution)/shard_map/pallas_call | solution.py:935
  272.8 2.2 shard_map.380
  275.0 4.3 %shard_map.381 = (f32[288,1152]{1,0:T(8,128)}, f32[288,1152]{1,0:T(8,128)}, f32[288,1000]{1,0:T(8,128)}, f32[4,1024]{1,0:T(4,128)S(1)}, f32[16,288]{1,0:T(8,128)S(1)}) custom-call(f32[32,1152]{1,0:T(8,128)S(1)} %get-tuple-element.206.refs_0_, bf16[1000,1152]{1,0:T(8,128)(2,1)} %refs_1_.5), custom_call_target="tpu_custom_call" | custom-call | flops 862499968 | bytes 1000 | tf_op jit(solution)/shard_map/pallas_call | solution.py:892
  281.4 2.2 shard_map.382
  (148 shorter events, 44.5 us)
Async XLA Ops:
  0.7 22.8 %collective-permute-start = (bf16[256,1152]{1,0:T(8,128)(2,1)}, bf16[256,1152]{1,0:T(8,128)(2,1)S(1)}, u32[]{:S(2)}, u32[]{:S(2)}) collective-permute-start(bf16[256,1152]{1,0:T(8,128)(2,1)} %refs_3_.2), channel_id=1, source_target_pairs={{0,2},{1,3},{2,0},{3,1},{4,6},{5,7},{6,4},{7,5},{8,10},{9,11},{10,... | collective-permute-start | bytes 1769480 | tf_op jit(solution)/shard_map/ppermute | solution.py:954
  24.2 15.9 %collective-permute-start.5 = (bf16[256,1152]{1,0:T(8,128)(2,1)}, bf16[256,1152]{1,0:T(8,128)(2,1)S(1)}, u32[]{:S(2)}, u32[]{:S(2)}) collective-permute-start(bf16[256,1152]{1,0:T(8,128)(2,1)} %get-tuple-element.118.refs_1_), channel_id=1, source_target_pairs={{0,2},{1,3},{2,0},{3,1},{4,6},{5,7},{6,4},{7,5},{8,10},{9,11},{10,... | collective-permute-start | bytes 1769480 | tf_op jit(solution)/shard_map/ppermute | solution.py:954
  35.0 5.3 %collective-permute-start.4 = (bf16[256,1152]{1,0:T(8,128)(2,1)S(1)}, bf16[256,1152]{1,0:T(8,128)(2,1)S(1)}, u32[]{:S(2)}, u32[]{:S(2)}) collective-permute-start(bf16[256,1152]{1,0:T(8,128)(2,1)S(1)} %get-tuple-element.123), channel_id=1, source_target_pairs={{0,1},{1,0},{2,3},{3,2},{4,5},{5,4},{6,7},{7,6},{8,9},{9,8},{10,11... | collective-permute-start | bytes 1769480 | tf_op jit(solution)/shard_map/ppermute | solution.py:954
  40.1 11.5 %collective-permute-start.7 = (bf16[2,256,384]{2,1,0:T(8,128)(2,1)S(1)}, bf16[2,256,384]{2,1,0:T(8,128)(2,1)S(1)}, u32[]{:S(2)}, u32[]{:S(2)}) collective-permute-start(bf16[2,256,384]{2,1,0:T(8,128)(2,1)S(1)} %copy-done.25), channel_id=1, source_target_pairs={{0,2},{1,3},{2,0},{3,1},{4,6},{5,7},{6,4},{7,5},{8,10},{9,11},{10,... | collective-permute-start | bytes 1179656 | tf_op jit(solution)/shard_map/ppermute | solution.py:954
  49.5 7.5 %collective-permute-start.8 = (bf16[256,1152]{1,0:T(8,128)(2,1)S(1)}, bf16[256,1152]{1,0:T(8,128)(2,1)S(1)}, u32[]{:S(2)}, u32[]{:S(2)}) collective-permute-start(bf16[256,1152]{1,0:T(8,128)(2,1)S(1)} %get-tuple-element.136), channel_id=1, source_target_pairs={{0,1},{1,0},{2,3},{3,2},{4,5},{5,4},{6,7},{7,6},{8,9},{9,8},{10,11... | collective-permute-start | bytes 1769480 | tf_op jit(solution)/shard_map/ppermute | solution.py:954
  55.4 39.3 %collective-permute-start.15 = (bf16[576,1152]{1,0:T(8,128)(2,1)S(1)}, bf16[576,1152]{1,0:T(8,128)(2,1)S(1)}, u32[]{:S(2)}, u32[]{:S(2)}) collective-permute-start(bf16[576,1152]{1,0:T(8,128)(2,1)S(1)} %get-tuple-element.160), channel_id=1, source_target_pairs={{0,4},{4,0},{8,12},{12,8},{16,20},{20,16},{24,28},{28,24},{1,5},{5... | collective-permute-start | bytes 3981320 | tf_op jit(solution)/shard_map/ppermute | solution.py:954
  57.2 14.7 %collective-permute-start.11 = (bf16[256,1152]{1,0:T(8,128)(2,1)S(1)}, bf16[256,1152]{1,0:T(8,128)(2,1)S(1)}, u32[]{:S(2)}, u32[]{:S(2)}) collective-permute-start(bf16[256,1152]{1,0:T(8,128)(2,1)S(1)} %shard_map.353), channel_id=1, source_target_pairs={{0,2},{1,3},{2,0},{3,1},{4,6},{5,7},{6,4},{7,5},{8,10},{9,11},{10,... | collective-permute-start | bytes 1769480 | tf_op jit(solution)/shard_map/ppermute | solution.py:954
  61.7 34.1 %collective-permute-start.16 = (bf16[576,1152]{1,0:T(8,128)(2,1)S(1)}, bf16[576,1152]{1,0:T(8,128)(2,1)S(1)}, u32[]{:S(2)}, u32[]{:S(2)}) collective-permute-start(bf16[576,1152]{1,0:T(8,128)(2,1)S(1)} %get-tuple-element.163), channel_id=1, source_target_pairs={{0,8},{4,12},{8,0},{12,4},{16,24},{20,28},{24,16},{28,20},{1,9},{5... | collective-permute-start | bytes 3981320 | tf_op jit(solution)/shard_map/ppermute | solution.py:954
  63.3 10.8 %collective-permute-start.12 = (bf16[2,256,384]{2,1,0:T(8,128)(2,1)S(1)}, bf16[2,256,384]{2,1,0:T(8,128)(2,1)S(1)}, u32[]{:S(2)}, u32[]{:S(2)}) collective-permute-start(bf16[2,256,384]{2,1,0:T(8,128)(2,1)S(1)} %collective-permute-done.7.refs_13_), channel_id=1, source_target_pairs={{0,1},{1,0},{2,3},{3,2},{4,5},{5,4},{6,7},{7,6},{8,9},{9,8},{10,11... | collective-permute-start | bytes 1179656 | tf_op jit(solution)/shard_map/ppermute | solution.py:954
  63.3 10.8 %collective-permute-start.13 = (bf16[256,384]{1,0:T(8,128)(2,1)S(1)}, bf16[256,384]{1,0:T(8,128)(2,1)S(1)}, u32[]{:S(2)}, u32[]{:S(2)}) collective-permute-start(bf16[256,384]{1,0:T(8,128)(2,1)S(1)} %copy-done.26), channel_id=1, source_target_pairs={{0,1},{1,0},{2,3},{3,2},{4,5},{5,4},{6,7},{7,6},{8,9},{9,8},{10,11... | collective-permute-start | bytes 589832 | tf_op jit(solution)/shard_map/ppermute | solution.py:954
  73.5 21.2 %collective-permute-start.14 = (bf16[256,1152]{1,0:T(8,128)(2,1)S(1)}, bf16[256,1152]{1,0:T(8,128)(2,1)S(1)}, u32[]{:S(2)}, u32[]{:S(2)}) collective-permute-start(bf16[256,1152]{1,0:T(8,128)(2,1)S(1)} %get-tuple-element.151.refs_1_.refs_7_), channel_id=1, source_target_pairs={{0,2},{1,3},{2,0},{3,1},{4,6},{5,7},{6,4},{7,5},{8,10},{9,11},{10,... | collective-permute-start | bytes 1769480 | tf_op jit(solution)/shard_map/ppermute | solution.py:954
  84.2 25.3 %collective-permute-start.18 = (bf16[2,288,896]{2,1,0:T(8,128)(2,1)S(1)}, bf16[2,288,896]{2,1,0:T(8,128)(2,1)S(1)}, u32[]{:S(2)}, u32[]{:S(2)}) collective-permute-start(bf16[2,288,896]{2,1,0:T(8,128)(2,1)S(1)} %get-tuple-element.172), channel_id=1, source_target_pairs={{0,2},{1,3},{2,0},{3,1},{4,6},{5,7},{6,4},{7,5},{8,10},{9,11},{10,... | collective-permute-start | bytes 3096584 | tf_op jit(solution)/shard_map/ppermute | solution.py:954
  96.8 17.4 %collective-permute-start.20 = (bf16[288,1152]{1,0:T(8,128)(2,1)S(1)}, bf16[288,1152]{1,0:T(8,128)(2,1)S(1)}, u32[]{:S(2)}, u32[]{:S(2)}) collective-permute-start(bf16[288,1152]{1,0:T(8,128)(2,1)S(1)} %get-tuple-element.173), channel_id=1, source_target_pairs={{0,4},{4,0},{8,12},{12,8},{16,20},{20,16},{24,28},{28,24},{1,5},{5... | collective-permute-start | bytes 1990664 | tf_op jit(solution)/shard_map/ppermute | solution.py:954
  97.4 17.0 %collective-permute-start.21 = (bf16[288,1152]{1,0:T(8,128)(2,1)S(1)}, bf16[288,1152]{1,0:T(8,128)(2,1)S(1)}, u32[]{:S(2)}, u32[]{:S(2)}) collective-permute-start(bf16[288,1152]{1,0:T(8,128)(2,1)S(1)} %get-tuple-element.175), channel_id=1, source_target_pairs={{0,8},{4,12},{8,0},{12,4},{16,24},{20,28},{24,16},{28,20},{1,9},{5... | collective-permute-start | bytes 1990664 | tf_op jit(solution)/shard_map/ppermute | solution.py:954
  115.7 32.0 %collective-permute-start.26 = (bf16[288,1152]{1,0:T(8,128)(2,1)S(1)}, bf16[288,1152]{1,0:T(8,128)(2,1)S(1)}, u32[]{:S(2)}, u32[]{:S(2)}) collective-permute-start(bf16[288,1152]{1,0:T(8,128)(2,1)S(1)} %shard_map.363.left), channel_id=1, source_target_pairs={{0,16},{4,20},{8,24},{12,28},{16,0},{20,4},{24,8},{28,12},{1,17},{... | collective-permute-start | bytes 1990664 | tf_op jit(solution)/shard_map/ppermute | solution.py:954
  125.1 25.0 %collective-permute-start.27 = (bf16[304,1152]{1,0:T(8,128)(2,1)S(1)}, bf16[304,1152]{1,0:T(8,128)(2,1)S(1)}, u32[]{:S(2)}, u32[]{:S(2)}) collective-permute-start(bf16[304,1152]{1,0:T(8,128)(2,1)S(1)} %get-tuple-element.186), channel_id=1, source_target_pairs={{0,4},{4,0},{8,12},{12,8},{16,20},{20,16},{24,28},{28,24},{1,5},{5... | collective-permute-start | bytes 2101256 | tf_op jit(solution)/shard_map/ppermute | solution.py:954
  147.9 27.9 %collective-permute-start.29 = (bf16[288,1152]{1,0:T(8,128)(2,1)S(1)}, bf16[288,1152]{1,0:T(8,128)(2,1)S(1)}, u32[]{:S(2)}, u32[]{:S(2)}) collective-permute-start(bf16[288,1152]{1,0:T(8,128)(2,1)S(1)} %shard_map.365.own), channel_id=1, source_target_pairs={{0,8},{4,12},{8,0},{12,4},{16,24},{20,28},{24,16},{28,20},{1,9},{5... | collective-permute-start | bytes 1990664 | tf_op jit(solution)/shard_map/ppermute | solution.py:954
  148.6 16.6 %collective-permute-start.28 = (bf16[288,1152]{1,0:T(8,128)(2,1)S(1)}, bf16[288,1152]{1,0:T(8,128)(2,1)S(1)}, u32[]{:S(2)}, u32[]{:S(2)}) collective-permute-start(bf16[288,1152]{1,0:T(8,128)(2,1)S(1)} %get-tuple-element.190), channel_id=1, source_target_pairs={{0,4},{4,0},{8,12},{12,8},{16,20},{20,16},{24,28},{28,24},{1,5},{5... | collective-permute-start | bytes 1990664 | tf_op jit(solution)/shard_map/ppermute | solution.py:954
  151.0 32.3 %collective-permute-start.30 = (bf16[288,1152]{1,0:T(8,128)(2,1)S(1)}, bf16[288,1152]{1,0:T(8,128)(2,1)S(1)}, u32[]{:S(2)}, u32[]{:S(2)}) collective-permute-start(bf16[288,1152]{1,0:T(8,128)(2,1)S(1)} %shard_map.367.left), channel_id=1, source_target_pairs={{0,16},{4,20},{8,24},{12,28},{16,0},{20,4},{24,8},{28,12},{1,17},{... | collective-permute-start | bytes 1990664 | tf_op jit(solution)/shard_map/ppermute | solution.py:954
  154.5 72.2 %collective-permute-start.9 = (bf16[2,256,1152]{2,1,0:T(8,128)(2,1)S(1)}, bf16[2,256,1152]{2,1,0:T(8,128)(2,1)S(1)}, u32[]{:S(2)}, u32[]{:S(2)}) collective-permute-start(bf16[2,256,1152]{2,1,0:T(8,128)(2,1)S(1)} %get-tuple-element.142), channel_id=1, source_target_pairs={{0,1},{1,0},{2,3},{3,2},{4,5},{5,4},{6,7},{7,6},{8,9},{9,8},{10,11... | collective-permute-start | bytes 3538952 | tf_op jit(solution)/shard_map/ppermute | solution.py:954
  183.5 26.5 %collective-permute-start.32 = (bf16[288,1152]{1,0:T(8,128)(2,1)S(1)}, bf16[288,1152]{1,0:T(8,128)(2,1)S(1)}, u32[]{:S(2)}, u32[]{:S(2)}) collective-permute-start(bf16[288,1152]{1,0:T(8,128)(2,1)S(1)} %shard_map.370.own), channel_id=1, source_target_pairs={{0,8},{4,12},{8,0},{12,4},{16,24},{20,28},{24,16},{28,20},{1,9},{5... | collective-permute-start | bytes 1990664 | tf_op jit(solution)/shard_map/ppermute | solution.py:954
  183.5 23.2 %collective-permute-start.31 = (bf16[152,1152]{1,0:T(8,128)(2,1)S(1)}, bf16[152,1152]{1,0:T(8,128)(2,1)S(1)}, u32[]{:S(2)}, u32[]{:S(2)}) collective-permute-start(bf16[152,1152]{1,0:T(8,128)(2,1)S(1)} %get-tuple-element.195), channel_id=1, source_target_pairs={{0,8},{4,12},{8,0},{12,4},{16,24},{20,28},{24,16},{28,20},{1,9},{5... | collective-permute-start | bytes 1050632 | tf_op jit(solution)/shard_map/ppermute | solution.py:954
  185.5 56.4 %collective-permute-start.36 = (bf16[576,1152]{1,0:T(8,128)(2,1)S(1)}, bf16[576,1152]{1,0:T(8,128)(2,1)S(1)}, u32[]{:S(2)}, u32[]{:S(2)}) collective-permute-start(bf16[576,1152]{1,0:T(8,128)(2,1)S(1)} %shard_map.369.own), channel_id=1, source_target_pairs={{0,4},{4,0},{8,12},{12,8},{16,20},{20,16},{24,28},{28,24},{1,5},{5... | collective-permute-start | bytes 3981320 | tf_op jit(solution)/shard_map/ppermute | solution.py:954
  206.8 16.6 %collective-permute-start.33 = (bf16[152,1152]{1,0:T(8,128)(2,1)S(1)}, bf16[152,1152]{1,0:T(8,128)(2,1)S(1)}, u32[]{:S(2)}, u32[]{:S(2)}) collective-permute-start(bf16[152,1152]{1,0:T(8,128)(2,1)S(1)} %shard_map.371.left), channel_id=1, source_target_pairs={{0,16},{4,20},{8,24},{12,28},{16,0},{20,4},{24,8},{28,12},{1,17},{... | collective-permute-start | bytes 1050632 | tf_op jit(solution)/shard_map/ppermute | solution.py:954
  208.2 15.4 %collective-permute-start.34 = (bf16[144,1152]{1,0:T(8,128)(2,1)S(1)}, bf16[144,1152]{1,0:T(8,128)(2,1)S(1)}, u32[]{:S(2)}, u32[]{:S(2)}) collective-permute-start(bf16[144,1152]{1,0:T(8,128)(2,1)S(1)} %get-tuple-element.199), channel_id=1, source_target_pairs={{0,8},{4,12},{8,0},{12,4},{16,24},{20,28},{24,16},{28,20},{1,9},{5... | collective-permute-start | bytes 995336 | tf_op jit(solution)/shard_map/ppermute | solution.py:954
  210.6 57.9 %collective-permute-start.39 = (bf16[576,1152]{1,0:T(8,128)(2,1)S(1)}, bf16[576,1152]{1,0:T(8,128)(2,1)S(1)}, u32[]{:S(2)}, u32[]{:S(2)}) collective-permute-start(bf16[576,1152]{1,0:T(8,128)(2,1)S(1)} %shard_map.372.own), channel_id=1, source_target_pairs={{0,4},{4,0},{8,12},{12,8},{16,20},{20,16},{24,28},{28,24},{1,5},{5... | collective-permute-start | bytes 3981320 | tf_op jit(solution)/shard_map/ppermute | solution.py:954
  223.5 17.3 %collective-permute-start.35 = (bf16[152,1152]{1,0:T(8,128)(2,1)S(1)}, bf16[152,1152]{1,0:T(8,128)(2,1)S(1)}, u32[]{:S(2)}, u32[]{:S(2)}) collective-permute-start(bf16[152,1152]{1,0:T(8,128)(2,1)S(1)} %shard_map.373.own), channel_id=1, source_target_pairs={{0,8},{4,12},{8,0},{12,4},{16,24},{20,28},{24,16},{28,20},{1,9},{5... | collective-permute-start | bytes 1050632 | tf_op jit(solution)/shard_map/ppermute | solution.py:954
  223.7 22.6 %collective-permute-start.37 = (bf16[144,1152]{1,0:T(8,128)(2,1)S(1)}, bf16[144,1152]{1,0:T(8,128)(2,1)S(1)}, u32[]{:S(2)}, u32[]{:S(2)}) collective-permute-start(bf16[144,1152]{1,0:T(8,128)(2,1)S(1)} %shard_map.374.left), channel_id=1, source_target_pairs={{0,16},{4,20},{8,24},{12,28},{16,0},{20,4},{24,8},{28,12},{1,17},{... | collective-permute-start | bytes 995336 | tf_op jit(solution)/shard_map/ppermute | solution.py:954
  226.9 39.6 %collective-permute-start.10 = (bf16[256,1152]{1,0:T(8,128)(2,1)S(1)}, bf16[256,1152]{1,0:T(8,128)(2,1)S(1)}, u32[]{:S(2)}, u32[]{:S(2)}) collective-permute-start(bf16[256,1152]{1,0:T(8,128)(2,1)S(1)} %fusion), channel_id=1, source_target_pairs={{0,2},{1,3},{2,0},{3,1},{4,6},{5,7},{6,4},{7,5},{8,10},{9,11},{10,... | collective-permute-start | bytes 1769480 | tf_op jit(solution)/shard_map/ppermute | solution.py:954
  241.4 31.5 %collective-permute-start.40 = (bf16[304,1152]{1,0:T(8,128)(2,1)S(1)}, bf16[304,1152]{1,0:T(8,128)(2,1)S(1)}, u32[]{:S(2)}, u32[]{:S(2)}) collective-permute-start(bf16[304,1152]{1,0:T(8,128)(2,1)S(1)} %shard_map.375.refs_1_), channel_id=1, source_target_pairs={{0,4},{4,0},{8,12},{12,8},{16,20},{20,16},{24,28},{28,24},{1,5},{5... | collective-permute-start | bytes 2101256 | tf_op jit(solution)/shard_map/ppermute | solution.py:954
  246.4 19.1 %collective-permute-start.38 = (bf16[144,1152]{1,0:T(8,128)(2,1)S(1)}, bf16[144,1152]{1,0:T(8,128)(2,1)S(1)}, u32[]{:S(2)}, u32[]{:S(2)}) collective-permute-start(bf16[144,1152]{1,0:T(8,128)(2,1)S(1)} %shard_map.377.own), channel_id=1, source_target_pairs={{0,4},{4,0},{8,12},{12,8},{16,20},{20,16},{24,28},{28,24},{1,5},{5... | collective-permute-start | bytes 995336 | tf_op jit(solution)/shard_map/ppermute | solution.py:954
  266.1 15.3 %collective-permute-start.41 = (bf16[288,1152]{1,0:T(8,128)(2,1)S(1)}, bf16[288,1152]{1,0:T(8,128)(2,1)S(1)}, u32[]{:S(2)}, u32[]{:S(2)}) collective-permute-start(bf16[288,1152]{1,0:T(8,128)(2,1)S(1)} %shard_map.378.refs_1_), channel_id=1, source_target_pairs={{0,8},{4,12},{8,0},{12,4},{16,24},{20,28},{24,16},{28,20},{1,9},{5... | collective-permute-start | bytes 1990664 | tf_op jit(solution)/shard_map/ppermute | solution.py:954
  (37 other events, 366.2 us)

commit v3 on v2

--- a/solution.py
+++ b/solution.py
@@ -728,6 +728,13 @@
     low_ref[...] = low[:body]
     low_ref.send()
     high_ref[...] = high[:body]
+
+
+def widen_plain_kernel(level, ranks, own, other, low_ref, high_ref):
+    bit = (ranks[1] >> level) & 1
+    low_ref[...] = jnp.where(bit == 0, own[...], other[...]).astype(F32)
+    low_ref.send()
+    high_ref[...] = jnp.where(bit == 0, other[...], own[...]).astype(F32)
 
 
 def widen_cross_kernel(level, ranks, own, other, low_ref, high_ref):
@@ -1320,19 +1327,20 @@
     first = Total(ranks, levels, keep_first, send_first, tail_rows // 2)
     last = down.finish([keep_second])
     last = first.split([last], 8.0)
-    second = Total(ranks, levels, keep_second, send_second, cross=True)
+    second = Total(ranks, levels, keep_second, send_second)
     last = up.exchange([last])
     out_far = swap(add_low(out_keep[1], out_got[1]), "mp", 2)
     last = second.split([last], 8.0)
     last = down.join([last])
+    last = first.exchange([last])
     last = up.finish([last])
-    last = first.exchange([last])
     last = up.join([last])
     last = first.finish([last])
     last = second.exchange([last])
     last = first.join([last])
     down_grad = widen(ranks, levels[0], down.keep, down.got, last)
-    last = second.finish([down_grad])
+    last = down_grad
+    last = second.finish([last])
     last = second.join([last])
     up_grad = widen(ranks, other_order[1], up.keep, up.got, last, cross=True)
     wide = shape_of(group_width, width, dtype=F32)
@@ -1345,7 +1353,7 @@
         deps=[up_grad],
     )
     value_grad, out_grad = run(
-        partial(widen_cross_kernel, levels[1]),
+        partial(widen_plain_kernel, levels[0]),
         [wide, wide],
         [ranks, second.keep, second.got],
         "svv",

time: 288 us -> 281 us (0.976)
  waiting for transfers between devices: 131 us -> 123 us
    ppermute x42, waiting for transfers between devices: 131 us -> 123 us  [swap(): return lax.ppermute(array, axis, [(i, i ^ distance) for i in range(size)])]
  transfers between devices with their start and end apart: 42 -> 42, of which waited for: 18 -> 19; matrix products, arithmetic and copies ran while one was open for 1% -> 1% of each run, Pallas kernels for 38% -> 39%
where the time goes in v3:
time: 281 us; the launch traced here: 278 us
  waiting for transfers between devices  123 us (44%)
  Pallas kernels  111 us (40%)
  starting transfers between devices  39.3 us (14%)
    ppermute x42, waiting for transfers between devices, swap(): return lax.ppermute(array, axis, [(i, i ^ distance) for i in range(size)])  123 us
    pallas_call x16, Pallas kernels, run(): pl.pallas_call(body, out_shape=outs, in_specs=[space[kind] for kind in ki...  91.7 us
    ppermute x42, starting transfers between devices, swap(): return lax.ppermute(array, axis, [(i, i ^ distance) for i in range(size)])  39.3 us
    pallas_call x2, Pallas kernels, widen(): pl.pallas_call(partial(widen_kernel, level, cross, each), out_shape=shape...  8.67 us
    pallas_call x16, Pallas kernels, quick(): pl.pallas_call(kernel, out_shape=outs, in_specs=[SMEM if given.shape == (...  6.89 us
  transfers between devices with their start and end apart: 42, of which 19 were waited for; matrix products, arithmetic and copies ran while one was open for 1% of the time, Pallas kernels for 39%

profile of v3, /device:TPU:0, one launch (start us, length us, event | category | flops | bytes accessed | tf_op | source)
XLA Modules:
  0.0 277.5 jit_solution(2418067432060995965)
XLA Ops:
  0.7 3.0 %collective-permute-start = (bf16[256,1152]{1,0:T(8,128)(2,1)}, bf16[256,1152]{1,0:T(8,128)(2,1)S(1)}, u32[]{:S(2)}, u32[]{:S(2)}) collective-permute-start(bf16[256,1152]{1,0:T(8,128)(2,1)} %refs_3_.2), channel_id=1, source_target_pairs={{0,2},{1,3},{2,0},{3,1},{4,6},{5,7},{6,4},{7,5},{8,10},{9,11},{10,... | collective-permute-start | bytes 1769480 | tf_op jit(solution)/shard_map/ppermute | solution.py:961
  4.3 19.2 %shard_map.348 = (bf16[4,256,384]{2,1,0:T(8,128)(2,1)}, bf16[4,256,384]{2,1,0:T(8,128)(2,1)}, bf16[4,256,384]{2,1,0:T(8,128)(2,1)}, bf16[16,256,256]{2,1,0:T(8,1...) custom-call(s32[2]{0:T(128)} %pad_add_fusion.refs_0_.ranks, ...), custom_call_target="tpu_custom_call" | custom-call | flops 20700000256 | bytes 1000 | tf_op jit(solution)/shard_map/pallas_call | solution.py:899
  24.3 3.5 %shard_map.349.refs_2_ = bf16[1024,1152]{1,0:T(8,128)(2,1)S(1)} custom-call(s32[2]{0:T(128)S(1)} %copy-done.9, s32[256,256]{1,0:T(8,128)S(1)} %copy-done.7, bf16[1024,1152]{1,0:T(8,128)(2,1)S(1)} %copy-done.6, f32[1152]{0:T(1024)S(1)} %copy-done.11, f32[1152]{0:T(1024)S(1)} %copy-done.19), custom_call_target="tpu_custom_call" | custom-call | flops 1380000000 | bytes 1000 | tf_op jit(solution)/shard_map/pallas_call | solution.py:1128
  27.8 7.2 %shard_map.350 = (bf16[512,1152]{1,0:T(8,128)(2,1)S(1)}, bf16[512,1152]{1,0:T(8,128)(2,1)S(1)}, bf16[512,1152]{1,0:T(8,128)(2,1)S(1)}, bf16[256,1152]{1,0:T(8,128)(2,1)S(1)}, bf16[256,1152]{1,0:T(8,128)(2,1)S(1)}) custom-call(s32[256,256]{1,0:T(8,128)S(1)} %copy-done.7, bf16[256,1152]{1,0:T(8,128)(2,1)S(1)} %copy-done.18, ...), custom_call_target="tpu_custom_call" | custom-call | flops 2484000000 | bytes 1000 | tf_op jit(solution)/shard_map/pallas_call | solution.py:899
  35.4 4.6 %collective-permute-done.5.refs_1_.refs_3_ = bf16[256,1152]{1,0:T(8,128)(2,1)S(1)} collective-permute-done((bf16[256,1152]{1,0:T(8,128)(2,1)}, bf16[256,1152]{1,0:T(8,128)(2,1)S(1)}, u32[]{:S(2)}, u32[]{:S(2)}) %collective-permute-start.5) | collective-permute-done | bytes 589856 | tf_op jit(solution)/shard_map/ppermute | solution.py:961
  42.1 7.4 %shard_map.351 = (bf16[512,1152]{1,0:T(8,128)(2,1)S(1)}, bf16[512,1152]{1,0:T(8,128)(2,1)S(1)}, bf16[512,1152]{1,0:T(8,128)(2,1)S(1)}, bf16[256,1152]{1,0:T(8,12...) custom-call(s32[256,256]{1,0:T(8,128)S(1)} %copy-done.7, ...), custom_call_target="tpu_custom_call" | custom-call | flops 2587500032 | bytes 1000 | tf_op jit(solution)/shard_map/pallas_call | solution.py:899
  51.6 3.8 %shard_map.352 = (bf16[576,1152]{1,0:T(8,128)(2,1)S(1)}, bf16[576,1152]{1,0:T(8,128)(2,1)S(1)}) custom-call(s32[2]{0:T(128)S(1)} %copy-done.9, bf16[512,1152]{1,0:T(8,128)(2,1)S(1)} %get-tuple-element.140.refs_1_.refs_0_, bf16[512,1152]{1,0:T(8,128)(2,1)S(1)} %get-tuple-element.131.refs_2_.refs_4_, bf16[512,1152]{1,0:T(8,128)(2,1)S(1)} %get-tuple-element.132.refs_3_.refs_1_, ...), custom_call_target="tpu_custom_call" | custom-call | flops 4830000128 | bytes 1000 | tf_op jit(solution)/shard_map/pallas_call | solution.py:899
  57.8 3.9 %shard_map.354 = (bf16[576,1152]{1,0:T(8,128)(2,1)S(1)}, bf16[576,1152]{1,0:T(8,128)(2,1)S(1)}) custom-call(s32[2]{0:T(128)S(1)} %copy-done.9, bf16[256,1152]{1,0:T(8,128)(2,1)S(1)} %copy-done.18, bf16[256,1152]{1,0:T(8,128)(2,1)S(1)} %collective-permute-done.2.refs_2_, bf16[256,1152]{1,0:T(8,128)(2,1)S(1)} %collective-permute-done.5.refs_1_.refs_3_, ...), custom_call_target="tpu_custom_call" | custom-call | flops 1690499968 | bytes 1000 | tf_op jit(solution)/shard_map/pallas_call | solution.py:899
  63.9 4.0 %shard_map.355 = (bf16[2,256,1152]{2,1,0:T(8,128)(2,1)S(1)}, bf16[2,256,1152]{2,1,0:T(8,128)(2,1)S(1)}) custom-call(bf16[512,1152]{1,0:T(8,128)(2,1)S(1)} %get-tuple-element.140.refs_1_.refs_0_, bf16[512,1152]{1,0:T(8,128)(2,1)S(1)} %get-tuple-element.132.refs_3_.refs_1_, bf16[1152,1152]{1,0:T(8,128)(2,1)S(1)} %copy-done.15), custom_call_target="tpu_custom_call" | custom-call | flops 1724999936 | bytes 1000 | tf_op jit(solution)/shard_map/pallas_call | solution.py:899
  67.9 4.0 %collective-permute-done.11.refs_2_ = bf16[256,1152]{1,0:T(8,128)(2,1)S(1)} collective-permute-done((bf16[256,1152]{1,0:T(8,128)(2,1)S(1)}, bf16[256,1152]{1,0:T(8,128)(2,1)S(1)}, u32[]{:S(2)}, u32[]{:S(2)}) %collective-permute-start.11) | collective-permute-done | bytes 589856 | tf_op jit(solution)/shard_map/ppermute | solution.py:961
  74.2 10.0 %shard_map.358 = (bf16[2,288,896]{2,1,0:T(8,128)(2,1)S(1)}, bf16[3,2,256,384]{3,2,1,0:T(8,128)(2,1)S(1)}, bf16[4,256,384]{2,1,0:T(8,128)(2,1)S(1)}) custom-call(s32[2]{0:T(128)S(1)} %copy-done.9, bf16[256,1152]{1,0:T(8,128)(2,1)S(1)} %get-tuple-element.151.refs_1_.refs_7_, bf16[1152,1152]{1,0:T(8,128)(2,1)S(1)} %copy-done.16, ...), custom_call_target="tpu_custom_call" | custom-call | flops 2863500032 | bytes 1000 | tf_op jit(solution)/shard_map/pallas_call | solution.py:899
  85.7 9.0 %shard_map.359 = (bf16[288,896]{1,0:T(8,128)(2,1)S(1)}, bf16[288,896]{1,0:T(8,128)(2,1)S(1)}, bf16[3,2,256,384]{3,2,1,0:T(8,128)(2,1)S(1)}) custom-call(s32[2]{0:T(128)S(1)} %copy-done.9, bf16[4,256,384]{2,1,0:T(8,128)(2,1)S(1)} %get-tuple-element.156.refs_1_, bf16[4,256,384]{2,1,0:T(8,128)(2,1)S(1)} %copy-done.22, bf16[4,256,384]{2,1,0:T(8,128)(2,1)S(1)} %copy-done.23, ...), custom_call_target="tpu_custom_call" | custom-call | flops 2863500032 | bytes 1000 | tf_op jit(solution)/shard_map/pallas_call | solution.py:899
  99.0 8.9 %shard_map.362 = (f32[8,1152]{1,0:T(8,128)S(1)}, f32[256,1152]{1,0:T(8,128)}) custom-call(s32[2]{0:T(128)S(1)} %copy-done.9, bf16[3,2,256,384]{3,2,1,0:T(8,128)(2,1)S(1)} %get-tuple-element.167.refs_1_, bf16[3,2,256,384]{3,2,1,0:T(8,128)(2,1)S(1)} %get-tuple-element.168.refs_2_, bf16[1152,1152]{1,0:T(8,128)(2,1)S(1)} %copy-done.1, ...), custom_call_target="tpu_custom_call" | custom-call | flops 2967000064 | bytes 1000 | tf_op jit(solution)/shard_map/pallas_call | solution.py:899
  109.5 2.4 collective-permute-done.19.refs_16_
  115.7 2.6 collective-permute-start.26
  119.0 6.1 %shard_map.364 = (bf16[304,1152]{1,0:T(8,128)(2,1)S(1)}, bf16[288,1152]{1,0:T(8,128)(2,1)S(1)}, bf16[304,1152]{1,0:T(8,128)(2,1)S(1)}, bf16[288,1152]{1,0:T(8,128)(2,1)S(1)}) custom-call(s32[2]{0:T(128)S(1)} %copy-done.9, s32[4]{0:T(128)S(1)} %copy-done.13, bf16[1024,1152]{1,0:T(8,128)(2,1)S(1)} %shard_map.349.refs_2_, ...), custom_call_target="tpu_custom_call" | custom-call | flops 1794000000 | bytes 1000 | tf_op jit(solution)/shard_map/pallas_call | solution.py:899
  127.2 20.5 %collective-permute-done.26.right = bf16[288,1152]{1,0:T(8,128)(2,1)S(1)} collective-permute-done((bf16[288,1152]{1,0:T(8,128)(2,1)S(1)}, bf16[288,1152]{1,0:T(8,128)(2,1)S(1)}, u32[]{:S(2)}, u32[]{:S(2)}) %collective-permute-start.26) | collective-permute-done | bytes 663584 | tf_op jit(solution)/shard_map/ppermute | solution.py:961
  149.5 3.4 %collective-permute-start.31 = (bf16[288,1152]{1,0:T(8,128)(2,1)S(1)}, bf16[288,1152]{1,0:T(8,128)(2,1)S(1)}, u32[]{:S(2)}, u32[]{:S(2)}) collective-permute-start(bf16[288,1152]{1,0:T(8,128)(2,1)S(1)} %shard_map.367.left), channel_id=1, source_target_pairs={{0,16},{4,20},{8,24},{12,28},{16,0},{20,4},{24,8},{28,12},{1,17},{... | collective-permute-start | bytes 1990664 | tf_op jit(solution)/shard_map/ppermute | solution.py:961
  153.0 4.1 %collective-permute-done.28.got = bf16[288,1152]{1,0:T(8,128)(2,1)S(1)} collective-permute-done((bf16[288,1152]{1,0:T(8,128)(2,1)S(1)}, bf16[288,1152]{1,0:T(8,128)(2,1)S(1)}, u32[]{:S(2)}, u32[]{:S(2)}) %collective-permute-start.28) | collective-permute-done | bytes 663584 | tf_op jit(solution)/shard_map/ppermute | solution.py:961
  157.8 20.9 %collective-permute-done.29.other = bf16[288,1152]{1,0:T(8,128)(2,1)S(1)} collective-permute-done((bf16[288,1152]{1,0:T(8,128)(2,1)S(1)}, bf16[288,1152]{1,0:T(8,128)(2,1)S(1)}, u32[]{:S(2)}, u32[]{:S(2)}) %collective-permute-start.29) | collective-permute-done | bytes 663584 | tf_op jit(solution)/shard_map/ppermute | solution.py:961
  179.4 6.3 %collective-permute-done.30.right = bf16[152,1152]{1,0:T(8,128)(2,1)S(1)} collective-permute-done((bf16[152,1152]{1,0:T(8,128)(2,1)S(1)}, bf16[152,1152]{1,0:T(8,128)(2,1)S(1)}, u32[]{:S(2)}, u32[]{:S(2)}) %collective-permute-start.30) | collective-permute-done | bytes 350240 | tf_op jit(solution)/shard_map/ppermute | solution.py:961
  189.0 3.3 %collective-permute-start.33 = (bf16[152,1152]{1,0:T(8,128)(2,1)S(1)}, bf16[152,1152]{1,0:T(8,128)(2,1)S(1)}, u32[]{:S(2)}, u32[]{:S(2)}) collective-permute-start(bf16[152,1152]{1,0:T(8,128)(2,1)S(1)} %shard_map.370.left), channel_id=1, source_target_pairs={{0,16},{4,20},{8,24},{12,28},{16,0},{20,4},{24,8},{28,12},{1,17},{... | collective-permute-start | bytes 1050632 | tf_op jit(solution)/shard_map/ppermute | solution.py:961
  192.7 18.7 %collective-permute-done.32.other = bf16[288,1152]{1,0:T(8,128)(2,1)S(1)} collective-permute-done((bf16[288,1152]{1,0:T(8,128)(2,1)S(1)}, bf16[288,1152]{1,0:T(8,128)(2,1)S(1)}, u32[]{:S(2)}, u32[]{:S(2)}) %collective-permute-start.32) | collective-permute-done | bytes 663584 | tf_op jit(solution)/shard_map/ppermute | solution.py:961
  214.7 3.8 %collective-permute-done.34.right = bf16[144,1152]{1,0:T(8,128)(2,1)S(1)} collective-permute-done((bf16[144,1152]{1,0:T(8,128)(2,1)S(1)}, bf16[144,1152]{1,0:T(8,128)(2,1)S(1)}, u32[]{:S(2)}, u32[]{:S(2)}) %collective-permute-start.34) | collective-permute-done | bytes 331808 | tf_op jit(solution)/shard_map/ppermute | solution.py:961
  218.6 3.2 %collective-permute-start.37 = (bf16[144,1152]{1,0:T(8,128)(2,1)S(1)}, bf16[144,1152]{1,0:T(8,128)(2,1)S(1)}, u32[]{:S(2)}, u32[]{:S(2)}) collective-permute-start(bf16[144,1152]{1,0:T(8,128)(2,1)S(1)} %shard_map.374.left), channel_id=1, source_target_pairs={{0,16},{4,20},{8,24},{12,28},{16,0},{20,4},{24,8},{28,12},{1,17},{... | collective-permute-start | bytes 995336 | tf_op jit(solution)/shard_map/ppermute | solution.py:961
  222.6 8.4 %collective-permute-done.35.other = bf16[152,1152]{1,0:T(8,128)(2,1)S(1)} collective-permute-done((bf16[152,1152]{1,0:T(8,128)(2,1)S(1)}, bf16[152,1152]{1,0:T(8,128)(2,1)S(1)}, u32[]{:S(2)}, u32[]{:S(2)}) %collective-permute-start.35) | collective-permute-done | bytes 350240 | tf_op jit(solution)/shard_map/ppermute | solution.py:961
  233.2 4.3 %shard_map.376 = f32[1152,1152]{1,0:T(8,128)} custom-call(s32[2]{0:T(128)S(1)} %copy-done.9, bf16[576,1152]{1,0:T(8,128)(2,1)S(1)} %shard_map.369.own, bf16[576,1152]{1,0:T(8,128)(2,1)S(1)} %collective-permute-done.36.other), custom_call_target="tpu_custom_call" | custom-call | flops 1207500032 | bytes 1000 | tf_op jit(solution)/shard_map/pallas_call | solution.py:942
  237.7 7.4 %collective-permute-done.38.other = bf16[144,1152]{1,0:T(8,128)(2,1)S(1)} collective-permute-done((bf16[144,1152]{1,0:T(8,128)(2,1)S(1)}, bf16[144,1152]{1,0:T(8,128)(2,1)S(1)}, u32[]{:S(2)}, u32[]{:S(2)}) %collective-permute-start.38) | collective-permute-done | bytes 331808 | tf_op jit(solution)/shard_map/ppermute | solution.py:961
  248.3 4.3 %shard_map.379 = f32[1152,1152]{1,0:T(8,128)} custom-call(s32[2]{0:T(128)S(1)} %copy-done.9, bf16[576,1152]{1,0:T(8,128)(2,1)S(1)} %shard_map.372.own, bf16[576,1152]{1,0:T(8,128)(2,1)S(1)} %collective-permute-done.39.other), custom_call_target="tpu_custom_call" | custom-call | flops 1207500032 | bytes 1000 | tf_op jit(solution)/shard_map/pallas_call | solution.py:942
  252.7 10.4 %collective-permute-done.40.refs_2_ = bf16[304,1152]{1,0:T(8,128)(2,1)S(1)} collective-permute-done((bf16[304,1152]{1,0:T(8,128)(2,1)S(1)}, bf16[304,1152]{1,0:T(8,128)(2,1)S(1)}, u32[]{:S(2)}, u32[]{:S(2)}) %collective-permute-start.40) | collective-permute-done | bytes 700448 | tf_op jit(solution)/shard_map/ppermute | solution.py:961
  265.2 4.3 %shard_map.381 = (f32[288,1152]{1,0:T(8,128)}, f32[288,1152]{1,0:T(8,128)}, f32[288,1000]{1,0:T(8,128)}, f32[4,1024]{1,0:T(4,128)S(1)}, f32[16,288]{1,0:T(8,128)S(1)}) custom-call(f32[32,1152]{1,0:T(8,128)S(1)} %get-tuple-element.206.refs_0_, bf16[1000,1152]{1,0:T(8,128)(2,1)} %refs_1_.5), custom_call_target="tpu_custom_call" | custom-call | flops 862499968 | bytes 1000 | tf_op jit(solution)/shard_map/pallas_call | solution.py:899
  271.5 3.7 %collective-permute-done.41.refs_2_ = bf16[288,1152]{1,0:T(8,128)(2,1)S(1)} collective-permute-done((bf16[288,1152]{1,0:T(8,128)(2,1)S(1)}, bf16[288,1152]{1,0:T(8,128)(2,1)S(1)}, u32[]{:S(2)}, u32[]{:S(2)}) %collective-permute-start.41) | collective-permute-done | bytes 663584 | tf_op jit(solution)/shard_map/ppermute | solution.py:961
  (148 shorter events, 49.2 us)
Async XLA Ops:
  0.7 22.8 %collective-permute-start = (bf16[256,1152]{1,0:T(8,128)(2,1)}, bf16[256,1152]{1,0:T(8,128)(2,1)S(1)}, u32[]{:S(2)}, u32[]{:S(2)}) collective-permute-start(bf16[256,1152]{1,0:T(8,128)(2,1)} %refs_3_.2), channel_id=1, source_target_pairs={{0,2},{1,3},{2,0},{3,1},{4,6},{5,7},{6,4},{7,5},{8,10},{9,11},{10,... | collective-permute-start | bytes 1769480 | tf_op jit(solution)/shard_map/ppermute | solution.py:961
  24.2 15.9 %collective-permute-start.5 = (bf16[256,1152]{1,0:T(8,128)(2,1)}, bf16[256,1152]{1,0:T(8,128)(2,1)S(1)}, u32[]{:S(2)}, u32[]{:S(2)}) collective-permute-start(bf16[256,1152]{1,0:T(8,128)(2,1)} %get-tuple-element.118.refs_1_), channel_id=1, source_target_pairs={{0,2},{1,3},{2,0},{3,1},{4,6},{5,7},{6,4},{7,5},{8,10},{9,11},{10,... | collective-permute-start | bytes 1769480 | tf_op jit(solution)/shard_map/ppermute | solution.py:961
  35.0 5.3 %collective-permute-start.4 = (bf16[256,1152]{1,0:T(8,128)(2,1)S(1)}, bf16[256,1152]{1,0:T(8,128)(2,1)S(1)}, u32[]{:S(2)}, u32[]{:S(2)}) collective-permute-start(bf16[256,1152]{1,0:T(8,128)(2,1)S(1)} %get-tuple-element.123), channel_id=1, source_target_pairs={{0,1},{1,0},{2,3},{3,2},{4,5},{5,4},{6,7},{7,6},{8,9},{9,8},{10,11... | collective-permute-start | bytes 1769480 | tf_op jit(solution)/shard_map/ppermute | solution.py:961
  40.1 11.5 %collective-permute-start.7 = (bf16[2,256,384]{2,1,0:T(8,128)(2,1)S(1)}, bf16[2,256,384]{2,1,0:T(8,128)(2,1)S(1)}, u32[]{:S(2)}, u32[]{:S(2)}) collective-permute-start(bf16[2,256,384]{2,1,0:T(8,128)(2,1)S(1)} %copy-done.25), channel_id=1, source_target_pairs={{0,2},{1,3},{2,0},{3,1},{4,6},{5,7},{6,4},{7,5},{8,10},{9,11},{10,... | collective-permute-start | bytes 1179656 | tf_op jit(solution)/shard_map/ppermute | solution.py:961
  49.5 7.5 %collective-permute-start.8 = (bf16[256,1152]{1,0:T(8,128)(2,1)S(1)}, bf16[256,1152]{1,0:T(8,128)(2,1)S(1)}, u32[]{:S(2)}, u32[]{:S(2)}) collective-permute-start(bf16[256,1152]{1,0:T(8,128)(2,1)S(1)} %get-tuple-element.136), channel_id=1, source_target_pairs={{0,1},{1,0},{2,3},{3,2},{4,5},{5,4},{6,7},{7,6},{8,9},{9,8},{10,11... | collective-permute-start | bytes 1769480 | tf_op jit(solution)/shard_map/ppermute | solution.py:961
  55.4 39.3 %collective-permute-start.15 = (bf16[576,1152]{1,0:T(8,128)(2,1)S(1)}, bf16[576,1152]{1,0:T(8,128)(2,1)S(1)}, u32[]{:S(2)}, u32[]{:S(2)}) collective-permute-start(bf16[576,1152]{1,0:T(8,128)(2,1)S(1)} %get-tuple-element.160), channel_id=1, source_target_pairs={{0,4},{4,0},{8,12},{12,8},{16,20},{20,16},{24,28},{28,24},{1,5},{5... | collective-permute-start | bytes 3981320 | tf_op jit(solution)/shard_map/ppermute | solution.py:961
  57.2 14.7 %collective-permute-start.11 = (bf16[256,1152]{1,0:T(8,128)(2,1)S(1)}, bf16[256,1152]{1,0:T(8,128)(2,1)S(1)}, u32[]{:S(2)}, u32[]{:S(2)}) collective-permute-start(bf16[256,1152]{1,0:T(8,128)(2,1)S(1)} %shard_map.353), channel_id=1, source_target_pairs={{0,2},{1,3},{2,0},{3,1},{4,6},{5,7},{6,4},{7,5},{8,10},{9,11},{10,... | collective-permute-start | bytes 1769480 | tf_op jit(solution)/shard_map/ppermute | solution.py:961
  61.7 34.1 %collective-permute-start.16 = (bf16[576,1152]{1,0:T(8,128)(2,1)S(1)}, bf16[576,1152]{1,0:T(8,128)(2,1)S(1)}, u32[]{:S(2)}, u32[]{:S(2)}) collective-permute-start(bf16[576,1152]{1,0:T(8,128)(2,1)S(1)} %get-tuple-element.163), channel_id=1, source_target_pairs={{0,8},{4,12},{8,0},{12,4},{16,24},{20,28},{24,16},{28,20},{1,9},{5... | collective-permute-start | bytes 3981320 | tf_op jit(solution)/shard_map/ppermute | solution.py:961
  63.3 10.8 %collective-permute-start.12 = (bf16[2,256,384]{2,1,0:T(8,128)(2,1)S(1)}, bf16[2,256,384]{2,1,0:T(8,128)(2,1)S(1)}, u32[]{:S(2)}, u32[]{:S(2)}) collective-permute-start(bf16[2,256,384]{2,1,0:T(8,128)(2,1)S(1)} %collective-permute-done.7.refs_13_), channel_id=1, source_target_pairs={{0,1},{1,0},{2,3},{3,2},{4,5},{5,4},{6,7},{7,6},{8,9},{9,8},{10,11... | collective-permute-start | bytes 1179656 | tf_op jit(solution)/shard_map/ppermute | solution.py:961
  63.3 10.8 %collective-permute-start.13 = (bf16[256,384]{1,0:T(8,128)(2,1)S(1)}, bf16[256,384]{1,0:T(8,128)(2,1)S(1)}, u32[]{:S(2)}, u32[]{:S(2)}) collective-permute-start(bf16[256,384]{1,0:T(8,128)(2,1)S(1)} %copy-done.26), channel_id=1, source_target_pairs={{0,1},{1,0},{2,3},{3,2},{4,5},{5,4},{6,7},{7,6},{8,9},{9,8},{10,11... | collective-permute-start | bytes 589832 | tf_op jit(solution)/shard_map/ppermute | solution.py:961
  73.5 21.2 %collective-permute-start.14 = (bf16[256,1152]{1,0:T(8,128)(2,1)S(1)}, bf16[256,1152]{1,0:T(8,128)(2,1)S(1)}, u32[]{:S(2)}, u32[]{:S(2)}) collective-permute-start(bf16[256,1152]{1,0:T(8,128)(2,1)S(1)} %get-tuple-element.151.refs_1_.refs_7_), channel_id=1, source_target_pairs={{0,2},{1,3},{2,0},{3,1},{4,6},{5,7},{6,4},{7,5},{8,10},{9,11},{10,... | collective-permute-start | bytes 1769480 | tf_op jit(solution)/shard_map/ppermute | solution.py:961
  84.2 25.3 %collective-permute-start.18 = (bf16[2,288,896]{2,1,0:T(8,128)(2,1)S(1)}, bf16[2,288,896]{2,1,0:T(8,128)(2,1)S(1)}, u32[]{:S(2)}, u32[]{:S(2)}) collective-permute-start(bf16[2,288,896]{2,1,0:T(8,128)(2,1)S(1)} %get-tuple-element.172), channel_id=1, source_target_pairs={{0,2},{1,3},{2,0},{3,1},{4,6},{5,7},{6,4},{7,5},{8,10},{9,11},{10,... | collective-permute-start | bytes 3096584 | tf_op jit(solution)/shard_map/ppermute | solution.py:961
  96.8 17.4 %collective-permute-start.20 = (bf16[288,1152]{1,0:T(8,128)(2,1)S(1)}, bf16[288,1152]{1,0:T(8,128)(2,1)S(1)}, u32[]{:S(2)}, u32[]{:S(2)}) collective-permute-start(bf16[288,1152]{1,0:T(8,128)(2,1)S(1)} %get-tuple-element.173), channel_id=1, source_target_pairs={{0,4},{4,0},{8,12},{12,8},{16,20},{20,16},{24,28},{28,24},{1,5},{5... | collective-permute-start | bytes 1990664 | tf_op jit(solution)/shard_map/ppermute | solution.py:961
  97.4 17.0 %collective-permute-start.21 = (bf16[288,1152]{1,0:T(8,128)(2,1)S(1)}, bf16[288,1152]{1,0:T(8,128)(2,1)S(1)}, u32[]{:S(2)}, u32[]{:S(2)}) collective-permute-start(bf16[288,1152]{1,0:T(8,128)(2,1)S(1)} %get-tuple-element.175), channel_id=1, source_target_pairs={{0,8},{4,12},{8,0},{12,4},{16,24},{20,28},{24,16},{28,20},{1,9},{5... | collective-permute-start | bytes 1990664 | tf_op jit(solution)/shard_map/ppermute | solution.py:961
  115.7 32.0 %collective-permute-start.26 = (bf16[288,1152]{1,0:T(8,128)(2,1)S(1)}, bf16[288,1152]{1,0:T(8,128)(2,1)S(1)}, u32[]{:S(2)}, u32[]{:S(2)}) collective-permute-start(bf16[288,1152]{1,0:T(8,128)(2,1)S(1)} %shard_map.363.left), channel_id=1, source_target_pairs={{0,16},{4,20},{8,24},{12,28},{16,0},{20,4},{24,8},{28,12},{1,17},{... | collective-permute-start | bytes 1990664 | tf_op jit(solution)/shard_map/ppermute | solution.py:961
  125.1 23.5 %collective-permute-start.27 = (bf16[304,1152]{1,0:T(8,128)(2,1)S(1)}, bf16[304,1152]{1,0:T(8,128)(2,1)S(1)}, u32[]{:S(2)}, u32[]{:S(2)}) collective-permute-start(bf16[304,1152]{1,0:T(8,128)(2,1)S(1)} %get-tuple-element.186), channel_id=1, source_target_pairs={{0,4},{4,0},{8,12},{12,8},{16,20},{20,16},{24,28},{28,24},{1,5},{5... | collective-permute-start | bytes 2101256 | tf_op jit(solution)/shard_map/ppermute | solution.py:961
  126.7 30.4 %collective-permute-start.28 = (bf16[288,1152]{1,0:T(8,128)(2,1)S(1)}, bf16[288,1152]{1,0:T(8,128)(2,1)S(1)}, u32[]{:S(2)}, u32[]{:S(2)}) collective-permute-start(bf16[288,1152]{1,0:T(8,128)(2,1)S(1)} %get-tuple-element.190), channel_id=1, source_target_pairs={{0,4},{4,0},{8,12},{12,8},{16,20},{20,16},{24,28},{28,24},{1,5},{5... | collective-permute-start | bytes 1990664 | tf_op jit(solution)/shard_map/ppermute | solution.py:961
  147.9 30.9 %collective-permute-start.29 = (bf16[288,1152]{1,0:T(8,128)(2,1)S(1)}, bf16[288,1152]{1,0:T(8,128)(2,1)S(1)}, u32[]{:S(2)}, u32[]{:S(2)}) collective-permute-start(bf16[288,1152]{1,0:T(8,128)(2,1)S(1)} %shard_map.365.own), channel_id=1, source_target_pairs={{0,8},{4,12},{8,0},{12,4},{16,24},{20,28},{24,16},{28,20},{1,9},{5... | collective-permute-start | bytes 1990664 | tf_op jit(solution)/shard_map/ppermute | solution.py:961
  149.5 36.3 %collective-permute-start.31 = (bf16[288,1152]{1,0:T(8,128)(2,1)S(1)}, bf16[288,1152]{1,0:T(8,128)(2,1)S(1)}, u32[]{:S(2)}, u32[]{:S(2)}) collective-permute-start(bf16[288,1152]{1,0:T(8,128)(2,1)S(1)} %shard_map.367.left), channel_id=1, source_target_pairs={{0,16},{4,20},{8,24},{12,28},{16,0},{20,4},{24,8},{28,12},{1,17},{... | collective-permute-start | bytes 1990664 | tf_op jit(solution)/shard_map/ppermute | solution.py:961
  153.0 32.7 %collective-permute-start.30 = (bf16[152,1152]{1,0:T(8,128)(2,1)S(1)}, bf16[152,1152]{1,0:T(8,128)(2,1)S(1)}, u32[]{:S(2)}, u32[]{:S(2)}) collective-permute-start(bf16[152,1152]{1,0:T(8,128)(2,1)S(1)} %get-tuple-element.194), channel_id=1, source_target_pairs={{0,8},{4,12},{8,0},{12,4},{16,24},{20,28},{24,16},{28,20},{1,9},{5... | collective-permute-start | bytes 1050632 | tf_op jit(solution)/shard_map/ppermute | solution.py:961
  153.0 68.8 %collective-permute-start.9 = (bf16[2,256,1152]{2,1,0:T(8,128)(2,1)S(1)}, bf16[2,256,1152]{2,1,0:T(8,128)(2,1)S(1)}, u32[]{:S(2)}, u32[]{:S(2)}) collective-permute-start(bf16[2,256,1152]{2,1,0:T(8,128)(2,1)S(1)} %get-tuple-element.142), channel_id=1, source_target_pairs={{0,1},{1,0},{2,3},{3,2},{4,5},{5,4},{6,7},{7,6},{8,9},{9,8},{10,11... | collective-permute-start | bytes 3538952 | tf_op jit(solution)/shard_map/ppermute | solution.py:961
  186.0 25.4 %collective-permute-start.32 = (bf16[288,1152]{1,0:T(8,128)(2,1)S(1)}, bf16[288,1152]{1,0:T(8,128)(2,1)S(1)}, u32[]{:S(2)}, u32[]{:S(2)}) collective-permute-start(bf16[288,1152]{1,0:T(8,128)(2,1)S(1)} %shard_map.371.own), channel_id=1, source_target_pairs={{0,8},{4,12},{8,0},{12,4},{16,24},{20,28},{24,16},{28,20},{1,9},{5... | collective-permute-start | bytes 1990664 | tf_op jit(solution)/shard_map/ppermute | solution.py:961
  187.5 45.7 %collective-permute-start.36 = (bf16[576,1152]{1,0:T(8,128)(2,1)S(1)}, bf16[576,1152]{1,0:T(8,128)(2,1)S(1)}, u32[]{:S(2)}, u32[]{:S(2)}) collective-permute-start(bf16[576,1152]{1,0:T(8,128)(2,1)S(1)} %shard_map.369.own), channel_id=1, source_target_pairs={{0,4},{4,0},{8,12},{12,8},{16,20},{20,16},{24,28},{28,24},{1,5},{5... | collective-permute-start | bytes 3981320 | tf_op jit(solution)/shard_map/ppermute | solution.py:961
  189.0 24.6 %collective-permute-start.33 = (bf16[152,1152]{1,0:T(8,128)(2,1)S(1)}, bf16[152,1152]{1,0:T(8,128)(2,1)S(1)}, u32[]{:S(2)}, u32[]{:S(2)}) collective-permute-start(bf16[152,1152]{1,0:T(8,128)(2,1)S(1)} %shard_map.370.left), channel_id=1, source_target_pairs={{0,16},{4,20},{8,24},{12,28},{16,0},{20,4},{24,8},{28,12},{1,17},{... | collective-permute-start | bytes 1050632 | tf_op jit(solution)/shard_map/ppermute | solution.py:961
  192.4 26.1 %collective-permute-start.34 = (bf16[144,1152]{1,0:T(8,128)(2,1)S(1)}, bf16[144,1152]{1,0:T(8,128)(2,1)S(1)}, u32[]{:S(2)}, u32[]{:S(2)}) collective-permute-start(bf16[144,1152]{1,0:T(8,128)(2,1)S(1)} %get-tuple-element.199), channel_id=1, source_target_pairs={{0,8},{4,12},{8,0},{12,4},{16,24},{20,28},{24,16},{28,20},{1,9},{5... | collective-permute-start | bytes 995336 | tf_op jit(solution)/shard_map/ppermute | solution.py:961
  212.0 36.3 %collective-permute-start.39 = (bf16[576,1152]{1,0:T(8,128)(2,1)S(1)}, bf16[576,1152]{1,0:T(8,128)(2,1)S(1)}, u32[]{:S(2)}, u32[]{:S(2)}) collective-permute-start(bf16[576,1152]{1,0:T(8,128)(2,1)S(1)} %shard_map.372.own), channel_id=1, source_target_pairs={{0,4},{4,0},{8,12},{12,8},{16,20},{20,16},{24,28},{28,24},{1,5},{5... | collective-permute-start | bytes 3981320 | tf_op jit(solution)/shard_map/ppermute | solution.py:961
  213.7 17.3 %collective-permute-start.35 = (bf16[152,1152]{1,0:T(8,128)(2,1)S(1)}, bf16[152,1152]{1,0:T(8,128)(2,1)S(1)}, u32[]{:S(2)}, u32[]{:S(2)}) collective-permute-start(bf16[152,1152]{1,0:T(8,128)(2,1)S(1)} %shard_map.373.own), channel_id=1, source_target_pairs={{0,8},{4,12},{8,0},{12,4},{16,24},{20,28},{24,16},{28,20},{1,9},{5... | collective-permute-start | bytes 1050632 | tf_op jit(solution)/shard_map/ppermute | solution.py:961
  218.6 19.0 %collective-permute-start.37 = (bf16[144,1152]{1,0:T(8,128)(2,1)S(1)}, bf16[144,1152]{1,0:T(8,128)(2,1)S(1)}, u32[]{:S(2)}, u32[]{:S(2)}) collective-permute-start(bf16[144,1152]{1,0:T(8,128)(2,1)S(1)} %shard_map.374.left), channel_id=1, source_target_pairs={{0,16},{4,20},{8,24},{12,28},{16,0},{20,4},{24,8},{28,12},{1,17},{... | collective-permute-start | bytes 995336 | tf_op jit(solution)/shard_map/ppermute | solution.py:961
  222.0 24.4 %collective-permute-start.10 = (bf16[256,1152]{1,0:T(8,128)(2,1)S(1)}, bf16[256,1152]{1,0:T(8,128)(2,1)S(1)}, u32[]{:S(2)}, u32[]{:S(2)}) collective-permute-start(bf16[256,1152]{1,0:T(8,128)(2,1)S(1)} %fusion), channel_id=1, source_target_pairs={{0,2},{1,3},{2,0},{3,1},{4,6},{5,7},{6,4},{7,5},{8,10},{9,11},{10,... | collective-permute-start | bytes 1769480 | tf_op jit(solution)/shard_map/ppermute | solution.py:961
  231.6 31.4 %collective-permute-start.40 = (bf16[304,1152]{1,0:T(8,128)(2,1)S(1)}, bf16[304,1152]{1,0:T(8,128)(2,1)S(1)}, u32[]{:S(2)}, u32[]{:S(2)}) collective-permute-start(bf16[304,1152]{1,0:T(8,128)(2,1)S(1)} %shard_map.375.refs_1_), channel_id=1, source_target_pairs={{0,4},{4,0},{8,12},{12,8},{16,20},{20,16},{24,28},{28,24},{1,5},{5... | collective-permute-start | bytes 2101256 | tf_op jit(solution)/shard_map/ppermute | solution.py:961
  237.6 7.5 %collective-permute-start.38 = (bf16[144,1152]{1,0:T(8,128)(2,1)S(1)}, bf16[144,1152]{1,0:T(8,128)(2,1)S(1)}, u32[]{:S(2)}, u32[]{:S(2)}) collective-permute-start(bf16[144,1152]{1,0:T(8,128)(2,1)S(1)} %shard_map.377.own), channel_id=1, source_target_pairs={{0,8},{4,12},{8,0},{12,4},{16,24},{20,28},{24,16},{28,20},{1,9},{5... | collective-permute-start | bytes 995336 | tf_op jit(solution)/shard_map/ppermute | solution.py:961
  245.8 29.4 %collective-permute-start.41 = (bf16[288,1152]{1,0:T(8,128)(2,1)S(1)}, bf16[288,1152]{1,0:T(8,128)(2,1)S(1)}, u32[]{:S(2)}, u32[]{:S(2)}) collective-permute-start(bf16[288,1152]{1,0:T(8,128)(2,1)S(1)} %shard_map.378.refs_1_), channel_id=1, source_target_pairs={{0,4},{4,0},{8,12},{12,8},{16,20},{20,16},{24,28},{28,24},{1,5},{5... | collective-permute-start | bytes 1990664 | tf_op jit(solution)/shard_map/ppermute | solution.py:961
  (37 other events, 354.8 us)
